TPU v7x, 32 devices: a whole 2x2x4 slice. The times are simulated.
32 devices in a mesh: seq: 16 (over z, y, core), ch: 2 (over x).
Axes of the slice: x: 2, y: 2, z: 4, core: 2. Of those that a mesh axis runs over, the one named last changes fastest.
Arguments:
- tokens: bfloat16 [16, 1280, 4096], P(None, None, 'seq'), may hold values from -6 to 6
- pad_mask: int32 [16, 4096], P(None, 'seq'), may hold values from 0 to 1, as said below
- cotangent: bfloat16 [16, 1280, 4096], P(None, 'ch', 'seq'), may hold values from -6 to 6
- ln1_gain: float32 [1280], replicated, may hold values from 0.25 to 1.75
- first_norm_bias: float32 [1280], replicated, may hold values from -3 to 3
- w_in: bfloat16 [640, 1280], P('ch'), may hold values from -0.15625 to 0.15625
- b_in: float32 [640], P('ch'), may hold values from -3 to 3
- ln2_gain: float32 [640], P('ch'), may hold values from 0.25 to 1.75
- ln2_bias: float32 [640], P('ch'), may hold values from -3 to 3
- conv_w: bfloat16 [5, 640, 640], P(None, 'ch'), may hold values from -0.109375 to 0.109375
- conv_b: float32 [640], P('ch'), may hold values from -3 to 3
- ln3_gain: float32 [640], P('ch'), may hold values from 0.25 to 1.75
- ln3_bias: float32 [640], P('ch'), may hold values from -3 to 3
- w_out: bfloat16 [640, 1280], P('ch'), may hold values from -0.25 to 0.25
- b_out: float32 [1280], P('ch'), may hold values from -3 to 3
Outputs:
- mixed: bfloat16 [16, 1280, 4096], P(None, 'ch', 'seq')
- grad_tokens: float32 [16, 1280, 4096], P(None, 'ch', 'seq')
- grad_ln1_gain: float32 [1280], P('ch')
- grad_ln1_bias: float32 [1280], P('ch')
- grad_w_in: float32 [640, 1280], P('ch')
- grad_b_in: float32 [640], P('ch')
- grad_ln2_gain: float32 [640], P('ch')
- grad_ln2_bias: float32 [640], P('ch')
- grad_conv_w: float32 [5, 640, 640], P(None, 'ch')
- grad_conv_b: float32 [640], P('ch')
- grad_ln3_gain: float32 [640], P('ch')
- grad_ln3_bias: float32 [640], P('ch')
- grad_w_out: float32 [640, 1280], P('ch')
- grad_b_out: float32 [1280], P('ch')
Inputs may be any that keep to these rules, and one draw needn't show every extreme that they name: `pad_mask`: in each sequence the ones form a prefix of 1024 to 4096 positions; the first sequence is all ones.
All inputs are finite; a program needn't handle non-finite values.
Results may differ from a plain program's by a relative error of at most 0.0066.
Values may be sent and summed in bfloat16 or wider, within the bound.
A program may use at most 256 MiB of HBM per device.

v0:
```python
import jax
import jax.numpy as jnp
from jax import lax
from jax.sharding import PartitionSpec as P

D = 1280
INNER = 640
KERNEL = 5
DILATION = 16


EPS = 1e-05


def with_halo(array, sides, width):
    for axis, dim in sides:
        count, length = (lax.axis_size(axis), array.shape[dim])
        up = [(i, (i + 1) % count) for i in range(count - 1)]
        down = [(j, i) for i, j in up]
        last = lax.slice_in_dim(array, length - width, length, axis=dim)
        leading = lax.slice_in_dim(array, 0, width, axis=dim)
        before = lax.ppermute(last, axis, up)
        after = lax.ppermute(leading, axis, down)
        array = jnp.concatenate([before, array, after], axis=dim)
    return array


def gelu_exact(value):
    return jax.nn.gelu(value, approximate=False)


def gelu_back(point, grad):
    return jax.vjp(gelu_exact, point)[1](grad)[0]


def column_slot(vector):
    return vector[None, :, None]


def own_slice(value, width, dim):
    return lax.dynamic_slice_in_dim(value, lax.axis_index("ch") * width, width, dim)


def forward(
    tokens,
    live_mask,
    ln1_gain,
    first_norm_bias,
    w_in,
    b_in,
    ln2_gain,
    ln2_bias,
    conv_w,
    conv_b,
    ln3_gain,
    ln3_bias,
):
    resid = tokens.astype(jnp.float32)
    mean_in = jnp.mean(resid, axis=1, keepdims=True)
    center = resid - mean_in
    scale_in = lax.rsqrt(jnp.mean(center * center, axis=1, keepdims=True) + EPS)
    first = gelu_exact(
        center * scale_in * column_slot(ln1_gain) + column_slot(first_norm_bias)
    ).astype(jnp.bfloat16)
    narrow = jnp.einsum(
        "sdl,ed->sel", first, w_in, preferred_element_type=jnp.float32
    ) + column_slot(b_in)
    total_mid, square_mid = lax.psum(
        (jnp.sum(narrow, axis=1), jnp.sum(narrow * narrow, axis=1)), "ch"
    )
    mean_mid = (total_mid / INNER)[:, None, :]
    scale_mid = lax.rsqrt(square_mid[:, None, :] / INNER - mean_mid * mean_mid + EPS)
    hat_mid = (narrow - mean_mid) * scale_mid
    pre_mid = hat_mid * column_slot(ln2_gain) + column_slot(ln2_bias)
    middle = (gelu_exact(pre_mid) * live_mask[:, None, :]).astype(jnp.bfloat16)
    reach = KERNEL // 2 * DILATION
    border_trimmed = with_halo(middle, (("seq", 2),), reach)
    padded = lax.all_gather(border_trimmed, "ch", axis=1, tiled=True)
    length_total = middle.shape[2]
    convolved = column_slot(conv_b) + jnp.zeros(middle.shape, jnp.float32)
    for kernel_tap in range(KERNEL):
        window = padded[:, :, kernel_tap * DILATION : kernel_tap * DILATION + length_total]
        convolved = convolved + jnp.einsum(
            "sil,oi->sol", window, conv_w[kernel_tap], preferred_element_type=jnp.float32
        )
    total_out, output_squared = lax.psum(
        (jnp.sum(convolved, axis=1), jnp.sum(convolved * convolved, axis=1)), "ch"
    )
    mean_out = (total_out / INNER)[:, None, :]
    scale_out = lax.rsqrt(output_squared[:, None, :] / INNER - mean_out * mean_out + EPS)
    hat_out = (convolved - mean_out) * scale_out
    pre_out = hat_out * column_slot(ln3_gain) + column_slot(ln3_bias)
    last = gelu_exact(pre_out).astype(jnp.bfloat16)
    return (
        mean_in,
        scale_in,
        first,
        hat_mid,
        scale_mid,
        pre_mid,
        padded,
        hat_out,
        scale_out,
        pre_out,
        last,
    )


def finish(own_tokens, last, w_out, b_out):
    branch = jnp.einsum("sil,id->sdl", last, w_out, preferred_element_type=jnp.float32)
    share = lax.psum_scatter(branch, "ch", scatter_dimension=1, tiled=True)
    return (own_tokens.astype(jnp.float32) + share + column_slot(b_out)).astype(jnp.bfloat16)


def body(
    tokens,
    pad_mask,
    cotangent,
    ln1_gain,
    first_norm_bias,
    w_in,
    b_in,
    ln2_gain,
    ln2_bias,
    conv_w,
    conv_b,
    ln3_gain,
    ln3_bias,
    w_out,
    b_out,
):
    live_mask = pad_mask.astype(jnp.float32)
    feature_share = b_out.shape[0]
    own_tokens = own_slice(tokens, feature_share, 1)
    early = forward(
        tokens,
        live_mask,
        ln1_gain,
        first_norm_bias,
        w_in,
        b_in,
        ln2_gain,
        ln2_bias,
        conv_w,
        conv_b,
        ln3_gain,
        ln3_bias,
    )
    mixed = finish(own_tokens, early[10], w_out, b_out)
    saved = forward(
        tokens,
        live_mask,
        ln1_gain,
        first_norm_bias,
        w_in,
        b_in,
        ln2_gain,
        ln2_bias,
        conv_w,
        conv_b,
        ln3_gain,
        ln3_bias,
    )
    (
        mean_in,
        scale_in,
        first,
        hat_mid,
        scale_mid,
        pre_mid,
        padded,
        hat_out,
        scale_out,
        pre_out,
        last,
    ) = saved
    length_total = tokens.shape[2]
    reach = KERNEL // 2 * DILATION
    grad_full = lax.all_gather(cotangent, "ch", axis=1, tiled=True)
    grad_w_out = jnp.einsum("sil,sdl->id", last, grad_full, preferred_element_type=jnp.float32)
    grad_b_out = jnp.sum(cotangent.astype(jnp.float32), axis=(0, 2))
    d_last = jnp.einsum("sdl,id->sil", grad_full, w_out, preferred_element_type=jnp.float32)
    d_pre_out = gelu_back(pre_out, d_last)
    grad_ln3_gain = jnp.sum(d_pre_out * hat_out, axis=(0, 2))
    grad_ln3_bias = jnp.sum(d_pre_out, axis=(0, 2))
    scaled_out = d_pre_out * column_slot(ln3_gain)
    sum_out, dot_out = lax.psum(
        (jnp.sum(scaled_out, axis=1), jnp.sum(scaled_out * hat_out, axis=1)), "ch"
    )
    d_conv = (
        scale_out
        * (scaled_out - sum_out[:, None, :] / INNER - hat_out * dot_out[:, None, :] / INNER)
    ).astype(jnp.bfloat16)
    grad_conv_b = jnp.sum(d_conv.astype(jnp.float32), axis=(0, 2))
    conv_terms = []
    for kernel_tap in range(KERNEL):
        window = padded[:, :, kernel_tap * DILATION : kernel_tap * DILATION + length_total]
        conv_terms.append(
            jnp.einsum("sil,sol->oi", window, d_conv, preferred_element_type=jnp.float32)
        )
    grad_conv_w = jnp.stack(conv_terms)
    padded_back = with_halo(d_conv, (("seq", 2),), reach)
    backward_portion = jnp.zeros((d_conv.shape[0], conv_w.shape[2], length_total), jnp.float32)
    for kernel_tap in range(KERNEL):
        start = (KERNEL - 1 - kernel_tap) * DILATION
        window = padded_back[:, :, start : start + length_total]
        backward_portion = backward_portion + jnp.einsum(
            "sol,oi->sil", window, conv_w[kernel_tap], preferred_element_type=jnp.float32
        )
    d_middle = lax.psum_scatter(backward_portion, "ch", scatter_dimension=1, tiled=True)
    d_pre_mid = gelu_back(pre_mid, d_middle * live_mask[:, None, :])
    grad_ln2_gain = jnp.sum(d_pre_mid * hat_mid, axis=(0, 2))
    grad_ln2_bias = jnp.sum(d_pre_mid, axis=(0, 2))
    scaled_mid = d_pre_mid * column_slot(ln2_gain)
    sum_mid, dot_mid = (
        lax.psum(jnp.sum(scaled_mid, axis=1).astype(jnp.bfloat16), "ch").astype(jnp.float32),
        lax.psum(jnp.sum(scaled_mid * hat_mid, axis=1).astype(jnp.bfloat16), "ch").astype(
            jnp.float32
        ),
    )
    d_narrow = (
        scale_mid
        * (scaled_mid - sum_mid[:, None, :] / INNER - hat_mid * dot_mid[:, None, :] / INNER)
    ).astype(jnp.bfloat16)
    grad_b_in = jnp.sum(d_narrow.astype(jnp.float32), axis=(0, 2))
    grad_w_in = jnp.einsum("sel,sdl->ed", d_narrow, first, preferred_element_type=jnp.float32)
    first_part = jnp.einsum("sel,ed->sdl", d_narrow, w_in, preferred_element_type=jnp.float32)
    d_first = lax.psum_scatter(first_part, "ch", scatter_dimension=1, tiled=True)
    gain_share = own_slice(ln1_gain, feature_share, 0)
    bias_share = own_slice(first_norm_bias, feature_share, 0)
    hat_share = (own_tokens.astype(jnp.float32) - mean_in) * scale_in
    pre_share = hat_share * column_slot(gain_share) + column_slot(bias_share)
    d_pre_in = gelu_back(pre_share, d_first)
    grad_ln1_gain = jnp.sum(d_pre_in * hat_share, axis=(0, 2))
    grad_ln1_bias = jnp.sum(d_pre_in, axis=(0, 2))
    scaled_in = d_pre_in * column_slot(gain_share)
    sum_in, dot_in = (
        lax.psum(jnp.sum(scaled_in, axis=1).astype(jnp.bfloat16), "ch").astype(jnp.float32),
        lax.psum(jnp.sum(scaled_in * hat_share, axis=1).astype(jnp.bfloat16), "ch").astype(
            jnp.float32
        ),
    )
    grad_tokens = scale_in * (
        scaled_in - sum_in[:, None, :] / D - hat_share * dot_in[:, None, :] / D
    ) + cotangent.astype(jnp.float32)
    summed = lax.psum(
        (
            grad_ln1_gain,
            grad_ln1_bias,
            grad_w_in,
            grad_b_in,
            grad_ln2_gain,
            grad_ln2_bias,
            grad_conv_w,
            grad_conv_b,
            grad_ln3_gain,
            grad_ln3_bias,
            grad_w_out,
            grad_b_out,
        ),
        "seq",
    )
    return (
        mixed,
        grad_tokens,
        summed[0],
        summed[1],
        summed[2],
        summed[3],
        summed[4],
        summed[5],
        summed[6],
        summed[7],
        summed[8],
        summed[9],
        summed[10],
        summed[11],
    )


def solution(mesh):
    in_specs = (
        P(None, None, "seq"),
        P(None, "seq"),
        P(None, "ch", "seq"),
        P(),
        P(),
        P("ch", None),
        P("ch"),
        P("ch"),
        P("ch"),
        P(None, "ch", None),
        P("ch"),
        P("ch"),
        P("ch"),
        P("ch", None),
        P("ch"),
    )
    out_specs = (
        P(None, "ch", "seq"),
        P(None, "ch", "seq"),
        P("ch"),
        P("ch"),
        P("ch", None),
        P("ch"),
        P("ch"),
        P("ch"),
        P(None, "ch", None),
        P("ch"),
        P("ch"),
        P("ch"),
        P("ch", None),
        P("ch"),
    )
    return jax.shard_map(body, mesh=mesh, in_specs=in_specs, out_specs=out_specs, check_vma=False)
```

profile of v0, /device:TPU:0, one launch (start us, length us, event | category | flops | bytes accessed | tf_op | source)
XLA Modules:
  0.0 1269.7 jit_solution(8072259258483843660)
XLA Ops:
  17.7 50.9 %fusion.8 = bf16[16,1280,256]{2,1,0:T(8,128)(2,1)S(1)} fusion(bf16[16,1280,256]{2,1,0:T(8,128)(2,1)S(1)} %copy-done.1, f32[1280]{0:T(1024)S(1)} %copy-done.20, f32[1280]{0:T(1024)S(1)} %copy-done.18, f32[16,256]{1,0:T(8,128)S(1)} %add_rsqrt_fusion.2, f32[16,256]{1,0:T(8,128)S(1)} %broadcast_multiply_fusion.3), kind=kLoop, calls=%fused_computation.11 | loop fusion | flops 367001600 | bytes 21014528 | tf_op jit(solution)/shard_map/convert_element_type | solution.py:64
  74.3 20.9 %all-reduce.4 = (f32[16,256]{1,0:T(8,128)S(1)}, f32[16,256]{1,0:T(8,128)S(1)}) all-reduce(f32[16,256]{1,0:T(8,128)S(1)} %get-tuple-element.53, f32[16,256]{1,0:T(8,128)S(1)} %get-tuple-element.52), channel_id=1, replica_groups=mesh['seq'=16,'ch'=2] {'ch'}, use_global_device_ids=true, to_apply=%region_5.0 | all-reduce | flops 8192 | bytes 65536 | tf_op jit(solution)/shard_map/psum | solution.py:68
  95.2 15.2 %multiply_convert_fusion.3 = (bf16[16,320,256]{2,1,0:T(8,128)(2,1)S(1)}, f32[16,320,256]{2,1,0:T(8,128)}) fusion(f32[16,256]{1,0:T(8,128)S(1)} %convert_element_type.69, f32[320]{0:T(512)S(1)} %copy-done.24, f32[320]{0:T(512)S(1)} %copy-done.16, f32[16,256]{1,0:T(8,128)S(1)} %get-tuple-element.100, f32[16,256]{1,0:T(8,128)S(1)} %get-tuple-element.99, ...), kind=kLoop, calls=%fused_computation.123 | loop fusion | flops 93061120 | bytes 13160192 | tf_op jit(solution)/shard_map/convert_element_type | solution.py:75
  132.3 103.3 %all-gather.3.cloned.1.call-done = bf16[16,640,320]{2,1,0:T(8,128)(2,1)} async-done(((bf16[16,320,320]{2,1,0:T(8,128)(2,1)}), bf16[16,640,320]{2,1,0:T(8,128)(2,1)}) %all-gather.3.cloned.1.call-update) | async-done | bytes 6553616 | tf_op jit(solution)/shard_map/all_gather | solution.py:78
  235.6 8.4 fusion.80
  256.5 9.5 bitcast_reduce_fusion
  265.9 8.5 all-reduce.3
  274.5 14.9 %multiply_convert_fusion.2 = (bf16[16,320,256]{2,1,0:T(8,128)(2,1)}, f32[16,320,256]{2,1,0:T(8,128)}) fusion(f32[320]{0:T(512)S(1)} %copy-done.28, f32[320]{0:T(512)S(1)} %copy-done.23, f32[16,256]{1,0:T(8,128)S(1)} %get-tuple-element.98, f32[16,256]{1,0:T(8,128)S(1)} %get-tuple-element.97, f32[16,256,320]{1,2,0:T(8,128)} %get-tuple-element.102), kind=kLoop, calls=%fused_computation.108 | loop fusion | flops 90439680 | bytes 13142528 | tf_op jit(solution)/shard_map/convert_element_type | solution.py:93
  289.4 77.7 %all-gather.5.cloned.1.call-done = bf16[16,1280,256]{2,1,0:T(8,128)(2,1)} async-done(((bf16[16,640,256]{2,1,0:T(8,128)(2,1)}), bf16[16,1280,256]{2,1,0:T(8,128)(2,1)}) %all-gather.5.cloned.1.call-update) | async-done | bytes 10485776 | tf_op jit(solution)/shard_map/all_gather | solution.py:179
  367.1 12.6 multiply_reduce_fusion.1
  379.7 7.2 all-reduce.2
  413.2 8.6 fusion.101
  421.8 7.8 fusion.98
  432.1 8.7 fusion.95
  440.7 22.9 %add_bitcast_fusion = f32[16,640,256]{2,1,0:T(8,128)} fusion(f32[16,256,640]{1,2,0:T(8,128)} %fusion.95, f32[16,256,640]{1,2,0:T(8,128)} %fusion.144, f32[16,256,640]{1,2,0:T(8,128)} %fusion.98, f32[16,256,640]{1,2,0:T(8,128)} %fusion.101, bf16[16,320,256]{2,1,0:T(8,128)(2,1)S(1)} %get-tuple-element.81, bf16[16,320,32]{2,1,0:T(8,128)(2,1)} %copy.49, ...), kind=kOutput, calls=%fused_computation.72 | convolution fusion | flops 1693450240 | bytes 56770560 | tf_op jit(solution)/shard_map/sol,oi->sil/dot_general | solution.py:207
  463.7 123.1 %reduce-scatter.6.cloned.1.call-done = f32[16,320,256]{2,1,0:T(8,128)} async-done(((f32[16,640,256]{2,1,0:T(8,128)}), f32[16,320,256]{2,1,0:T(8,128)}) %reduce-scatter.6.cloned.1.call-update) | async-done | bytes 5242896 | tf_op jit(solution)/shard_map/reduce_scatter | solution.py:210
  586.8 10.1 multiply_reduce_fusion.2
  596.9 6.9 all-reduce.6
  610.8 10.0 convolution_bitcast_fusion
  620.9 12.5 convolution_bitcast_fusion.1
  634.2 8.4 copy.52
  647.9 7.9 copy.60
  682.3 7.9 convolution_bitcast_fusion.2
  695.0 161.3 %reduce-scatter.8.cloned.1.call-done = f32[16,640,256]{1,2,0:T(8,128)} async-done(((f32[16,1280,256]{1,2,0:T(8,128)}), f32[16,640,256]{1,2,0:T(8,128)}) %reduce-scatter.8.cloned.1.call-update) | async-done | bytes 10485776 | tf_op jit(solution)/shard_map/reduce_scatter | solution.py:228
  856.3 34.6 %fusion.41 = (f32[640]{0:T(1024)S(1)}, bf16[16,256]{1,0:T(8,128)(2,1)S(1)}, bf16[16,256]{1,0:T(8,128)(2,1)S(1)}, f32[640]{0:T(1024)S(1)}, f32[16,640,256]{1,2,0:T(8,128)}) fusion(bf16[16,640,256]{1,2,0:T(8,128)(2,1)} %copy.60, f32[16,256]{1,0:T(8,128)S(1)} %copy-done.13, f32[16,256]{1,0:T(8,128)S(1)} %copy-done.15, f32[640]{0:T(1024)S(1)} %dynamic_slice.10, ...), kind=kLoop, calls=%fused_computation.57 | loop fusion | flops 217570048 | bytes 26273792 | tf_op jit(solution)/shard_map/reduce_sum | solution.py:234
  890.9 7.2 all-reduce.5
  898.1 194.9 %reduce-scatter.4.cloned.1.call-done = f32[16,640,256]{1,2,0:T(8,128)} async-done(((f32[16,1280,256]{1,2,0:T(8,128)}), f32[16,640,256]{1,2,0:T(8,128)}) %reduce-scatter.4.cloned.1.call-update) | async-done | bytes 10485776 | tf_op jit(solution)/shard_map/reduce_scatter | solution.py:111
  1093.1 18.0 %convert_reduce_fusion.1 = (f32[640]{0:T(1024)S(1)}, f32[16,640,256]{1,2,0:T(8,128)}, bf16[16,640,256]{1,2,0:T(8,128)(2,1)}) fusion(bf16[16,640,256]{1,2,0:T(8,128)(2,1)} %copy.52, f32[16,256]{1,0:T(8,128)S(1)} %convert_element_type.82, f32[16,256]{1,0:T(8,128)S(1)} %copy-done.13, bf16[16,640,256]{1,2,0:T(8,128)(2,1)} %copy.60, ...), kind=kLoop, calls=%fused_computation.32 | loop fusion | flops 39320960 | bytes 47259136 | tf_op jit(solution)/shard_map/reduce_sum | solution.py:181
  1111.1 11.3 copy.54
  1122.4 7.9 copy.53
  1130.3 63.3 %all-reduce = (f32[640]{0:T(1024)}, f32[640]{0:T(1024)}, f32[320]{0:T(512)}, f32[320]{0:T(512)}, f32[320]{0:T(512)}, /*index=5*/f32[320]{0:T(512)}, f32[320]{0:T(512)}, f32[320]{0:T(512)}, f32[640]{0:T(1024)}) all-reduce(f32[640]{0:T(1024)S(1)} %get-tuple-element.42, ...), channel_id=1, replica_groups=mesh['seq'=16,'ch'=2] {'seq'}, use_global_device_ids=true, to_apply=%region_26.0 | all-reduce | flops 3840 | bytes 30720 | tf_op jit(solution)/shard_map/psum | solution.py:246
  1193.6 60.6 %all-reduce.9.cloned.1.call-done = (f32[320,1280]{1,0:T(8,128)}, f32[5,320,640]{2,1,0:T(8,128)}, f32[320,1280]{1,0:T(8,128)}) async-done(((f32[320,1280]{1,0:T(8,128)}, f32[5,320,640]{2,1,0:T(8,128)}, f32[320,1280]{1,0:T(8,128)}), (f32[320,1280]{1,0:T(8,128)}, f32[5,320,640]{2,1,0:T(8,128)}, f32[320,1280]{1,0:T(8,128)})) %all-reduce.9.cloned.1.call-update) | async-done | bytes 7372816 | tf_op jit(solution)/shard_map/psum | solution.py:246
  (136 shorter events, 132.0 us)
Async XLA Ops:
  7.2 359.9 %copy-start = (bf16[320,1280]{1,0:T(8,128)(2,1)S(1)}, bf16[320,1280]{1,0:T(8,128)(2,1)}, u32[]{:S(2)}) copy-start(bf16[320,1280]{1,0:T(8,128)(2,1)} %param.28) | copy-start | bytes 2457604
  7.2 228.4 %all-gather.3.cloned.1.call-start = ((), (), s32[]{:S(2)}) async-start(), calls=%async_computation.3 | async-start | bytes 11796480 | tf_op jit(solution)/shard_map/all_gather | solution.py:78
  17.6 50.9 %copy-start.10 = (bf16[320,1280]{1,0:T(8,128)(2,1)S(1)}, bf16[320,1280]{1,0:T(8,128)(2,1)}, u32[]{:S(2)}) copy-start(bf16[320,1280]{1,0:T(8,128)(2,1)} %param.20) | copy-start | bytes 2457604
  17.6 50.9 %copy-start.17 = (f32[320]{0:T(512)S(1)}, f32[320]{0:T(512)}, u32[]{:S(2)}) copy-start(f32[320]{0:T(512)} %param.21) | copy-start | bytes 3844
  68.6 26.6 %copy-start.16 = (f32[320]{0:T(512)S(1)}, f32[320]{0:T(512)}, u32[]{:S(2)}) copy-start(f32[320]{0:T(512)} %param.22) | copy-start | bytes 3844
  68.6 26.6 %copy-start.24 = (f32[320]{0:T(512)S(1)}, f32[320]{0:T(512)}, u32[]{:S(2)}) copy-start(f32[320]{0:T(512)} %param.23) | copy-start | bytes 3844
  114.8 5.6 collective-permute-start
  119.1 4.8 collective-permute-start.1
  131.5 104.1 %copy-start.8 = (bf16[5,320,640]{2,1,0:T(8,128)(2,1)S(1)}, bf16[5,320,640]{2,1,0:T(8,128)(2,1)}, u32[]{:S(2)}) copy-start(bf16[5,320,640]{2,1,0:T(8,128)(2,1)} %param.24) | copy-start | bytes 6144004
  131.5 235.6 %all-gather.5.cloned.1.call-start = ((), (), s32[]{:S(2)}) async-start(), calls=%async_computation.5 | async-start | bytes 15728640 | tf_op jit(solution)/shard_map/all_gather | solution.py:179
  132.3 454.5 %reduce-scatter.6.cloned.1.call-start = ((), (), s32[]{:S(2)}) async-start(), calls=%async_computation.6 | async-start | bytes 15728640 | tf_op jit(solution)/shard_map/reduce_scatter | solution.py:210
  235.6 8.4 copy-start.2
  256.4 18.1 %copy-start.23 = (f32[320]{0:T(512)S(1)}, f32[320]{0:T(512)}, u32[]{:S(2)}) copy-start(f32[320]{0:T(512)} %param.26) | copy-start | bytes 3844
  256.5 18.1 %copy-start.28 = (f32[320]{0:T(512)S(1)}, f32[320]{0:T(512)}, u32[]{:S(2)}) copy-start(f32[320]{0:T(512)} %param.27) | copy-start | bytes 3844
  397.0 13.9 %collective-permute-start.2 = (bf16[16,320,32]{1,2,0:T(8,128)(2,1)}, bf16[16,320,32]{1,2,0:T(8,128)(2,1)}, u32[]{:S(2)}, u32[]{:S(2)}) collective-permute-start(bf16[16,320,32]{1,2,0:T(8,128)(2,1)} %copy.43), channel_id=1, source_target_pairs={{2,0},{4,2},{6,4},{8,6},{10,8},{12,10},{14,12},{16,14},{18,16},{20... | collective-permute-start | bytes 983048 | tf_op jit(solution)/shard_map/ppermute | solution.py:23
  400.6 29.0 %collective-permute-start.3 = (bf16[16,320,32]{1,2,0:T(8,128)(2,1)}, bf16[16,320,32]{1,2,0:T(8,128)(2,1)}, u32[]{:S(2)}, u32[]{:S(2)}) collective-permute-start(bf16[16,320,32]{1,2,0:T(8,128)(2,1)} %copy.48), channel_id=1, source_target_pairs={{0,2},{2,4},{4,6},{6,8},{8,10},{10,12},{12,14},{14,16},{16,18},{18... | collective-permute-start | bytes 983048 | tf_op jit(solution)/shard_map/ppermute | solution.py:22
  413.2 8.6 copy-start.6
  463.6 392.7 %reduce-scatter.8.cloned.1.call-start = ((), (), s32[]{:S(2)}) async-start(), calls=%async_computation.7 | async-start | bytes 31457280 | tf_op jit(solution)/shard_map/reduce_scatter | solution.py:228
  620.8 472.2 %reduce-scatter.4.cloned.1.call-start = ((), (), s32[]{:S(2)}) async-start(), calls=%async_computation.4 | async-start | bytes 31457280 | tf_op jit(solution)/shard_map/reduce_scatter | solution.py:111
  633.4 620.8 %all-reduce.9.cloned.1.call-start = ((), (), s32[]{:S(2)}) async-start(), calls=%async_computation.8 | async-start | bytes 14745600 | tf_op jit(solution)/shard_map/psum | solution.py:246
  661.5 13.6 %slice-start = ((s8[7864320]{0:T(1024)(128)(4,1)}), s8[4194304]{0:T(1024)(128)(4,1)S(1)}, s32[]{:S(2)}) async-start(s8[7864320]{0:T(1024)(128)(4,1)} %bitcast.157), calls=%async_computation.9 | async-start | bytes 8388608
  678.7 11.5 slice-start.2
  678.7 11.5 slice-start.3
  682.3 7.9 copy-start.4
  682.3 7.9 slice-start.4
  695.0 161.3 %copy-start.13 = (f32[16,256]{1,0:T(8,128)S(1)}, f32[16,256]{1,0:T(8,128)}, u32[]{:S(2)}) copy-start(f32[16,256]{1,0:T(8,128)} %copy-done.12) | copy-start | bytes 49156
  695.0 161.3 %copy-start.15 = (f32[16,256]{1,0:T(8,128)S(1)}, f32[16,256]{1,0:T(8,128)}, u32[]{:S(2)}) copy-start(f32[16,256]{1,0:T(8,128)} %copy-done.14) | copy-start | bytes 49156
  695.0 398.1 %copy-start.26 = (f32[640]{0:T(1024)S(1)}, f32[640]{0:T(1024)}, u32[]{:S(2)}) copy-start(f32[640]{0:T(1024)} %param.29) | copy-start | bytes 7684
  1122.4 7.9 copy-start.25
  1122.4 7.9 copy-start.29
  1122.4 7.9 copy-start.30
  1254.2 7.2 copy-start.9
  (14 other events, 48.2 us)
Sparse Core Ops, SparseCore 0:
  131.6 103.8 all-gather.2
  237.1 129.8 all-gather.4
  463.7 122.9 reduce-scatter.5
  620.9 235.3 reduce-scatter.7
  858.5 234.5 reduce-scatter.3
  1098.1 156.0 all-reduce.8
where the time goes:
time: 1270 us
  waiting for transfers between devices  723 us (57%)
  other arithmetic  168 us (13%)
  matrix products  165 us (13%)
  blocking collectives  114 us (9%)
  local copies, waits for them, and re-layouts  76.4 us (6%)
  between operations  14.7 us (1%)
    reduce_scatter x1, waiting for transfers between devices, finish(): share = lax.psum_scatter(branch, 'ch', scatter_dimension=1, tiled=True)  195 us
    reduce_scatter x1, waiting for transfers between devices, body(): lax.psum_scatter(first_part, 'ch', scatter_dimension=1, tiled=True)  161 us
    reduce_scatter x1, waiting for transfers between devices, body(): lax.psum_scatter(backward_portion, 'ch', scatter_dimension=1, tiled=True)  123 us
    all_gather x1, waiting for transfers between devices, forward(): padded = lax.all_gather(border_trimmed, 'ch', axis=1, tiled=True)  103 us
    all_gather x1, waiting for transfers between devices, body(): grad_full = lax.all_gather(cotangent, 'ch', axis=1, tiled=True)  77.7 us
    psum x1, blocking collectives, body(): lax.psum((grad_ln1_gain, grad_ln1_bias, grad_w_in, grad_b_in, grad_ln2_ga...  63.3 us
    psum x1, waiting for transfers between devices, body(): lax.psum((grad_ln1_gain, grad_ln1_bias, grad_w_in, grad_b_in, grad_ln2_ga...  60.6 us
    dot_general x5, matrix products, body(): jnp.einsum('sol,oi->sil', window, conv_w[kernel_tap], preferred_element_t...  54.5 us
  transfers between devices with their start and end apart: 10, of which 7 were waited for; matrix products, arithmetic and copies ran while one was open for 18% of the time, Pallas kernels for 0%

commit v1 on v0

v1 whole, which is shorter than its diff:
```python
import functools
import math

import jax
import jax.numpy as jnp
from jax import lax
from jax.experimental import pallas as pl
from jax.experimental.pallas import tpu as pltpu
from jax.sharding import PartitionSpec as P

D = 1280
INNER = 640
KERNEL = 5
DILATION = 16
REACH = KERNEL // 2 * DILATION
EPS = 1e-05
HALF_ROOT = math.sqrt(0.5)
DENSITY = 1.0 / math.sqrt(2.0 * math.pi)
F32 = jnp.float32
BF16 = jnp.bfloat16
LANES = 128
VMEM_BYTES = 60 * 1024 * 1024


def rows_of(width):
    return next(r for r in (64, 32, 16) if width % r == 0)


def fold_rows(v):
    return v.reshape(v.shape[0] // 8, 8, v.shape[1]).sum(0)


def fold_lanes(v):
    out = v[:, :LANES]
    for j in range(1, v.shape[1] // LANES):
        out = out + v[:, j * LANES : (j + 1) * LANES]
    return out


def spread(p, length):
    return jnp.concatenate([p] * (length // LANES), axis=1)


def loop(width, body, init):
    rows = rows_of(width)

    def step(i, carry):
        return body(pl.ds(pl.multiple_of(i * rows, rows), rows), carry)

    return lax.fori_loop(0, width // rows, step, init)


def norm_stats(load, width, length):
    zero = jnp.zeros((8, length), F32)
    total = loop(width, lambda sl, a: a + fold_rows(load(sl)), zero)
    mean = total.sum(0, keepdims=True) / width

    def square(sl, a):
        c = load(sl) - mean
        return a + fold_rows(c * c)

    total = loop(width, square, zero)
    return mean, lax.rsqrt(total.sum(0, keepdims=True) / width + EPS)


def cdf(p):
    return 0.5 + 0.5 * lax.erf(p * HALF_ROOT)


def slope(p, phi):
    return phi + p * (DENSITY * jnp.exp(p * p * -0.5))


def call(kernel, grid, in_specs, out_specs, out_shape, scratch=(), prefetch=1, aliases=None, cost=None):
    return pl.pallas_call(
        kernel,
        grid_spec=pltpu.PrefetchScalarGridSpec(
            num_scalar_prefetch=prefetch,
            grid=grid,
            in_specs=in_specs,
            out_specs=out_specs,
            scratch_shapes=list(scratch),
        ),
        out_shape=out_shape,
        input_output_aliases=aliases or {},
        cost_estimate=cost,
        compiler_params=pltpu.CompilerParams(vmem_limit_bytes=VMEM_BYTES),
    )


def cost_of(macs, bytes_accessed):
    return pl.CostEstimate(flops=int(2 * macs), bytes_accessed=int(bytes_accessed), transcendentals=0)


def whole(shape):
    return pl.BlockSpec(shape, lambda i, pre: (0,) * len(shape), pipeline_mode=pl.Buffered(1))


def sds(shape, dtype):
    return jax.ShapeDtypeStruct(shape, dtype)


def first_kernel(pre, x_ref, p_ref, first_ref, stat_ref):
    length = x_ref.shape[2]
    mean, scale = norm_stats(lambda sl: x_ref[0, sl, :].astype(F32), D, length)
    stat_ref[0, 0:1, :] = mean
    stat_ref[0, 1:2, :] = scale

    def body(sl, carry):
        hat = (x_ref[0, sl, :].astype(F32) - mean) * scale
        point = hat * spread(p_ref[0, sl, :], length) + spread(p_ref[1, sl, :], length)
        first_ref[0, sl, :] = (point * cdf(point)).astype(BF16)
        return carry

    loop(D, body, 0)


def first_call(pre, tokens, p1, count, offset):
    seqs, _, length = tokens.shape
    return call(
        first_kernel,
        (count,),
        [
            pl.BlockSpec((1, D, length), lambda i, pre: ((pre[0] + offset + i) % seqs, 0, 0)),
            whole((2, D, LANES)),
        ],
        (
            pl.BlockSpec((1, D, length), lambda i, pre: (i, 0, 0)),
            pl.BlockSpec((1, 2, length), lambda i, pre: (i, 0, 0)),
        ),
        (sds((count, D, length), BF16), sds((count, 2, length), F32)),
        cost=cost_of(count * D * length * 40, count * D * length * 4),
    )(pre, tokens, p1)


def middle_kernel(group, keep, pre, first_ref, mask_ref, w_ref, p_ref, mid_ref, lead_ref, trail_ref, *rest):
    nar_ref = rest[-1]
    length = first_ref.shape[2]
    nar_ref[...] = jnp.dot(w_ref[...], first_ref[0], preferred_element_type=F32)
    mean, scale = norm_stats(lambda sl: nar_ref[sl, :] + spread(p_ref[0, sl, :], length), INNER, length)
    mask = mask_ref[0].astype(F32)

    def body(sl, carry):
        hat = (nar_ref[sl, :] + spread(p_ref[0, sl, :], length) - mean) * scale
        point = hat * spread(p_ref[1, sl, :], length) + spread(p_ref[2, sl, :], length)
        phi = cdf(point)
        mid_ref[0, sl, :] = (point * phi * mask).astype(BF16)
        if keep:
            rest[0][0, sl, :] = hat.astype(BF16)
            rest[1][0, sl, :] = (slope(point, phi) * mask).astype(BF16)
        return carry

    loop(INNER, body, 0)
    if keep:
        rest[2][0] = scale
    place = pl.program_id(0) % group
    for k in range(group):

        @pl.when(place == k)
        def _():
            lead_ref[0, :, k * REACH : (k + 1) * REACH] = mid_ref[0, :, :REACH]
            trail_ref[0, :, k * REACH : (k + 1) * REACH] = mid_ref[0, :, length - REACH :]


def middle_call(pre, first, mask, w_in, p2, count, offset, group, keep):
    _, _, length = first.shape
    seqs = mask.shape[0]
    edge = pl.BlockSpec((1, INNER, group * REACH), lambda i, pre: (i // group, 0, 0))
    edge_shape = sds((count // group, INNER, group * REACH), BF16)
    own = pl.BlockSpec((1, INNER, length), lambda i, pre: (i, 0, 0))
    outs = [own, edge, edge]
    shapes = [sds((count, INNER, length), BF16), edge_shape, edge_shape]
    if keep:
        outs += [own, own, pl.BlockSpec((1, 1, length), lambda i, pre: (i, 0, 0))]
        shapes += [sds((count, INNER, length), BF16)] * 2 + [sds((count, 1, length), F32)]
    return call(
        functools.partial(middle_kernel, group, keep),
        (count,),
        [
            pl.BlockSpec((1, D, length), lambda i, pre: (i, 0, 0)),
            pl.BlockSpec((1, 1, length), lambda i, pre: ((pre[0] + offset + i) % seqs, 0, 0)),
            whole((INNER, D)),
            whole((3, INNER, LANES)),
        ],
        tuple(outs),
        tuple(shapes),
        scratch=[pltpu.VMEM((INNER, length), F32)],
        cost=cost_of(count * INNER * D * length * 1.5, count * (D + INNER * 3) * length * 2),
    )(pre, first, mask.reshape(seqs, 1, length), w_in, p2)


def gather_windows(group, place, body_ref, before_ref, after_ref, pad_ref, cat_ref, order):
    width, length = body_ref.shape[1], body_ref.shape[2]
    pad_ref[:, LANES : LANES + length] = body_ref[0]
    for k in range(group):

        @pl.when(place == k)
        def _():
            pad_ref[:, LANES - REACH : LANES] = before_ref[0, :, k * REACH : (k + 1) * REACH]
            pad_ref[:, LANES + length : LANES + length + REACH] = after_ref[0, :, k * REACH : (k + 1) * REACH]

    for tap in range(KERNEL):
        start = LANES + order * (tap - KERNEL // 2) * DILATION
        cat_ref[tap * width : (tap + 1) * width, :] = pad_ref[:, start : start + length]


def last_kernel(
    group, keep, pre, mid_ref, before_ref, after_ref, x_ref, dy_ref, wc_ref, wo_ref, p_ref, b_ref, *rest
):
    if keep:
        mixed_ref, gw_ref, gb_ref, hat_ref, gp_ref, scale_ref = rest[:6]
    else:
        mixed_ref, gw_ref, gb_ref = rest[1:4]
    pad_ref, cat_ref, conv_ref, last_ref = rest[-4:]
    length = mid_ref.shape[2]
    step = pl.program_id(0)
    gather_windows(group, step % group, mid_ref, before_ref, after_ref, pad_ref, cat_ref, 1)
    conv_ref[...] = jnp.dot(wc_ref[...], cat_ref[...], preferred_element_type=F32)
    mean, scale = norm_stats(lambda sl: conv_ref[sl, :] + spread(p_ref[0, sl, :], length), INNER, length)

    def body(sl, carry):
        hat = (conv_ref[sl, :] + spread(p_ref[0, sl, :], length) - mean) * scale
        point = hat * spread(p_ref[1, sl, :], length) + spread(p_ref[2, sl, :], length)
        phi = cdf(point)
        last_ref[sl, :] = (point * phi).astype(BF16)
        if keep:
            hat_ref[0, sl, :] = hat.astype(BF16)
            gp_ref[0, sl, :] = slope(point, phi).astype(BF16)
        return carry

    loop(INNER, body, 0)
    if keep:
        scale_ref[0] = scale
    branch = jnp.dot(wo_ref[...], last_ref[...], preferred_element_type=F32)
    mixed_ref[0] = (x_ref[0].astype(F32) + branch + spread(b_ref[...], length)).astype(BF16)

    @pl.when(step == 0)
    def _():
        gw_ref[...] = jnp.zeros_like(gw_ref)
        gb_ref[...] = jnp.zeros_like(gb_ref)

    gw_ref[...] += lax.dot_general(
        last_ref[...], dy_ref[0], (((1,), (1,)), ((), ())), preferred_element_type=F32
    )
    gb_ref[...] += fold_lanes(dy_ref[0].astype(F32))


def last_call(pre, mid, before, after, tokens, cot, wc, wo_t, p2, b_out, count, offset, group, keep, mixed):
    _, _, length = mid.shape
    seqs, share, _ = cot.shape
    edge = pl.BlockSpec((1, INNER, group * REACH), lambda i, pre: (i // group, 0, 0))
    own = pl.BlockSpec((1, INNER, length), lambda i, pre: (i, 0, 0))

    def seq_at(i, pre):
        return (pre[0] + offset + i) % seqs

    outs = [
        pl.BlockSpec((1, share, length), lambda i, pre: (seq_at(i, pre), 0, 0)),
        pl.BlockSpec((INNER, share), lambda i, pre: (0, 0)),
        pl.BlockSpec((share, LANES), lambda i, pre: (0, 0)),
    ]
    shapes = [sds((seqs, share, length), BF16), sds((INNER, share), F32), sds((share, LANES), F32)]
    in_specs = [
        own,
        edge,
        edge,
        pl.BlockSpec((1, share, length), lambda i, pre: (seq_at(i, pre), pre[1], 0)),
        pl.BlockSpec((1, share, length), lambda i, pre: (seq_at(i, pre), 0, 0)),
        whole((INNER, KERNEL * INNER)),
        whole((share, INNER)),
        whole((3, INNER, LANES)),
        whole((share, LANES)),
    ]
    args = [pre, mid, before, after, tokens, cot, wc, wo_t, p2, b_out]
    aliases = None
    if keep:
        outs += [own, own, pl.BlockSpec((1, 1, length), lambda i, pre: (i, 0, 0))]
        shapes += [sds((count, INNER, length), BF16)] * 2 + [sds((count, 1, length), F32)]
    else:
        in_specs.append(pl.BlockSpec(memory_space=pl.ANY))
        args.append(mixed)
        aliases = {len(args) - 1: 0}
    return call(
        functools.partial(last_kernel, group, keep),
        (count,),
        in_specs,
        tuple(outs),
        tuple(shapes),
        scratch=[
            pltpu.VMEM((INNER, length + 2 * LANES), BF16),
            pltpu.VMEM((KERNEL * INNER, length), BF16),
            pltpu.VMEM((INNER, length), F32),
            pltpu.VMEM((INNER, length), BF16),
        ],
        aliases=aliases,
        cost=cost_of(count * INNER * (KERNEL * INNER + 2 * share) * length * 1.3, count * share * 6 * length * 2),
    )(*args)


def rear_kernel(group, chs, pre, *refs):
    dy_refs = refs[:chs]
    w_ref, hat_ref, gp_ref, scale_ref, p_ref = refs[chs : chs + 5]
    dconv_ref, lead_ref, trail_ref, gg_ref, gb_ref, gc_ref = refs[chs + 5 : chs + 11]
    dy_ref, d_ref = refs[chs + 11 :]
    share, length = dy_refs[0].shape[1], dy_refs[0].shape[2]
    step = pl.program_id(0)

    @pl.when(step == 0)
    def _():
        gg_ref[...] = jnp.zeros_like(gg_ref)
        gb_ref[...] = jnp.zeros_like(gb_ref)
        gc_ref[...] = jnp.zeros_like(gc_ref)

    for r in range(chs):
        at = pl.multiple_of(((pre[1] + chs - r) % chs) * share, share)
        dy_ref[pl.ds(at, share), :] = dy_refs[r][0]
    d_ref[...] = jnp.dot(w_ref[...], dy_ref[...], preferred_element_type=F32)
    scale = scale_ref[0]
    zero = jnp.zeros((8, length), F32)

    def body(sl, carry):
        d_pre = d_ref[sl, :] * gp_ref[0, sl, :].astype(F32)
        hat = hat_ref[0, sl, :].astype(F32)
        gg_ref[sl, :] += fold_lanes(d_pre * hat)
        gb_ref[sl, :] += fold_lanes(d_pre)
        e = d_pre * spread(p_ref[0, sl, :], length)
        d_ref[sl, :] = e
        return carry[0] + fold_rows(e), carry[1] + fold_rows(e * hat)

    total, dot = loop(INNER, body, (zero, zero))
    total = total.sum(0, keepdims=True) * (scale / INNER)
    dot = dot.sum(0, keepdims=True) * (scale / INNER)

    def finish(sl, carry):
        v = (d_ref[sl, :] * scale - total - hat_ref[0, sl, :].astype(F32) * dot).astype(BF16)
        dconv_ref[0, sl, :] = v
        gc_ref[sl, :] += fold_lanes(v.astype(F32))
        return carry

    loop(INNER, finish, 0)
    place = step % group
    for k in range(group):

        @pl.when(place == k)
        def _():
            lead_ref[0, :, k * REACH : (k + 1) * REACH] = dconv_ref[0, :, :REACH]
            trail_ref[0, :, k * REACH : (k + 1) * REACH] = dconv_ref[0, :, length - REACH :]


def rear_call(pre, cot, others, w_out, hat, gp, scale, p2, begin, count, group):
    seqs, share, length = cot.shape
    chs = 1 + len(others)
    edge = pl.BlockSpec((1, INNER, group * REACH), lambda i, pre: (i // group, 0, 0))
    edge_shape = sds((count // group, INNER, group * REACH), BF16)
    own = pl.BlockSpec((1, INNER, length), lambda i, pre: (i, 0, 0))
    kept = pl.BlockSpec((1, INNER, length), lambda i, pre: (begin + i, 0, 0))
    part = pl.BlockSpec((INNER, LANES), lambda i, pre: (0, 0))
    part_shape = sds((INNER, LANES), F32)
    return call(
        functools.partial(rear_kernel, group, chs),
        (count,),
        [pl.BlockSpec((1, share, length), lambda i, pre: (pre[0] + begin + i, 0, 0))]
        + [pl.BlockSpec((1, share, length), lambda i, pre: (i, 0, 0))] * (chs - 1)
        + [
            whole((INNER, D)),
            kept,
            kept,
            pl.BlockSpec((1, 1, length), lambda i, pre: (begin + i, 0, 0)),
            whole((1, INNER, LANES)),
        ],
        (own, edge, edge, part, part, part),
        (sds((count, INNER, length), BF16), edge_shape, edge_shape, part_shape, part_shape, part_shape),
        scratch=[pltpu.VMEM((D, length), BF16), pltpu.VMEM((INNER, length), F32)],
        cost=cost_of(count * INNER * D * length * 1.5, count * INNER * 5 * length * 2),
    )(pre, cot, *others, w_out, hat, gp, scale, p2)


def front_kernel(group, chs, pre, *refs):
    (
        dconv_ref,
        before_ref,
        after_ref,
        mid_ref,
        hat_ref,
        gp_ref,
        scale_ref,
        x_ref,
        stat_ref,
        dy_ref,
        wc_ref,
        wi_ref,
        p2_ref,
        p1_ref,
    ) = refs[:14]
    refs = refs[14:]
    gt_ref = refs[0]
    send_refs = refs[1:chs]
    gcw_ref, gwi_ref, gg2_ref, gb2_ref, gbi_ref, gg1_ref, gb1_ref = refs[chs : chs + 7]
    pad_ref, cat_ref, d_ref, dn_ref, df_ref, first_ref = refs[chs + 7 :]
    share, length = dy_ref.shape[1], dy_ref.shape[2]
    step = pl.program_id(0)

    @pl.when(step == 0)
    def _():
        for ref in (gcw_ref, gwi_ref, gg2_ref, gb2_ref, gbi_ref, gg1_ref, gb1_ref):
            ref[...] = jnp.zeros_like(ref)

    gather_windows(group, step % group, dconv_ref, before_ref, after_ref, pad_ref, cat_ref, -1)
    d_ref[...] = jnp.dot(wc_ref[...], cat_ref[...], preferred_element_type=F32)
    gcw_ref[...] += lax.dot_general(
        cat_ref[...], mid_ref[0], (((1,), (1,)), ((), ())), preferred_element_type=F32
    )
    scale = scale_ref[0]
    zero = jnp.zeros((8, length), F32)

    def body(sl, carry):
        d_pre = d_ref[sl, :] * gp_ref[0, sl, :].astype(F32)
        hat = hat_ref[0, sl, :].astype(F32)
        gg2_ref[sl, :] += fold_lanes(d_pre * hat)
        gb2_ref[sl, :] += fold_lanes(d_pre)
        e = d_pre * spread(p2_ref[0, sl, :], length)
        d_ref[sl, :] = e
        return carry[0] + fold_rows(e), carry[1] + fold_rows(e * hat)

    total, dot = loop(INNER, body, (zero, zero))
    total = total.sum(0, keepdims=True) * (scale / INNER)
    dot = dot.sum(0, keepdims=True) * (scale / INNER)

    def finish(sl, carry):
        v = (d_ref[sl, :] * scale - total - hat_ref[0, sl, :].astype(F32) * dot).astype(BF16)
        dn_ref[sl, :] = v
        gbi_ref[sl, :] += fold_lanes(v.astype(F32))
        return carry

    loop(INNER, finish, 0)
    df_ref[...] = jnp.dot(wi_ref[...], dn_ref[...], preferred_element_type=F32)
    mean_in, scale_in = stat_ref[0, 0:1, :], stat_ref[0, 1:2, :]

    def inner(sl, carry):
        hat = (x_ref[0, sl, :].astype(F32) - mean_in) * scale_in
        gain = spread(p1_ref[0, sl, :], length)
        point = hat * gain + spread(p1_ref[1, sl, :], length)
        phi = cdf(point)
        first_ref[sl, :] = (point * phi).astype(BF16)
        d_pre = df_ref[sl, :] * slope(point, phi)
        gg1_ref[sl, :] += fold_lanes(d_pre * hat)
        gb1_ref[sl, :] += fold_lanes(d_pre)
        e = d_pre * gain
        df_ref[sl, :] = e
        return carry[0] + fold_rows(e), carry[1] + fold_rows(e * hat)

    total, dot = loop(D, inner, (zero, zero))
    total = total.sum(0, keepdims=True) * (scale_in / D)
    dot = dot.sum(0, keepdims=True) * (scale_in / D)
    gwi_ref[...] += lax.dot_general(
        dn_ref[...], first_ref[...], (((1,), (1,)), ((), ())), preferred_element_type=F32
    )
    rows = rows_of(share)
    for r in range(chs):
        base = ((pre[1] + r) % chs) * share

        def out(i, carry):
            to = pl.ds(pl.multiple_of(i * rows, rows), rows)
            sl = pl.ds(pl.multiple_of(base + i * rows, rows), rows)
            hat = (x_ref[0, sl, :].astype(F32) - mean_in) * scale_in
            v = df_ref[sl, :] * scale_in - total - hat * dot
            if r == 0:
                gt_ref[0, to, :] = v + dy_ref[0, to, :].astype(F32)
            else:
                send_refs[r - 1][0, to, :] = v.astype(BF16)
            return carry

        lax.fori_loop(0, share // rows, out, 0)


def front_call(
    pre, dconv, before, after, mid, hat, gp, scale, tokens, stat, cot, wc_t, wi_t, p2, p1, chs, begin, count, group, gt
):
    seqs, share, length = cot.shape
    edge = pl.BlockSpec((1, INNER, group * REACH), lambda i, pre: (i // group, 0, 0))
    own = pl.BlockSpec((1, INNER, length), lambda i, pre: (i, 0, 0))
    kept = pl.BlockSpec((1, INNER, length), lambda i, pre: (begin + i, 0, 0))

    def seq_block(rows):
        return pl.BlockSpec((1, rows, length), lambda i, pre: (pre[0] + begin + i, 0, 0))

    def const(shape):
        return pl.BlockSpec(shape, lambda i, pre: (0,) * len(shape))

    in_specs = [
        own,
        edge,
        edge,
        kept,
        kept,
        kept,
        pl.BlockSpec((1, 1, length), lambda i, pre: (begin + i, 0, 0)),
        seq_block(D),
        pl.BlockSpec((1, 2, length), lambda i, pre: (begin + i, 0, 0)),
        seq_block(share),
        whole((INNER, KERNEL * INNER)),
        whole((D, INNER)),
        whole((1, INNER, LANES)),
        whole((2, D, LANES)),
    ]
    args = [pre, dconv, before, after, mid, hat, gp, scale, tokens, stat, cot, wc_t, wi_t, p2, p1]
    aliases = None
    kernel = functools.partial(front_kernel, group, chs)
    if gt is not None:
        in_specs.append(pl.BlockSpec(memory_space=pl.ANY))
        args.append(gt)
        aliases = {len(args) - 1: 0}

        def kernel(pre, *refs):
            front_kernel(group, chs, pre, *refs[:14], *refs[15:])

    inner_part, outer_part = (INNER, LANES), (D, LANES)
    consts = [(KERNEL * INNER, INNER), (INNER, D), inner_part, inner_part, inner_part, outer_part, outer_part]
    return call(
        kernel,
        (count,),
        in_specs,
        tuple(
            [seq_block(share)]
            + [pl.BlockSpec((1, share, length), lambda i, pre: (i, 0, 0))] * (chs - 1)
            + [const(s) for s in consts]
        ),
        tuple(
            [sds((seqs, share, length), F32)]
            + [sds((count, share, length), BF16)] * (chs - 1)
            + [sds(s, F32) for s in consts]
        ),
        scratch=[
            pltpu.VMEM((INNER, length + 2 * LANES), BF16),
            pltpu.VMEM((KERNEL * INNER, length), BF16),
            pltpu.VMEM((INNER, length), F32),
            pltpu.VMEM((INNER, length), BF16),
            pltpu.VMEM((D, length), F32),
            pltpu.VMEM((D, length), BF16),
        ],
        aliases=aliases,
        cost=cost_of(count * INNER * (2 * KERNEL * INNER + 2 * D) * length * 1.3, count * D * 8 * length * 2),
    )(*args)


def add_kernel(pre, part_ref, dy_ref, _, gt_ref):
    gt_ref[...] = part_ref[...].astype(F32) + dy_ref[...].astype(F32)


def add_call(pre, part, cot, gt, start):
    seqs, share, length = cot.shape
    count = part.shape[0]
    at = lambda i, pre: (pre[start] + i, 0, 0)
    return call(
        add_kernel,
        (count,),
        [
            pl.BlockSpec((1, share, length), lambda i, pre: (i, 0, 0)),
            pl.BlockSpec((1, share, length), at),
            pl.BlockSpec(memory_space=pl.ANY),
        ],
        pl.BlockSpec((1, share, length), at),
        sds((seqs, share, length), F32),
        aliases={3: 0},
        cost=cost_of(count * share * length, count * share * length * 8),
    )(pre, part, cot, gt)


def rotate(value, axis, count, by):
    return lax.ppermute(value, axis, [(i, (i + by) % count) for i in range(count)])


def shift(value, by):
    count = lax.axis_size("seq")
    pairs = [(i, i + by) for i in range(count) if 0 <= i + by < count]
    return lax.ppermute(value, "seq", pairs)


def rims(lead, trail):
    return shift(trail, 1), shift(lead, -1)


def full_weight(own, axis, ch, chs):
    seq = lax.axis_size("seq")
    rows = own.shape[axis]
    if rows % (seq * 4) == 0 and chs == 2:
        piece_rows = rows // seq
        piece = lax.dynamic_slice_in_dim(own, lax.axis_index("seq") * piece_rows, piece_rows, axis)
        piece = rotate(piece, "ch", 2, 1)
        other = lax.all_gather(piece, "seq", axis=axis, tiled=True)
        first = jnp.where(ch == 0, own, other)
        second = jnp.where(ch == 0, other, own)
        return jnp.concatenate([first, second], axis=axis)
    return lax.all_gather(own, "ch", axis=axis, tiled=True)


def lane_copies(vectors):
    return jnp.broadcast_to(vectors[..., None], vectors.shape + (LANES,))


def body(
    tokens,
    pad_mask,
    cotangent,
    ln1_gain,
    first_norm_bias,
    w_in,
    b_in,
    ln2_gain,
    ln2_bias,
    conv_w,
    conv_b,
    ln3_gain,
    ln3_bias,
    w_out,
    b_out,
):
    chs = lax.axis_size("ch")
    ch = lax.axis_index("ch")
    seqs, _, length = tokens.shape
    share = b_out.shape[0]
    part = b_in.shape[0]
    n = seqs // chs
    group = min(4, n // 2)
    pieces = 2
    size = n // pieces
    starts = [((ch + chs - r) % chs) * n for r in range(1, chs)]
    pre = jnp.stack(
        [ch * n, ch] + [s + q * size for s in starts for q in range(pieces)]
    ).astype(jnp.int32)

    others = []
    for q in range(pieces):
        got = []
        for r in range(1, chs):
            to = (ch + r) % chs
            block = lax.dynamic_slice_in_dim(cotangent, to * n + q * size, size, 0)
            got.append(rotate(block, "ch", chs, r))
        others.append(got)

    inner = jnp.stack([b_in, ln2_gain, ln2_bias, conv_b, ln3_gain, ln3_bias])
    inner = lax.all_gather(inner, "ch", axis=1, tiled=True)
    p1 = lane_copies(jnp.stack([ln1_gain, first_norm_bias]))
    p2 = lane_copies(inner)
    bo = lane_copies(b_out)
    w_in_full = full_weight(w_in, 0, ch, chs)
    conv_full = full_weight(conv_w, 1, ch, chs)
    w_out_full = full_weight(w_out, 0, ch, chs)
    wc = conv_full.transpose(1, 0, 2).reshape(INNER, KERNEL * INNER)
    wc_t = conv_full.transpose(2, 0, 1).reshape(INNER, KERNEL * INNER)
    wi_t = w_in_full.T
    wo_t = lax.dynamic_slice_in_dim(w_out_full, ch * share, share, 1).T

    first_own, stat_own = first_call(pre, tokens, p1, n, 0)
    first_oth, _ = first_call(pre, tokens, p1, seqs - n, n)
    mid_own, lead, trail, hat_mid, gp_mid, scale_mid = middle_call(
        pre, first_own, pad_mask, w_in_full, p2[0:3], n, 0, group, True
    )
    before, after = rims(lead, trail)
    mid_oth, lead, trail = middle_call(pre, first_oth, pad_mask, w_in_full, p2[0:3], seqs - n, n, group, False)
    before_oth, after_oth = rims(lead, trail)
    mixed, gwo_own, gbo_own, hat_out, gp_out, scale_out = last_call(
        pre, mid_own, before, after, tokens, cotangent, wc, wo_t, p2[3:6], bo, n, 0, group, True, None
    )
    rear = []
    for q in range(pieces):
        dconv, lead, trail, *sums = rear_call(
            pre, cotangent, others[q], w_out_full, hat_out, gp_out, scale_out, p2[4:5], q * size, size, group
        )
        rear.append((dconv, rims(lead, trail), sums))
    gt = None
    back = []
    sends = []
    for q in range(pieces):
        dconv, (lead, trail), _ = rear[q]
        gt, *rest = front_call(
            pre, dconv, lead, trail, mid_own, hat_mid, gp_mid, scale_mid, tokens, stat_own, cotangent,
            wc_t, wi_t, p2[1:2], p1, chs, q * size, size, group, gt,
        )
        sends.append([rotate(v, "ch", chs, r + 1) for r, v in enumerate(rest[: chs - 1])])
        back.append(rest[chs - 1 :])
    mixed, gwo_oth, gbo_oth = last_call(
        pre, mid_oth, before_oth, after_oth, tokens, cotangent, wc, wo_t, p2[3:6], bo, seqs - n, n, group, False, mixed
    )
    for q in range(pieces):
        for r in range(chs - 1):
            gt = add_call(pre, sends[q][r], cotangent, gt, 2 + r * pieces + q)

    gcw, gwi, gg2, gb2, gbi, gg1, gb1 = (sum(v[1:], v[0]) for v in zip(*back))
    gg3, gb3, gcb = (sum(v[1:], v[0]) for v in zip(*(r[2] for r in rear)))
    gwo = gwo_own + gwo_oth
    gbo = gbo_own + gbo_oth

    gwo_sum = lax.psum(gwo, "seq")
    gwo_all = lax.all_to_all(gwo_sum.astype(BF16), "ch", 0, 1, tiled=True).astype(F32)
    gcw = lax.psum_scatter(gcw.reshape(KERNEL, INNER, INNER), "ch", scatter_dimension=1, tiled=True)
    gcw = lax.psum(gcw, "seq")
    gwi = lax.psum_scatter(gwi, "ch", scatter_dimension=0, tiled=True)
    gwi = lax.psum(gwi, "seq")
    small = jnp.stack([v.sum(1) for v in (gbi, gg2, gb2, gcb, gg3, gb3)]).reshape(-1)
    outer = jnp.stack([gg1.sum(1), gb1.sum(1)]).reshape(-1)
    bo_slot = lax.dynamic_update_slice(jnp.zeros((D,), F32), gbo.sum(1), (ch * share,))
    total = lax.psum(jnp.concatenate([small, outer, bo_slot]), ("seq", "ch"))
    inner_sums = lax.dynamic_slice_in_dim(total[: 6 * INNER].reshape(6, INNER), ch * part, part, 1)
    outer_sums = lax.dynamic_slice_in_dim(total[6 * INNER :].reshape(3, D), ch * share, share, 1)
    return (
        mixed,
        gt,
        outer_sums[0],
        outer_sums[1],
        gwi,
        inner_sums[0],
        inner_sums[1],
        inner_sums[2],
        gcw,
        inner_sums[3],
        inner_sums[4],
        inner_sums[5],
        gwo_all,
        outer_sums[2],
    )


def solution(mesh):
    in_specs = (
        P(None, None, "seq"),
        P(None, "seq"),
        P(None, "ch", "seq"),
        P(),
        P(),
        P("ch", None),
        P("ch"),
        P("ch"),
        P("ch"),
        P(None, "ch", None),
        P("ch"),
        P("ch"),
        P("ch"),
        P("ch", None),
        P("ch"),
    )
    out_specs = (
        P(None, "ch", "seq"),
        P(None, "ch", "seq"),
        P("ch"),
        P("ch"),
        P("ch", None),
        P("ch"),
        P("ch"),
        P("ch"),
        P(None, "ch", None),
        P("ch"),
        P("ch"),
        P("ch"),
        P("ch", None),
        P("ch"),
    )
    return jax.shard_map(body, mesh=mesh, in_specs=in_specs, out_specs=out_specs, check_vma=False)
```

time: 1270 us -> 797 us (0.63)
  waiting for transfers between devices: 723 us -> 101 us
  Pallas kernels: 0 us -> 250 us
  matrix products: 165 us -> 0 us
  blocking collectives: 114 us -> 272 us
  other arithmetic: 168 us -> 44.1 us
  starting transfers between devices: 8.65 us -> 33.7 us
    reduce_scatter x3 -> x2, waiting for transfers between devices: 479 us -> 101 us  [the longest x1 99.6 us: body(): lax.psum_scatter(gcw.reshape(KERNEL, INNER, INNER), 'ch', scatter_dimensi...]
    pallas_call x0 -> x12, Pallas kernels: none -> 250 us  [the longest x2 82.5 us: front_call(): call(kernel, (count,), in_specs, tuple([seq_block(share)] + [pl.BlockSpec...]
    all_gather x2 -> x1, waiting for transfers between devices: 181 us -> 0.01 us  [full_weight(): other = lax.all_gather(piece, 'seq', axis=axis, tiled=True)]
    dot_general x21 -> x0, matrix products: 165 us -> none  [the longest x5 54.5 us: body(): jnp.einsum('sol,oi->sil', window, conv_w[kernel_tap], preferred_element_t...]
    all_gather x0 -> x3, blocking collectives: none -> 105 us  [the longest x1 56.1 us: body(): inner = lax.all_gather(inner, 'ch', axis=1, tiled=True)]
    convert_element_type x6 -> x0, other arithmetic: 81 us -> none  [the longest x1 50.9 us: forward(): first = gelu_exact(center * scale_in * column_slot(ln1_gain) + column_slo...]
    reduce_sum x7 -> x6, other arithmetic: 82.1 us -> 6.46 us  [the longest x4 3.21 us: body(): v.sum(1)]
    psum x1, waiting for transfers between devices: 60.6 us -> 0.01 us  [body(): gwi = lax.psum(gwi, 'seq')]
  transfers between devices with their start and end apart: 10 -> 20, of which waited for: 7 -> 2; matrix products, arithmetic and copies ran while one was open for 18% -> 13% of each run, Pallas kernels for 0% -> 26%
where the time goes in v1:
time: 797 us; the launch traced here: 789 us
  blocking collectives  272 us (34%)
  Pallas kernels  250 us (31%)
  waiting for transfers between devices  101 us (13%)
  local copies, waits for them, and re-layouts  73.1 us (9%)
  other arithmetic  44.1 us (6%)
  starting transfers between devices  33.7 us (4%)
  between operations  15 us (2%)
    reduce_scatter x1, waiting for transfers between devices, body(): lax.psum_scatter(gcw.reshape(KERNEL, INNER, INNER), 'ch', scatter_dimensi...  99.6 us
    psum x1, blocking collectives, body(): total = lax.psum(jnp.concatenate([small, outer, bo_slot]), ('seq', 'ch'))  87.3 us
    pallas_call x2, Pallas kernels, front_call(): call(kernel, (count,), in_specs, tuple([seq_block(share)] + [pl.BlockSpec...  82.5 us
    psum x1, blocking collectives, body(): gwo_sum = lax.psum(gwo, 'seq')  79.6 us
    pallas_call x2, Pallas kernels, last_call(): call(functools.partial(last_kernel, group, keep), (count,), in_specs, tup...  79 us
    all_gather x1, blocking collectives, body(): inner = lax.all_gather(inner, 'ch', axis=1, tiled=True)  56.1 us
    all_gather x2, blocking collectives, full_weight(): other = lax.all_gather(piece, 'seq', axis=axis, tiled=True)  49.2 us
    pallas_call x2, Pallas kernels, middle_call(): call(functools.partial(middle_kernel, group, keep), (count,), [pl.BlockSp...  33.3 us
  transfers between devices with their start and end apart: 20, of which 2 were waited for; matrix products, arithmetic and copies ran while one was open for 13% of the time, Pallas kernels for 26%

profile of v1, /device:TPU:0, one launch (start us, length us, event | category | flops | bytes accessed | tf_op | source)
XLA Modules:
  0.0 788.9 jit_solution(11418661555363772680)
XLA Ops:
  20.9 56.1 %all-gather.1 = f32[2,320,6]{1,2,0:T(8,128)S(1)} all-gather(f32[1,320,6]{1,2,0:T(8,128)S(1)} %bitcast.36), channel_id=1, replica_groups=mesh['seq'=16,'ch'=2] {'ch'}, dimensions={0}, use_global_device_ids=true | all-gather | bytes 23040 | tf_op jit(solution)/shard_map/all_gather | solution.py:642
  80.5 4.9 copy.97
  87.6 13.0 %shard_map.256 = (bf16[8,1280,256]{2,1,0:T(8,128)(2,1)}, f32[8,2,256]{2,1,0:T(2,128)}) custom-call(s32[4]{0:T(128)} %pad_add_fusion.pre, bf16[16,1280,256]{2,1,0:T(8,128)(2,1)} %refs_7_.3, f32[2,1280,128]{2,1,0:T(8,128)} %broadcast_in_dim.27.p_ref.refs_13_), custom_call_target="tpu_custom_call" | custom-call | flops 209715200 | bytes 10485760 | tf_op jit(solution)/shard_map/pallas_call | solution.py:120
  100.6 28.9 %all-gather = bf16[16,20,1280]{2,1,0:T(8,128)(2,1)S(1)} all-gather(bf16[1,20,1280]{2,1,0:T(8,128)(2,1)S(1)} %bitcast.35), channel_id=1, replica_groups=mesh['seq'=16,'ch'=2] {'seq'}, dimensions={0}, use_global_device_ids=true | all-gather | bytes 870400 | tf_op jit(solution)/shard_map/all_gather | solution.py:590
  131.0 20.3 %all-gather.2 = bf16[16,20,1280]{2,1,0:T(8,128)(2,1)S(1)} all-gather(bf16[1,20,1280]{2,1,0:T(8,128)(2,1)S(1)} %bitcast.34), channel_id=1, replica_groups=mesh['seq'=16,'ch'=2] {'seq'}, dimensions={0}, use_global_device_ids=true | all-gather | bytes 870400 | tf_op jit(solution)/shard_map/all_gather | solution.py:590
  155.8 3.6 copy.108.refs_2_
  163.7 3.5 copy.95.w_ref
  168.5 17.6 %shard_map.257 = (bf16[8,640,256]{2,1,0:T(8,128)(2,1)}, bf16[2,640,128]{2,1,0:T(8,128)(2,1)}, bf16[2,640,128]{2,1,0:T(8,128)(2,1)}, bf16[8,640,256]{2,1,0:T(8,12...) custom-call(s32[4]{0:T(128)} %pad_add_fusion.pre, bf16[8,1280,256]{2,1,0:T(8,128)(2,1)} %get-tuple-element.69.first_ref, ...), custom_call_target="tpu_custom_call" | custom-call | flops 5033164800 | bytes 13107200 | tf_op jit(solution)/shard_map/pallas_call | solution.py:176
  193.6 5.5 copy.98
  205.5 6.8 copy.107.wc_ref
  212.3 5.2 fusion.6
  217.4 7.8 copy.109
  225.3 6.9 copy.112.refs_10_
  234.3 40.0 %shard_map.258 = (bf16[16,640,256]{2,1,0:T(8,128)(2,1)}, f32[640,640]{1,0:T(8,128)}, f32[640,128]{1,0:T(8,128)}, bf16[8,640,256]{2,1,0:T(8,128)(2,1)}, bf16[8,64...) custom-call(s32[4]{0:T(128)} %pad_add_fusion.pre, bf16[8,640,256]{2,1,0:T(8,128)(2,1)} %get-tuple-element.70.mid_ref.refs_3_, ...), custom_call_target="tpu_custom_call" | custom-call | flops 15267266560 | bytes 15728640 | tf_op jit(solution)/shard_map/pallas_call | solution.py:283
  275.3 9.7 %shard_map.261 = (bf16[4,640,256]{2,1,0:T(8,128)(2,1)}, bf16[1,640,128]{2,1,0:T(8,128)(2,1)}, bf16[1,640,128]{2,1,0:T(8,128)(2,1)}, f32[640,128]{1,0:T(8,128)}, f32[640,128]{1,0:T(8,128)}, /*index=5*/f32[640,128]{1,0:T(8,128)}) custom-call(s32[4]{0:T(128)} %pad_add_fusion.pre, bf16[16,640,256]{2,1,0:T(8,128)(2,1)} %dy_ref.7, ...), custom_call_target="tpu_custom_call" | custom-call | flops 2516582400 | bytes 6553600 | tf_op jit(solution)/shard_map/pallas_call | solution.py:359
  289.8 9.8 %shard_map.260 = (bf16[4,640,256]{2,1,0:T(8,128)(2,1)}, bf16[1,640,128]{2,1,0:T(8,128)(2,1)}, bf16[1,640,128]{2,1,0:T(8,128)(2,1)}, f32[640,128]{1,0:T(8,128)}, f32[640,128]{1,0:T(8,128)}, /*index=5*/f32[640,128]{1,0:T(8,128)}) custom-call(s32[4]{0:T(128)} %pad_add_fusion.pre, bf16[16,640,256]{2,1,0:T(8,128)(2,1)} %dy_ref.7, ...), custom_call_target="tpu_custom_call" | custom-call | flops 2516582400 | bytes 6553600 | tf_op jit(solution)/shard_map/pallas_call | solution.py:359
  299.5 4.3 collective-permute-start.8
  306.2 41.0 %shard_map.262 = (f32[16,640,256]{2,1,0:T(8,128)}, bf16[4,640,256]{2,1,0:T(8,128)(2,1)}, f32[3200,640]{1,0:T(8,128)}, f32[640,1280]{1,0:T(8,128)}, f32[640,128]{...) custom-call(s32[4]{0:T(128)} %pad_add_fusion.pre, ...), custom_call_target="tpu_custom_call" | custom-call | flops 15267266560 | bytes 20971520 | tf_op jit(solution)/shard_map/pallas_call | solution.py:519
  348.0 41.5 %shard_map.263 = (f32[16,640,256]{2,1,0:T(8,128)}, bf16[4,640,256]{2,1,0:T(8,128)(2,1)}, f32[3200,640]{1,0:T(8,128)}, f32[640,1280]{1,0:T(8,128)}, f32[640,128]{...) custom-call(s32[4]{0:T(128)} %pad_add_fusion.pre, ...), custom_call_target="tpu_custom_call", output_to_operand_aliasing={{0}: (15, {})} | custom-call | flops 15267266560 | bytes 20971520 | tf_op jit(solution)/shard_map/pallas_call | solution.py:519
  389.5 4.0 add.100
  393.6 10.2 %add.102 = f32[3200,640]{1,0:T(8,128)} add(f32[3200,640]{1,0:T(8,128)} %get-tuple-element.112, f32[3200,640]{1,0:T(8,128)} %get-tuple-element.113) | non-fusion elementwise | flops 2048000 | bytes 24576000 | tf_op jit(solution)/shard_map/add | solution.py:689
  403.8 13.0 %shard_map.254 = (bf16[8,1280,256]{2,1,0:T(8,128)(2,1)}, f32[8,2,256]{2,1,0:T(2,128)}) custom-call(s32[4]{0:T(128)} %pad_add_fusion.pre, bf16[16,1280,256]{2,1,0:T(8,128)(2,1)} %refs_7_.3, f32[2,1280,128]{2,1,0:T(8,128)} %broadcast_in_dim.27.p_ref.refs_13_), custom_call_target="tpu_custom_call" | custom-call | flops 209715200 | bytes 10485760 | tf_op jit(solution)/shard_map/pallas_call | solution.py:120
  416.8 15.7 %shard_map.255 = (bf16[8,640,256]{2,1,0:T(8,128)(2,1)}, bf16[2,640,128]{2,1,0:T(8,128)(2,1)}, bf16[2,640,128]{2,1,0:T(8,128)(2,1)}) custom-call(s32[4]{0:T(128)} %pad_add_fusion.pre, bf16[8,1280,256]{2,1,0:T(8,128)(2,1)} %get-tuple-element.65.first_ref, s32[16,1,256]{2,1,0:T(1,128)} %reshape.88.mask_ref, bf16[640,1280]{1,0:T(8,128)(2,1)} %copy.95.w_ref, ...), custom_call_target="tpu_custom_call" | custom-call | flops 5033164800 | bytes 13107200 | tf_op jit(solution)/shard_map/pallas_call | solution.py:176
  432.6 4.2 collective-permute-start.1
  439.7 99.6 %reduce-scatter.5.cloned.1.call-done = f32[5,320,640]{2,1,0:T(8,128)} async-done(((f32[5,640,640]{2,1,0:T(8,128)}), f32[5,320,640]{2,1,0:T(8,128)}) %reduce-scatter.5.cloned.1.call-update) | async-done | bytes 4096016 | tf_op jit(solution)/shard_map/reduce_scatter | solution.py:696
  540.2 38.9 %shard_map.259 = (bf16[16,640,256]{2,1,0:T(8,128)(2,1)}, f32[640,640]{1,0:T(8,128)}, f32[640,128]{1,0:T(8,128)}) custom-call(s32[4]{0:T(128)} %pad_add_fusion.pre, bf16[8,640,256]{2,1,0:T(8,128)(2,1)} %get-tuple-element.66.mid_ref, bf16[2,640,128]{2,1,0:T(8,128)(2,1)} %copy-done.26, ...), custom_call_target="tpu_custom_call", output_to_operand_aliasing={{0}: (10, {})} | custom-call | flops 15267266560 | bytes 15728640 | tf_op jit(solution)/shard_map/pallas_call | solution.py:283
  580.8 79.6 %all-reduce.5 = bf16[640,640]{1,0:T(8,128)(2,1)} all-reduce(f32[640,640]{1,0:T(8,128)S(1)} %add.103), channel_id=1, replica_groups=mesh['seq'=16,'ch'=2] {'seq'}, use_global_device_ids=true, to_apply=%region_14.15 | all-reduce | flops 409600 | bytes 2457600 | tf_op jit(solution)/shard_map/psum | solution.py:694
  660.4 3.7 all-to-all-start
  673.2 87.3 %psum.28 = f32[7680]{0:T(1024)S(1)} all-reduce(f32[7680]{0:T(1024)S(1)} %pad_maximum_fusion.3), channel_id=1, replica_groups=mesh['seq'=16,'ch'=2] {'seq','ch'}, use_global_device_ids=true, to_apply=%region_9.10 | all-reduce | flops 7680 | bytes 61440 | tf_op jit(solution)/shard_map/psum | solution.py:703
  764.4 4.7 shard_map.264._
  770.2 4.7 shard_map.265
  777.5 4.4 copy.125
  (175 shorter events, 77.9 us)
Async XLA Ops:
  7.2 186.4 %all-gather.5.cloned.1.call-start = ((), (), s32[]{:S(2)}) async-start(), calls=%async_computation.3 | async-start | bytes 3481600 | tf_op jit(solution)/shard_map/all_gather | solution.py:590
  8.1 122.8 %collective-permute-start.4 = (bf16[20,1280]{1,0:T(8,128)(2,1)S(1)}, bf16[20,1280]{1,0:T(8,128)(2,1)S(1)}, u32[]{:S(2)}, u32[]{:S(2)}) collective-permute-start(bf16[20,1280]{1,0:T(8,128)(2,1)S(1)} %constant_dynamic-slice_fusion.3), channel_id=1, source_target_pairs={{0,1},{1,0},{2,3},{3,2},{4,5},{5,4},{6,7},{7,6},{8,9},{9,8},{10,11... | collective-permute-start | bytes 153608 | tf_op jit(solution)/shard_map/ppermute | solution.py:570
  12.1 88.5 %collective-permute-start = (bf16[20,1280]{1,0:T(8,128)(2,1)S(1)}, bf16[20,1280]{1,0:T(8,128)(2,1)S(1)}, u32[]{:S(2)}, u32[]{:S(2)}) collective-permute-start(bf16[20,1280]{1,0:T(8,128)(2,1)S(1)} %constant_dynamic-slice_fusion.5), channel_id=1, source_target_pairs={{0,1},{1,0},{2,3},{3,2},{4,5},{5,4},{6,7},{7,6},{8,9},{9,8},{10,11... | collective-permute-start | bytes 153608 | tf_op jit(solution)/shard_map/ppermute | solution.py:570
  13.1 64.0 %collective-permute-start.3 = (bf16[5,20,640]{2,1,0:T(8,128)(2,1)S(1)}, bf16[5,20,640]{2,1,0:T(8,128)(2,1)S(1)}, u32[]{:S(2)}, u32[]{:S(2)}) collective-permute-start(bf16[5,20,640]{2,1,0:T(8,128)(2,1)S(1)} %constant_dynamic-slice_fusion.4), channel_id=1, source_target_pairs={{0,1},{1,0},{2,3},{3,2},{4,5},{5,4},{6,7},{7,6},{8,9},{9,8},{10,11... | collective-permute-start | bytes 384008 | tf_op jit(solution)/shard_map/ppermute | solution.py:570
  15.2 5.6 copy-start.18
  15.3 63.3 %copy-start.7 = (bf16[320,1280]{1,0:T(8,128)(2,1)S(1)}, bf16[320,1280]{1,0:T(8,128)(2,1)}, u32[]{:S(2)}) copy-start(bf16[320,1280]{1,0:T(8,128)(2,1)} %param.20) | copy-start | bytes 2457604
  18.7 61.2 %copy-start.8 = (bf16[320,1280]{1,0:T(8,128)(2,1)S(1)}, bf16[320,1280]{1,0:T(8,128)(2,1)}, u32[]{:S(2)}) copy-start(bf16[320,1280]{1,0:T(8,128)(2,1)} %param.28) | copy-start | bytes 2457604
  18.7 255.7 %collective-permute-start.10 = (bf16[4,640,256]{2,1,0:T(8,128)(2,1)}, bf16[4,640,256]{2,1,0:T(8,128)(2,1)}, u32[]{:S(2)}, u32[]{:S(2)}) collective-permute-start(bf16[4,640,256]{2,1,0:T(8,128)(2,1)} %get-tuple-element.129), channel_id=1, source_target_pairs={{0,1},{1,0},{2,3},{3,2},{4,5},{5,4},{6,7},{7,6},{8,9},{9,8},{10,11... | collective-permute-start | bytes 3932168 | tf_op jit(solution)/shard_map/ppermute | solution.py:570
  18.8 271.0 %collective-permute-start.7 = (bf16[4,640,256]{2,1,0:T(8,128)(2,1)}, bf16[4,640,256]{2,1,0:T(8,128)(2,1)}, u32[]{:S(2)}, u32[]{:S(2)}) collective-permute-start(bf16[4,640,256]{2,1,0:T(8,128)(2,1)} %get-tuple-element.130), channel_id=1, source_target_pairs={{0,1},{1,0},{2,3},{3,2},{4,5},{5,4},{6,7},{7,6},{8,9},{9,8},{10,11... | collective-permute-start | bytes 3932168 | tf_op jit(solution)/shard_map/ppermute | solution.py:570
  77.8 361.9 %reduce-scatter.3.cloned.1.call-start = ((), (), s32[]{:S(2)}) async-start(), calls=%async_computation.4 | async-start | bytes 4915200 | tf_op jit(solution)/shard_map/reduce_scatter | solution.py:698
  186.1 5.8 copy-start.2
  186.1 46.1 %collective-permute-start.5 = (bf16[2,640,128]{2,1,0:T(8,128)(2,1)}, bf16[2,640,128]{2,1,0:T(8,128)(2,1)}, u32[]{:S(2)}, u32[]{:S(2)}) collective-permute-start(bf16[2,640,128]{2,1,0:T(8,128)(2,1)} %get-tuple-element.71), channel_id=1, source_target_pairs={{0,2},{2,4},{4,6},{6,8},{8,10},{10,12},{12,14},{14,16},{16,18},{18... | collective-permute-start | bytes 983048 | tf_op jit(solution)/shard_map/ppermute | solution.py:576
  189.2 42.9 %collective-permute-start.6 = (bf16[2,640,128]{2,1,0:T(8,128)(2,1)}, bf16[2,640,128]{2,1,0:T(8,128)(2,1)}, u32[]{:S(2)}, u32[]{:S(2)}) collective-permute-start(bf16[2,640,128]{2,1,0:T(8,128)(2,1)} %get-tuple-element.72), channel_id=1, source_target_pairs={{2,0},{4,2},{6,4},{8,6},{10,8},{12,10},{14,12},{16,14},{18,16},{20... | collective-permute-start | bytes 983048 | tf_op jit(solution)/shard_map/ppermute | solution.py:576
  225.3 6.9 copy-start.19
  285.0 20.4 %collective-permute-start.11 = (bf16[1,640,128]{2,1,0:T(8,128)(2,1)}, bf16[1,640,128]{2,1,0:T(8,128)(2,1)S(1)}, u32[]{:S(2)}, u32[]{:S(2)}) collective-permute-start(bf16[1,640,128]{2,1,0:T(8,128)(2,1)} %get-tuple-element.86), channel_id=1, source_target_pairs={{0,2},{2,4},{4,6},{6,8},{8,10},{10,12},{12,14},{14,16},{16,18},{18... | collective-permute-start | bytes 491528 | tf_op jit(solution)/shard_map/ppermute | solution.py:576
  288.5 16.9 %collective-permute-start.12 = (bf16[1,640,128]{2,1,0:T(8,128)(2,1)}, bf16[1,640,128]{2,1,0:T(8,128)(2,1)S(1)}, u32[]{:S(2)}, u32[]{:S(2)}) collective-permute-start(bf16[1,640,128]{2,1,0:T(8,128)(2,1)} %get-tuple-element.87), channel_id=1, source_target_pairs={{2,0},{4,2},{6,4},{8,6},{10,8},{12,10},{14,12},{16,14},{18,16},{20... | collective-permute-start | bytes 491528 | tf_op jit(solution)/shard_map/ppermute | solution.py:576
  299.5 47.7 %collective-permute-start.8 = (bf16[1,640,128]{2,1,0:T(8,128)(2,1)}, bf16[1,640,128]{2,1,0:T(8,128)(2,1)S(1)}, u32[]{:S(2)}, u32[]{:S(2)}) collective-permute-start(bf16[1,640,128]{2,1,0:T(8,128)(2,1)} %get-tuple-element.79), channel_id=1, source_target_pairs={{0,2},{2,4},{4,6},{6,8},{8,10},{10,12},{12,14},{14,16},{16,18},{18... | collective-permute-start | bytes 491528 | tf_op jit(solution)/shard_map/ppermute | solution.py:576
  303.8 43.5 %collective-permute-start.9 = (bf16[1,640,128]{2,1,0:T(8,128)(2,1)}, bf16[1,640,128]{2,1,0:T(8,128)(2,1)S(1)}, u32[]{:S(2)}, u32[]{:S(2)}) collective-permute-start(bf16[1,640,128]{2,1,0:T(8,128)(2,1)} %get-tuple-element.80), channel_id=1, source_target_pairs={{2,0},{4,2},{6,4},{8,6},{10,8},{12,10},{14,12},{16,14},{18,16},{20... | collective-permute-start | bytes 491528 | tf_op jit(solution)/shard_map/ppermute | solution.py:576
  348.0 41.5 %copy-start.3 = (f32[640,1280]{1,0:T(8,128)S(1)}, f32[640,1280]{1,0:T(8,128)}, u32[]{:S(2)}) copy-start(f32[640,1280]{1,0:T(8,128)} %get-tuple-element.110) | copy-start | bytes 9830404
  393.5 145.8 %reduce-scatter.5.cloned.1.call-start = ((), (), s32[]{:S(2)}) async-start(), calls=%async_computation.5 | async-start | bytes 12288000 | tf_op jit(solution)/shard_map/reduce_scatter | solution.py:696
  403.8 371.1 %all-reduce.4.cloned.1.call-start = ((), (), s32[]{:S(2)}) async-start(), calls=%async_computation.6 | async-start | bytes 11468800 | tf_op jit(solution)/shard_map/psum | solution.py:699
  432.6 106.8 %collective-permute-start.1 = (bf16[2,640,128]{2,1,0:T(8,128)(2,1)}, bf16[2,640,128]{2,1,0:T(8,128)(2,1)S(1)}, u32[]{:S(2)}, u32[]{:S(2)}) collective-permute-start(bf16[2,640,128]{2,1,0:T(8,128)(2,1)} %get-tuple-element.67), channel_id=1, source_target_pairs={{0,2},{2,4},{4,6},{6,8},{8,10},{10,12},{12,14},{14,16},{16,18},{18... | collective-permute-start | bytes 983048 | tf_op jit(solution)/shard_map/ppermute | solution.py:576
  436.7 102.6 %collective-permute-start.2 = (bf16[2,640,128]{2,1,0:T(8,128)(2,1)}, bf16[2,640,128]{2,1,0:T(8,128)(2,1)S(1)}, u32[]{:S(2)}, u32[]{:S(2)}) collective-permute-start(bf16[2,640,128]{2,1,0:T(8,128)(2,1)} %get-tuple-element.68), channel_id=1, source_target_pairs={{2,0},{4,2},{6,4},{8,6},{10,8},{12,10},{14,12},{16,14},{18,16},{20... | collective-permute-start | bytes 983048 | tf_op jit(solution)/shard_map/ppermute | solution.py:576
  540.2 38.9 %copy-start.4 = (f32[640,640]{1,0:T(8,128)S(1)}, f32[640,640]{1,0:T(8,128)}, u32[]{:S(2)}) copy-start(f32[640,640]{1,0:T(8,128)} %get-tuple-element.114) | copy-start | bytes 4915204
  580.7 83.3 %copy-start.9 = (f32[640,128]{1,0:T(8,128)S(1)}, f32[640,128]{1,0:T(8,128)}, u32[]{:S(2)}) copy-start(f32[640,128]{1,0:T(8,128)} %get-tuple-element.100) | copy-start | bytes 983044
  580.7 83.3 %copy-start.10 = (f32[640,128]{1,0:T(8,128)S(1)}, f32[640,128]{1,0:T(8,128)}, u32[]{:S(2)}) copy-start(f32[640,128]{1,0:T(8,128)} %get-tuple-element.102) | copy-start | bytes 983044
  580.7 83.3 %copy-start.11 = (f32[640,128]{1,0:T(8,128)S(1)}, f32[640,128]{1,0:T(8,128)}, u32[]{:S(2)}) copy-start(f32[640,128]{1,0:T(8,128)} %get-tuple-element.101) | copy-start | bytes 983044
  580.8 83.3 %copy-start.12 = (f32[640,128]{1,0:T(8,128)S(1)}, f32[640,128]{1,0:T(8,128)}, u32[]{:S(2)}) copy-start(f32[640,128]{1,0:T(8,128)} %get-tuple-element.103) | copy-start | bytes 983044
  580.8 83.8 %copy-start.13 = (f32[640,128]{1,0:T(8,128)S(1)}, f32[640,128]{1,0:T(8,128)}, u32[]{:S(2)}) copy-start(f32[640,128]{1,0:T(8,128)} %get-tuple-element.108) | copy-start | bytes 983044
  660.4 101.6 %all-to-all-start = ((bf16[2,320,640]{2,1,0:T(8,128)(2,1)}), bf16[2,320,640]{2,1,0:T(8,128)(2,1)S(1)}, u32[]{:S(2)}, u32[]{:S(2)}) async-start(bf16[2,320,640]{2,1,0:T(8,128)(2,1)} %bitcast.16), calls=%async_computation.2 | async-start | bytes 1638400 | tf_op jit(solution)/shard_map/all_to_all | solution.py:695
  666.0 103.1 %collective-permute-start.13 = (bf16[4,640,256]{2,1,0:T(8,128)(2,1)}, bf16[4,640,256]{2,1,0:T(8,128)(2,1)S(1)}, u32[]{:S(2)}, u32[]{:S(2)}) collective-permute-start(bf16[4,640,256]{2,1,0:T(8,128)(2,1)} %get-tuple-element.89), channel_id=1, source_target_pairs={{0,1},{1,0},{2,3},{3,2},{4,5},{5,4},{6,7},{7,6},{8,9},{9,8},{10,11... | collective-permute-start | bytes 3932168 | tf_op jit(solution)/shard_map/ppermute | solution.py:570
  668.1 95.3 %collective-permute-start.14 = (bf16[4,640,256]{2,1,0:T(8,128)(2,1)}, bf16[4,640,256]{2,1,0:T(8,128)(2,1)S(1)}, u32[]{:S(2)}, u32[]{:S(2)}) collective-permute-start(bf16[4,640,256]{2,1,0:T(8,128)(2,1)} %get-tuple-element.90), channel_id=1, source_target_pairs={{0,1},{1,0},{2,3},{3,2},{4,5},{5,4},{6,7},{7,6},{8,9},{9,8},{10,11... | collective-permute-start | bytes 3932168 | tf_op jit(solution)/shard_map/ppermute | solution.py:570
  (20 other events, 63.2 us)
Sparse Core Ops, SparseCore 0:
  78.0 53.4 all-gather.4
  393.6 46.0 reduce-scatter.2
  442.1 97.1 reduce-scatter.4
  542.9 142.3 all-reduce.3

commit v2 on v1

--- a/solution.py
+++ b/solution.py
@@ -100,7 +100,59 @@
     return jax.ShapeDtypeStruct(shape, dtype)
 
 
-def first_kernel(pre, x_ref, p_ref, first_ref, stat_ref):
+def weight_copies(own_refs, full_refs, sems):
+    seq, ch = lax.axis_index("seq"), lax.axis_index("ch")
+    core, row = seq % 2, (seq // 2) % 2
+    send_sem, recv_sem = sems
+    across, along, beside = {"ch": 1 - ch}, {"seq": seq + 2 - 4 * row}, {"seq": seq + 1 - 2 * core}
+
+    def part(ref, at, size):
+        at = pl.multiple_of(at, 16)
+        return ref.at[:, pl.ds(at, size), :] if len(ref.shape) == 3 else ref.at[pl.ds(at, size), :]
+
+    (w_in, conv, w_out), (w_in_full, conv_full, w_out_full) = own_refs, full_refs
+    items = [
+        (w_in, w_in_full),
+        (conv.at[pl.ds(0, 2)], conv_full.at[pl.ds(0, 2)]),
+        (conv.at[pl.ds(2, 3)], conv_full.at[pl.ds(2, 3)]),
+        (w_out, w_out_full),
+    ]
+    local, first_hop, second_hop, third_hop = [], [], [], []
+    for k, (own, full) in enumerate(items):
+        half = own.shape[-2]
+        size = half // 4
+
+        def remote(src, dst, slot, device):
+            return pltpu.make_async_remote_copy(
+                src_ref=src,
+                dst_ref=dst,
+                send_sem=send_sem.at[k, slot],
+                recv_sem=recv_sem.at[k, slot],
+                device_id=device,
+                device_id_type=pl.DeviceIdType.MESH,
+            )
+
+        quarter = (row * 2 + core) * size
+        local.append(remote(own, part(full, ch * half, half), 4, beside))
+        first_hop.append(remote(part(own, quarter, size), part(full, ch * half + quarter, size), 0, across))
+        landed = (1 - ch) * half
+        mine = part(full, landed + quarter, size)
+        second_hop.append(remote(mine, mine, 1, along))
+        both = []
+        for j, r in enumerate((row, 1 - row)):
+            piece = part(full, landed + (r * 2 + core) * size, size)
+            both.append(remote(piece, piece, 2 + j, beside))
+        third_hop.append(both)
+    return local, first_hop, second_hop, third_hop
+
+
+def first_kernel(comm, pre, x_ref, p_ref, *rest):
+    if comm:
+        own_refs, own_vec, first_ref, stat_ref = rest[:3], rest[3], rest[4], rest[5]
+        full_refs, full_vec = rest[6:9], rest[9]
+        exchange(own_refs, own_vec, full_refs, full_vec, rest[10:12], rest[12:])
+    else:
+        first_ref, stat_ref = rest
     length = x_ref.shape[2]
     mean, scale = norm_stats(lambda sl: x_ref[0, sl, :].astype(F32), D, length)
     stat_ref[0, 0:1, :] = mean
@@ -115,22 +167,110 @@
     loop(D, body, 0)
 
 
-def first_call(pre, tokens, p1, count, offset):
+def exchange(own_refs, own_vec, full_refs, full_vec, sems, vec_sems):
+    step, steps = pl.program_id(0), pl.num_programs(0)
+    seq, ch = lax.axis_index("seq"), lax.axis_index("ch")
+    core, row = seq % 2, (seq // 2) % 2
+    local, first_hop, second_hop, third_hop = weight_copies(own_refs, full_refs, sems)
+    vec_local = pltpu.make_async_copy(own_vec, full_vec.at[ch], vec_sems[0])
+    vec_remote = pltpu.make_async_remote_copy(
+        src_ref=own_vec,
+        dst_ref=full_vec.at[ch],
+        send_sem=vec_sems[1],
+        recv_sem=vec_sems[2],
+        device_id={"ch": 1 - ch},
+        device_id_type=pl.DeviceIdType.MESH,
+    )
+
+    @pl.when(step == 0)
+    def _():
+        barrier = pltpu.get_barrier_semaphore()
+        for device in ({"ch": 1 - ch}, {"seq": seq + 2 - 4 * row}, {"seq": seq + 1 - 2 * core}):
+            pl.semaphore_signal(barrier, inc=1, device_id=device, device_id_type=pl.DeviceIdType.MESH)
+        pl.semaphore_wait(barrier, 3)
+        vec_remote.start()
+        first_hop[0].start()
+        vec_local.start()
+        for copy in local:
+            copy.start()
+
+    for k in range(4):
+
+        if k > 0:
+
+            @pl.when(step == (0, 1, 4, 7)[k])
+            def _():
+                first_hop[k].start()
+
+        @pl.when(step == (4, 7, 10, 12)[k])
+        def _():
+            first_hop[k].wait()
+            second_hop[k].start()
+            third_hop[k][0].start()
+
+        @pl.when(step == (7, 10, 14, 15)[k])
+        def _():
+            second_hop[k].wait()
+            third_hop[k][1].start()
+
+    @pl.when(step == steps - 1)
+    def _():
+        vec_remote.wait()
+        vec_local.wait()
+        for k in range(4):
+            local[k].wait()
+            third_hop[k][0].wait()
+            third_hop[k][1].wait()
+
+
+def first_call(pre, tokens, p1, weights, vec):
     seqs, _, length = tokens.shape
-    return call(
-        first_kernel,
-        (count,),
-        [
-            pl.BlockSpec((1, D, length), lambda i, pre: ((pre[0] + offset + i) % seqs, 0, 0)),
-            whole((2, D, LANES)),
-        ],
-        (
-            pl.BlockSpec((1, D, length), lambda i, pre: (i, 0, 0)),
-            pl.BlockSpec((1, 2, length), lambda i, pre: (i, 0, 0)),
-        ),
-        (sds((count, D, length), BF16), sds((count, 2, length), F32)),
-        cost=cost_of(count * D * length * 40, count * D * length * 4),
-    )(pre, tokens, p1)
+    comm = weights is not None
+    any_spec = pl.BlockSpec(memory_space=pl.ANY)
+    in_specs = [pl.BlockSpec((1, D, length), lambda i, pre: ((pre[0] + i) % seqs, 0, 0)), whole((2, D, LANES))]
+    out_specs = [
+        pl.BlockSpec((1, D, length), lambda i, pre: (i, 0, 0)),
+        pl.BlockSpec((1, 2, length), lambda i, pre: (i, 0, 0)),
+    ]
+    shapes = [sds((seqs, D, length), BF16), sds((seqs, 2, length), F32)]
+    args, scratch = [pre, tokens, p1], []
+    if comm:
+        in_specs += [any_spec] * 4
+        out_specs += [any_spec] * 4
+        shapes += [sds(w.shape[:-2] + (2 * w.shape[-2], w.shape[-1]), BF16) for w in weights]
+        shapes.append(sds((2,) + vec.shape, F32))
+        args += list(weights) + [vec]
+        dma = pltpu.SemaphoreType.DMA
+        scratch = [dma((4, 5)), dma((4, 5)), dma, dma, dma]
+
+    def kernel(*refs):
+        first_kernel(comm, *refs)
+
+    if comm:
+
+        def at(i):
+            return ((lax.axis_index("ch") * (seqs // 2) + i) % seqs, 0, 0)
+
+        return pl.pallas_call(
+            lambda *refs: first_kernel(True, None, *refs),
+            grid=(seqs,),
+            in_specs=[
+                pl.BlockSpec((1, D, length), at),
+                pl.BlockSpec((2, D, LANES), lambda i: (0, 0, 0), pipeline_mode=pl.Buffered(1)),
+            ]
+            + [any_spec] * 4,
+            out_specs=tuple(
+                [pl.BlockSpec((1, D, length), lambda i: (i, 0, 0)), pl.BlockSpec((1, 2, length), lambda i: (i, 0, 0))]
+                + [any_spec] * 4
+            ),
+            out_shape=tuple(shapes),
+            scratch_shapes=scratch,
+            cost_estimate=cost_of(seqs * D * length * 40, seqs * D * length * 4),
+            compiler_params=pltpu.CompilerParams(
+                vmem_limit_bytes=VMEM_BYTES, collective_id=1, has_side_effects=True
+            ),
+        )(*args[1:])
+    return call(kernel, (seqs,), in_specs, tuple(out_specs), tuple(shapes))(*args)
 
 
 def middle_kernel(group, keep, pre, first_ref, mask_ref, w_ref, p_ref, mid_ref, lead_ref, trail_ref, *rest):
@@ -177,7 +317,7 @@
         functools.partial(middle_kernel, group, keep),
         (count,),
         [
-            pl.BlockSpec((1, D, length), lambda i, pre: (i, 0, 0)),
+            pl.BlockSpec((1, D, length), lambda i, pre: (offset + i, 0, 0)),
             pl.BlockSpec((1, 1, length), lambda i, pre: ((pre[0] + offset + i) % seqs, 0, 0)),
             whole((INNER, D)),
             whole((3, INNER, LANES)),
@@ -205,13 +345,15 @@
 
 
 def last_kernel(
-    group, keep, pre, mid_ref, before_ref, after_ref, x_ref, dy_ref, wc_ref, wo_ref, p_ref, b_ref, *rest
+    group, keep, pre, mid_ref, before_ref, after_ref, x_ref, wc_ref, wo_ref, p_ref, b_ref, *rest
 ):
     if keep:
-        mixed_ref, gw_ref, gb_ref, hat_ref, gp_ref, scale_ref = rest[:6]
+        mixed_ref, hat_ref, gp_ref, scale_ref, last_ref = rest[:5]
+        last_ref = last_ref.at[0]
+        pad_ref, cat_ref, conv_ref = rest[-3:]
     else:
-        mixed_ref, gw_ref, gb_ref = rest[1:4]
-    pad_ref, cat_ref, conv_ref, last_ref = rest[-4:]
+        mixed_ref = rest[1]
+        pad_ref, cat_ref, conv_ref, last_ref = rest[-4:]
     length = mid_ref.shape[2]
     step = pl.program_id(0)
     gather_windows(group, step % group, mid_ref, before_ref, after_ref, pad_ref, cat_ref, 1)
@@ -234,49 +376,41 @@
     branch = jnp.dot(wo_ref[...], last_ref[...], preferred_element_type=F32)
     mixed_ref[0] = (x_ref[0].astype(F32) + branch + spread(b_ref[...], length)).astype(BF16)
 
-    @pl.when(step == 0)
-    def _():
-        gw_ref[...] = jnp.zeros_like(gw_ref)
-        gb_ref[...] = jnp.zeros_like(gb_ref)
-
-    gw_ref[...] += lax.dot_general(
-        last_ref[...], dy_ref[0], (((1,), (1,)), ((), ())), preferred_element_type=F32
-    )
-    gb_ref[...] += fold_lanes(dy_ref[0].astype(F32))
-
-
-def last_call(pre, mid, before, after, tokens, cot, wc, wo_t, p2, b_out, count, offset, group, keep, mixed):
+
+def last_call(pre, mid, before, after, tokens, wc, wo_t, p2, b_out, count, offset, group, keep, mixed):
     _, _, length = mid.shape
-    seqs, share, _ = cot.shape
+    seqs, share = tokens.shape[0], wo_t.shape[0]
     edge = pl.BlockSpec((1, INNER, group * REACH), lambda i, pre: (i // group, 0, 0))
     own = pl.BlockSpec((1, INNER, length), lambda i, pre: (i, 0, 0))
 
     def seq_at(i, pre):
         return (pre[0] + offset + i) % seqs
 
-    outs = [
-        pl.BlockSpec((1, share, length), lambda i, pre: (seq_at(i, pre), 0, 0)),
-        pl.BlockSpec((INNER, share), lambda i, pre: (0, 0)),
-        pl.BlockSpec((share, LANES), lambda i, pre: (0, 0)),
-    ]
-    shapes = [sds((seqs, share, length), BF16), sds((INNER, share), F32), sds((share, LANES), F32)]
+    outs = [pl.BlockSpec((1, share, length), lambda i, pre: (seq_at(i, pre), 0, 0))]
+    shapes = [sds((seqs, share, length), BF16)]
     in_specs = [
         own,
         edge,
         edge,
         pl.BlockSpec((1, share, length), lambda i, pre: (seq_at(i, pre), pre[1], 0)),
-        pl.BlockSpec((1, share, length), lambda i, pre: (seq_at(i, pre), 0, 0)),
         whole((INNER, KERNEL * INNER)),
         whole((share, INNER)),
         whole((3, INNER, LANES)),
         whole((share, LANES)),
     ]
-    args = [pre, mid, before, after, tokens, cot, wc, wo_t, p2, b_out]
+    args = [pre, mid, before, after, tokens, wc, wo_t, p2, b_out]
     aliases = None
+    scratch = [
+        pltpu.VMEM((INNER, length + 2 * LANES), BF16),
+        pltpu.VMEM((KERNEL * INNER, length), BF16),
+        pltpu.VMEM((INNER, length), F32),
+    ]
     if keep:
-        outs += [own, own, pl.BlockSpec((1, 1, length), lambda i, pre: (i, 0, 0))]
-        shapes += [sds((count, INNER, length), BF16)] * 2 + [sds((count, 1, length), F32)]
+        outs += [own, own, pl.BlockSpec((1, 1, length), lambda i, pre: (i, 0, 0)), own]
+        saved = sds((count, INNER, length), BF16)
+        shapes += [saved, saved, sds((count, 1, length), F32), saved]
     else:
+        scratch.append(pltpu.VMEM((INNER, length), BF16))
         in_specs.append(pl.BlockSpec(memory_space=pl.ANY))
         args.append(mixed)
         aliases = {len(args) - 1: 0}
@@ -286,22 +420,17 @@
         in_specs,
         tuple(outs),
         tuple(shapes),
-        scratch=[
-            pltpu.VMEM((INNER, length + 2 * LANES), BF16),
-            pltpu.VMEM((KERNEL * INNER, length), BF16),
-            pltpu.VMEM((INNER, length), F32),
-            pltpu.VMEM((INNER, length), BF16),
-        ],
+        scratch=scratch,
         aliases=aliases,
-        cost=cost_of(count * INNER * (KERNEL * INNER + 2 * share) * length * 1.3, count * share * 6 * length * 2),
+        cost=cost_of(count * INNER * (KERNEL * INNER + share) * length * 1.3, count * share * 6 * length * 2),
     )(*args)
 
 
 def rear_kernel(group, chs, pre, *refs):
     dy_refs = refs[:chs]
-    w_ref, hat_ref, gp_ref, scale_ref, p_ref = refs[chs : chs + 5]
-    dconv_ref, lead_ref, trail_ref, gg_ref, gb_ref, gc_ref = refs[chs + 5 : chs + 11]
-    dy_ref, d_ref = refs[chs + 11 :]
+    w_ref, hat_ref, gp_ref, last_ref, scale_ref, p_ref = refs[chs : chs + 6]
+    dconv_ref, lead_ref, trail_ref, gg_ref, gb_ref, gc_ref, gw_ref, go_ref = refs[chs + 6 : chs + 14]
+    dy_ref, d_ref = refs[chs + 14 :]
     share, length = dy_refs[0].shape[1], dy_refs[0].shape[2]
     step = pl.program_id(0)
 
@@ -310,11 +439,17 @@
         gg_ref[...] = jnp.zeros_like(gg_ref)
         gb_ref[...] = jnp.zeros_like(gb_ref)
         gc_ref[...] = jnp.zeros_like(gc_ref)
+        gw_ref[...] = jnp.zeros_like(gw_ref)
+        go_ref[...] = jnp.zeros_like(go_ref)
 
     for r in range(chs):
         at = pl.multiple_of(((pre[1] + chs - r) % chs) * share, share)
         dy_ref[pl.ds(at, share), :] = dy_refs[r][0]
     d_ref[...] = jnp.dot(w_ref[...], dy_ref[...], preferred_element_type=F32)
+    gw_ref[...] += lax.dot_general(
+        last_ref[0], dy_ref[...], (((1,), (1,)), ((), ())), preferred_element_type=F32
+    )
+    go_ref[...] += fold_lanes(dy_ref[...].astype(F32))
     scale = scale_ref[0]
     zero = jnp.zeros((8, length), F32)
 
@@ -347,7 +482,7 @@
             trail_ref[0, :, k * REACH : (k + 1) * REACH] = dconv_ref[0, :, length - REACH :]
 
 
-def rear_call(pre, cot, others, w_out, hat, gp, scale, p2, begin, count, group):
+def rear_call(pre, cot, others, w_out, hat, gp, last, scale, p2, begin, count, group):
     seqs, share, length = cot.shape
     chs = 1 + len(others)
     edge = pl.BlockSpec((1, INNER, group * REACH), lambda i, pre: (i // group, 0, 0))
@@ -365,14 +500,33 @@
             whole((INNER, D)),
             kept,
             kept,
+            kept,
             pl.BlockSpec((1, 1, length), lambda i, pre: (begin + i, 0, 0)),
             whole((1, INNER, LANES)),
         ],
-        (own, edge, edge, part, part, part),
-        (sds((count, INNER, length), BF16), edge_shape, edge_shape, part_shape, part_shape, part_shape),
+        (
+            own,
+            edge,
+            edge,
+            part,
+            part,
+            part,
+            pl.BlockSpec((INNER, D), lambda i, pre: (0, 0)),
+            pl.BlockSpec((D, LANES), lambda i, pre: (0, 0)),
+        ),
+        (
+            sds((count, INNER, length), BF16),
+            edge_shape,
+            edge_shape,
+            part_shape,
+            part_shape,
+            part_shape,
+            sds((INNER, D), F32),
+            sds((D, LANES), F32),
+        ),
         scratch=[pltpu.VMEM((D, length), BF16), pltpu.VMEM((INNER, length), F32)],
         cost=cost_of(count * INNER * D * length * 1.5, count * INNER * 5 * length * 2),
-    )(pre, cot, *others, w_out, hat, gp, scale, p2)
+    )(pre, cot, *others, w_out, hat, gp, last, scale, p2)
 
 
 def front_kernel(group, chs, pre, *refs):
@@ -566,6 +720,188 @@
     )(pre, part, cot, gt)
 
 
+def turn_kernel(pre, w_ref, flat_ref, turned_ref):
+    unit = (
+        lax.broadcasted_iota(jnp.int32, (INNER, INNER), 0) == lax.broadcasted_iota(jnp.int32, (INNER, INNER), 1)
+    ).astype(F32).astype(BF16)
+    flat_ref[...] = w_ref[0]
+    turned_ref[...] = lax.dot_general(
+        unit, w_ref[0], (((1,), (1,)), ((), ())), preferred_element_type=F32
+    ).astype(BF16)
+
+
+def turn_call(pre, conv):
+    block = pl.BlockSpec((INNER, INNER), lambda k, pre: (0, k))
+    shape = sds((INNER, KERNEL * INNER), BF16)
+    return call(
+        turn_kernel,
+        (KERNEL,),
+        [pl.BlockSpec((1, INNER, INNER), lambda k, pre: (k, 0, 0))],
+        (block, block),
+        (shape, shape),
+        cost=cost_of(KERNEL * INNER**3, KERNEL * INNER * INNER * 6),
+    )(pre, conv)
+
+
+def reduce_kernel(stages, half_rows, *refs):
+    gcw_ref, gwi_ref, gwo_ref, small_ref, out_ref = refs[:5]
+    acc, send, recv, swap, res, load_sem, send_sem, recv_sem = refs[5:]
+    seq, ch = lax.axis_index("seq"), lax.axis_index("ch")
+    streams = len(stages)
+    rows = acc.shape[1] // streams
+    bits = sorted(stages[0])
+
+    def partner(b):
+        return {"seq": seq + (1 - 2 * ((seq // (1 << b)) % 2)) * (1 << b)}
+
+    loads = []
+    for h in range(2):
+        mine = pl.ds(h * half_rows, half_rows)
+        pieces = [gcw_ref.at[k, mine, :] for k in range(KERNEL)]
+        for ref in (gwi_ref, gwo_ref):
+            pieces += [ref.at[mine, pl.ds(j * INNER, INNER)] for j in range(D // INNER)]
+        for j, piece in enumerate(pieces):
+            loads.append((piece, acc.at[h, pl.ds(j * half_rows, half_rows), :]))
+        used = len(pieces) * half_rows
+        loads.append((small_ref.at[h], acc.at[h, pl.ds(used, small_ref.shape[1]), :]))
+        used += small_ref.shape[1]
+        acc[h, used:, :] = jnp.zeros((acc.shape[1] - used, INNER), F32)
+    loads = [pltpu.make_async_copy(a, b, load_sem.at[j]) for j, (a, b) in enumerate(loads)]
+    for copy in loads:
+        copy.start()
+
+    barrier = pltpu.get_barrier_semaphore()
+    for device in [partner(b) for b in bits] + [{"ch": 1 - ch}]:
+        pl.semaphore_signal(barrier, inc=1, device_id=device, device_id_type=pl.DeviceIdType.MESH)
+    pl.semaphore_wait(barrier, len(bits) + 1)
+    for copy in loads:
+        copy.wait()
+
+    def remote(src, dst, slot, device):
+        return pltpu.make_async_remote_copy(
+            src_ref=src,
+            dst_ref=dst,
+            send_sem=send_sem.at[slot],
+            recv_sem=recv_sem.at[slot],
+            device_id=device,
+            device_id_type=pl.DeviceIdType.MESH,
+        )
+
+    def sliced(count, body):
+        step = next(r for r in (96, 48, 32, 16) if count % r == 0)
+
+        def one(i, carry):
+            body(pl.multiple_of(i * step, 16), step)
+            return carry
+
+        lax.fori_loop(0, count // step, one, 0)
+
+    low = [jnp.int32(q * rows) for q in range(streams)]
+    size = rows
+    at = 0
+    pending = [None] * streams
+    slot = 0
+    for t in range(len(bits)):
+        size //= 2
+        for q in range(streams):
+            if pending[q] is not None:
+                pending[q]()
+            b = stages[q][t]
+            bit = (seq // (1 << b)) % 2
+            away = low[q] + (1 - bit) * size
+            low[q] = low[q] + bit * size
+            keep = low[q]
+            for h in range(2):
+
+                def pack(i, step, h=h):
+                    send[q, h, pl.ds(at + i, step), :] = acc[
+                        h, pl.ds(pl.multiple_of(away + i, 16), step), :
+                    ].astype(BF16)
+
+                sliced(size, pack)
+            window = pl.ds(at, size)
+            copy = remote(send.at[q, :, window, :], recv.at[q, :, window, :], slot, partner(b))
+            copy.start()
+
+            def finish(q=q, at=at, size=size, keep=keep, copy=copy):
+                copy.wait()
+                for h in range(2):
+
+                    def add(i, step, h=h):
+                        place = pl.ds(pl.multiple_of(keep + i, 16), step)
+                        acc[h, place, :] += recv[q, h, pl.ds(at + i, step), :].astype(F32)
+
+                    sliced(size, add)
+
+            pending[q] = finish
+            slot += 1
+        at += size
+
+    swaps = []
+    for q in range(streams):
+        pending[q]()
+        swap[0, q] = acc[1 - ch, pl.ds(pl.multiple_of(low[q], 16), size), :].astype(BF16)
+        copy = remote(swap.at[0, q], swap.at[1, q], slot, {"ch": 1 - ch})
+        copy.start()
+        swaps.append(copy)
+        slot += 1
+    waiting = [None] * streams
+    for q in range(streams):
+        swaps[q].wait()
+        place = pl.ds(pl.multiple_of(low[q], 16), size)
+        res[place, :] = (acc[ch, place, :] + swap[1, q].astype(F32)).astype(BF16)
+    for t in reversed(range(len(bits))):
+        for q in range(streams):
+            if waiting[q] is not None:
+                waiting[q].wait()
+            b = stages[q][t]
+            place = pl.ds(pl.multiple_of(low[q], 16), size)
+            copy = remote(res.at[place, :], res.at[place, :], slot, partner(b))
+            copy.start()
+            waiting[q] = copy
+            low[q] = low[q] - ((seq // (1 << b)) % 2) * size
+            slot += 1
+        size *= 2
+    for q in range(streams):
+        waiting[q].wait()
+    done = pltpu.make_async_copy(res, out_ref, load_sem.at[0])
+    done.start()
+    done.wait()
+
+
+def reduce_call(gcw, gwi, gwo, small, seq_count):
+    half_rows = INNER // 2
+    levels = seq_count.bit_length() - 1
+    used = half_rows * (KERNEL + 2 * D // INNER) + small.shape[1]
+    unit = 2 * seq_count * 16
+    rows = -(-used // unit) * unit
+    order = list(range(levels))
+    stages = (tuple(order), tuple(order[:1] + order[2:] + order[1:2]))
+    streams = len(stages)
+    moved = rows // streams - rows // streams // seq_count
+    last = rows // streams // seq_count
+    slots = streams * (2 * levels + 1)
+    any_spec = pl.BlockSpec(memory_space=pl.ANY)
+    return pl.pallas_call(
+        functools.partial(reduce_kernel, stages, half_rows),
+        in_specs=[any_spec] * 4,
+        out_specs=any_spec,
+        out_shape=sds((rows, INNER), BF16),
+        scratch_shapes=[
+            pltpu.VMEM((2, rows, INNER), F32),
+            pltpu.VMEM((streams, 2, moved, INNER), BF16),
+            pltpu.VMEM((streams, 2, moved, INNER), BF16),
+            pltpu.VMEM((2, streams, last, INNER), BF16),
+            pltpu.VMEM((rows, INNER), BF16),
+            pltpu.SemaphoreType.DMA((2 * (KERNEL + 2 * D // INNER + 1),)),
+            pltpu.SemaphoreType.DMA((slots,)),
+            pltpu.SemaphoreType.DMA((slots,)),
+        ],
+        cost_estimate=cost_of(0, rows * INNER * 12),
+        compiler_params=pltpu.CompilerParams(vmem_limit_bytes=VMEM_BYTES, collective_id=2, has_side_effects=True),
+    )(gcw, gwi, gwo, small)
+
+
 def rotate(value, axis, count, by):
     return lax.ppermute(value, axis, [(i, (i + by) % count) for i in range(count)])
 
@@ -580,18 +916,8 @@
     return shift(trail, 1), shift(lead, -1)
 
 
-def full_weight(own, axis, ch, chs):
-    seq = lax.axis_size("seq")
-    rows = own.shape[axis]
-    if rows % (seq * 4) == 0 and chs == 2:
-        piece_rows = rows // seq
-        piece = lax.dynamic_slice_in_dim(own, lax.axis_index("seq") * piece_rows, piece_rows, axis)
-        piece = rotate(piece, "ch", 2, 1)
-        other = lax.all_gather(piece, "seq", axis=axis, tiled=True)
-        first = jnp.where(ch == 0, own, other)
-        second = jnp.where(ch == 0, other, own)
-        return jnp.concatenate([first, second], axis=axis)
-    return lax.all_gather(own, "ch", axis=axis, tiled=True)
+def own_slice(value, width, dim):
+    return lax.dynamic_slice_in_dim(value, lax.axis_index("ch") * width, width, dim)
 
 
 def lane_copies(vectors):
@@ -621,88 +947,91 @@
     share = b_out.shape[0]
     part = b_in.shape[0]
     n = seqs // chs
-    group = min(4, n // 2)
-    pieces = 2
-    size = n // pieces
+    group = min(4, n)
     starts = [((ch + chs - r) % chs) * n for r in range(1, chs)]
-    pre = jnp.stack(
-        [ch * n, ch] + [s + q * size for s in starts for q in range(pieces)]
-    ).astype(jnp.int32)
+    pre = jnp.stack([ch * n, ch] + starts).astype(jnp.int32)
+    pair = chs == 2
+
+    p1 = lane_copies(jnp.stack([ln1_gain, first_norm_bias]))
+    bo = lane_copies(b_out)
+    vec = jnp.stack([b_in, ln2_gain, ln2_bias, conv_b, ln3_gain, ln3_bias, b_in, b_in])
+    if pair:
+        first, stat, w_in_full, conv_full, w_out_full, vec_full = first_call(
+            pre, tokens, p1, (w_in, conv_w, w_out), vec
+        )
+        inner = vec_full.transpose(1, 0, 2).reshape(8, INNER)[:6]
+    else:
+        first, stat = first_call(pre, tokens, p1, None, None)
+        w_in_full = lax.all_gather(w_in, "ch", axis=0, tiled=True)
+        conv_full = lax.all_gather(conv_w, "ch", axis=1, tiled=True)
+        w_out_full = lax.all_gather(w_out, "ch", axis=0, tiled=True)
+        inner = lax.all_gather(vec, "ch", axis=1, tiled=True)[:6]
 
     others = []
-    for q in range(pieces):
-        got = []
-        for r in range(1, chs):
-            to = (ch + r) % chs
-            block = lax.dynamic_slice_in_dim(cotangent, to * n + q * size, size, 0)
-            got.append(rotate(block, "ch", chs, r))
-        others.append(got)
-
-    inner = jnp.stack([b_in, ln2_gain, ln2_bias, conv_b, ln3_gain, ln3_bias])
-    inner = lax.all_gather(inner, "ch", axis=1, tiled=True)
-    p1 = lane_copies(jnp.stack([ln1_gain, first_norm_bias]))
+    for r in range(1, chs):
+        block = lax.dynamic_slice_in_dim(cotangent, ((ch + r) % chs) * n, n, 0)
+        block, _ = lax.optimization_barrier((block, stat))
+        others.append(rotate(block, "ch", chs, r))
     p2 = lane_copies(inner)
-    bo = lane_copies(b_out)
-    w_in_full = full_weight(w_in, 0, ch, chs)
-    conv_full = full_weight(conv_w, 1, ch, chs)
-    w_out_full = full_weight(w_out, 0, ch, chs)
-    wc = conv_full.transpose(1, 0, 2).reshape(INNER, KERNEL * INNER)
-    wc_t = conv_full.transpose(2, 0, 1).reshape(INNER, KERNEL * INNER)
+    wc, wc_t = turn_call(pre, conv_full)
     wi_t = w_in_full.T
     wo_t = lax.dynamic_slice_in_dim(w_out_full, ch * share, share, 1).T
 
-    first_own, stat_own = first_call(pre, tokens, p1, n, 0)
-    first_oth, _ = first_call(pre, tokens, p1, seqs - n, n)
     mid_own, lead, trail, hat_mid, gp_mid, scale_mid = middle_call(
-        pre, first_own, pad_mask, w_in_full, p2[0:3], n, 0, group, True
+        pre, first, pad_mask, w_in_full, p2[0:3], n, 0, group, True
     )
     before, after = rims(lead, trail)
-    mid_oth, lead, trail = middle_call(pre, first_oth, pad_mask, w_in_full, p2[0:3], seqs - n, n, group, False)
+    mid_oth, lead, trail = middle_call(pre, first, pad_mask, w_in_full, p2[0:3], seqs - n, n, group, False)
     before_oth, after_oth = rims(lead, trail)
-    mixed, gwo_own, gbo_own, hat_out, gp_out, scale_out = last_call(
-        pre, mid_own, before, after, tokens, cotangent, wc, wo_t, p2[3:6], bo, n, 0, group, True, None
-    )
-    rear = []
-    for q in range(pieces):
-        dconv, lead, trail, *sums = rear_call(
-            pre, cotangent, others[q], w_out_full, hat_out, gp_out, scale_out, p2[4:5], q * size, size, group
+    mixed, hat_out, gp_out, scale_out, last_own = last_call(
+        pre, mid_own, before, after, tokens, wc, wo_t, p2[3:6], bo, n, 0, group, True, None
+    )
+    dconv, lead, trail, gg3, gb3, gcb, gwo, gbo = rear_call(
+        pre, cotangent, others, w_out_full, hat_out, gp_out, last_own, scale_out, p2[4:5], 0, n, group
+    )
+    lead, trail = rims(lead, trail)
+    gt, *rest = front_call(
+        pre, dconv, lead, trail, mid_own, hat_mid, gp_mid, scale_mid, tokens, stat, cotangent,
+        wc_t, wi_t, p2[1:2], p1, chs, 0, n, group, None,
+    )
+    sends = [rotate(v, "ch", chs, r + 1) for r, v in enumerate(rest[: chs - 1])]
+    gcw, gwi, gg2, gb2, gbi, gg1, gb1 = rest[chs - 1 :]
+    mixed, = last_call(
+        pre, mid_oth, before_oth, after_oth, tokens, wc, wo_t, p2[3:6], bo, seqs - n, n, group, False, mixed
+    )
+    gcw = gcw.reshape(KERNEL, INNER, INNER)
+    inner_sums = jnp.stack([v.sum(1) for v in (gbi, gg2, gb2, gcb, gg3, gb3)])
+    outer_sums = jnp.stack([v.sum(1) for v in (gg1, gb1, gbo)])
+
+    if pair:
+        small = jnp.concatenate(
+            [
+                inner_sums.reshape(6, 2, part).transpose(1, 0, 2).reshape(2, 3, INNER),
+                outer_sums.reshape(3, 2, share).transpose(1, 0, 2),
+                jnp.zeros((2, 10, INNER), F32),
+            ],
+            axis=1,
         )
-        rear.append((dconv, rims(lead, trail), sums))
-    gt = None
-    back = []
-    sends = []
-    for q in range(pieces):
-        dconv, (lead, trail), _ = rear[q]
-        gt, *rest = front_call(
-            pre, dconv, lead, trail, mid_own, hat_mid, gp_mid, scale_mid, tokens, stat_own, cotangent,
-            wc_t, wi_t, p2[1:2], p1, chs, q * size, size, group, gt,
-        )
-        sends.append([rotate(v, "ch", chs, r + 1) for r, v in enumerate(rest[: chs - 1])])
-        back.append(rest[chs - 1 :])
-    mixed, gwo_oth, gbo_oth = last_call(
-        pre, mid_oth, before_oth, after_oth, tokens, cotangent, wc, wo_t, p2[3:6], bo, seqs - n, n, group, False, mixed
-    )
-    for q in range(pieces):
-        for r in range(chs - 1):
-            gt = add_call(pre, sends[q][r], cotangent, gt, 2 + r * pieces + q)
-
-    gcw, gwi, gg2, gb2, gbi, gg1, gb1 = (sum(v[1:], v[0]) for v in zip(*back))
-    gg3, gb3, gcb = (sum(v[1:], v[0]) for v in zip(*(r[2] for r in rear)))
-    gwo = gwo_own + gwo_oth
-    gbo = gbo_own + gbo_oth
-
-    gwo_sum = lax.psum(gwo, "seq")
-    gwo_all = lax.all_to_all(gwo_sum.astype(BF16), "ch", 0, 1, tiled=True).astype(F32)
-    gcw = lax.psum_scatter(gcw.reshape(KERNEL, INNER, INNER), "ch", scatter_dimension=1, tiled=True)
-    gcw = lax.psum(gcw, "seq")
-    gwi = lax.psum_scatter(gwi, "ch", scatter_dimension=0, tiled=True)
-    gwi = lax.psum(gwi, "seq")
-    small = jnp.stack([v.sum(1) for v in (gbi, gg2, gb2, gcb, gg3, gb3)]).reshape(-1)
-    outer = jnp.stack([gg1.sum(1), gb1.sum(1)]).reshape(-1)
-    bo_slot = lax.dynamic_update_slice(jnp.zeros((D,), F32), gbo.sum(1), (ch * share,))
-    total = lax.psum(jnp.concatenate([small, outer, bo_slot]), ("seq", "ch"))
-    inner_sums = lax.dynamic_slice_in_dim(total[: 6 * INNER].reshape(6, INNER), ch * part, part, 1)
-    outer_sums = lax.dynamic_slice_in_dim(total[6 * INNER :].reshape(3, D), ch * share, share, 1)
+        total = reduce_call(gcw, gwi, gwo, small, lax.axis_size("seq"))
+        gcw = total[: KERNEL * part].reshape(KERNEL, part, INNER).astype(F32)
+        base = KERNEL * part
+        wide = []
+        for k in range(2):
+            blocks = [total[base + (2 * k + j) * part : base + (2 * k + j + 1) * part] for j in range(2)]
+            wide.append(jnp.concatenate(blocks, axis=1).astype(F32))
+        gwi, gwo = wide
+        base += 4 * part
+        inner_sums = total[base : base + 3].reshape(6, part).astype(F32)
+        outer_sums = total[base + 3 : base + 6].astype(F32)
+    else:
+        gcw, gwi, gwo, inner_sums, outer_sums = lax.psum((gcw, gwi, gwo, inner_sums, outer_sums), ("seq", "ch"))
+        gcw = own_slice(gcw, part, 1)
+        gwi = own_slice(gwi, part, 0)
+        gwo = own_slice(gwo, part, 0)
+        inner_sums = own_slice(inner_sums, part, 1)
+        outer_sums = own_slice(outer_sums, share, 1)
+    for r in range(chs - 1):
+        gt = add_call(pre, sends[r], cotangent, gt, 2 + r)
     return (
         mixed,
         gt,
@@ -716,7 +1045,7 @@
         inner_sums[3],
         inner_sums[4],
         inner_sums[5],
-        gwo_all,
+        gwo,
         outer_sums[2],
     )
 

time: 797 us -> 411 us (0.52)
  blocking collectives: 272 us -> 0 us
  Pallas kernels: 250 us -> 353 us
  waiting for transfers between devices: 101 us -> 0.02 us
  local copies, waits for them, and re-layouts: 73.1 us -> 29.5 us
  other arithmetic: 44.1 us -> 10.1 us
  starting transfers between devices: 33.7 us -> 15.8 us
  between operations: 15 us -> 0.93 us
    psum x2 -> x0, blocking collectives: 167 us -> none  [the longest x1 87.3 us: body(): total = lax.psum(jnp.concatenate([small, outer, bo_slot]), ('seq', 'ch'))]
    pallas_call x2 -> x3, Pallas kernels: 26 us -> 160 us  [the longest x1 112 us: reduce_call(): pl.pallas_call(functools.partial(reduce_kernel, stages, half_rows), in_sp...]
    all_gather x3 -> x0, blocking collectives: 105 us -> none  [the longest x1 56.1 us: body(): inner = lax.all_gather(inner, 'ch', axis=1, tiled=True)]
    reduce_scatter x2 -> x0, waiting for transfers between devices: 101 us -> none  [the longest x1 99.6 us: body(): lax.psum_scatter(gcw.reshape(KERNEL, INNER, INNER), 'ch', scatter_dimensi...]
    unnamed x74 -> x30, local copies, waits for them, and re-layouts: 21.6 us -> 0.87 us
    pallas_call x2, Pallas kernels: 79 us -> 59.9 us  [last_call(): call(functools.partial(last_kernel, group, keep), (count,), in_specs, tup...]
    add x3 -> x0, other arithmetic: 15.8 us -> none  [the longest x2 14.2 us: body(): gcw, gwi, gg2, gb2, gbi, gg1, gb1 = (sum(v[1:], v[0]) for v in zip(*back))]
    reshape x4 -> x1, local copies, waits for them, and re-layouts: 13.7 us -> 0.08 us  [body(): inner_sums.reshape(6, 2, part).transpose(1, 0, 2).reshape(2, 3, INNER)]
  transfers between devices with their start and end apart: 20 -> 8, of which waited for: 2 -> 0; matrix products, arithmetic and copies ran while one was open for 13% -> 7% of each run, Pallas kernels for 26% -> 70%
where the time goes in v2:
time: 411 us; the launch traced here: 410 us
  Pallas kernels  353 us (86%)
  local copies, waits for them, and re-layouts  29.5 us (7%)
  starting transfers between devices  15.8 us (4%)
  other arithmetic  10.1 us (2%)
    pallas_call x1, Pallas kernels, reduce_call(): pl.pallas_call(functools.partial(reduce_kernel, stages, half_rows), in_sp...  112 us
    pallas_call x1, Pallas kernels, front_call(): call(kernel, (count,), in_specs, tuple([seq_block(share)] + [pl.BlockSpec...  71 us
    pallas_call x2, Pallas kernels, last_call(): call(functools.partial(last_kernel, group, keep), (count,), in_specs, tup...  59.9 us
    pallas_call x1, Pallas kernels, first_call(): pl.pallas_call(lambda *refs: first_kernel(True, None, *refs), grid=(seqs,...  38.8 us
    pallas_call x2, Pallas kernels, middle_call(): call(functools.partial(middle_kernel, group, keep), (count,), [pl.BlockSp...  33.5 us
    pallas_call x1, Pallas kernels, rear_call(): call(functools.partial(rear_kernel, group, chs), (count,), [pl.BlockSpec(...  21 us
    ppermute x6, starting transfers between devices, shift(): return lax.ppermute(value, 'seq', pairs)  13.6 us
    pallas_call x1, Pallas kernels, turn_call(): call(turn_kernel, (KERNEL,), [pl.BlockSpec((1, INNER, INNER), lambda k, p...  9.43 us
  transfers between devices with their start and end apart: 8, of which 0 were waited for; matrix products, arithmetic and copies ran while one was open for 7% of the time, Pallas kernels for 70%

profile of v2, /device:TPU:0, one launch (start us, length us, event | category | flops | bytes accessed | tf_op | source)
XLA Modules:
  0.0 409.7 jit_solution(19065433635134110)
XLA Ops:
  6.2 3.4 constant_dynamic-slice_fusion
  10.2 1.5 broadcast_in_dim.27.refs_1_.refs_13_
  11.7 38.8 %shard_map.254 = (bf16[16,1280,256]{2,1,0:T(8,128)(2,1)}, f32[16,2,256]{2,1,0:T(2,128)}, bf16[640,1280]{1,0:T(8,128)(2,1)}, bf16[5,640,640]{2,1,0:T(8,128)(2,1)}...) custom-call(bf16[16,1280,256]{2,1,0:T(8,128)(2,1)} %refs_7_.1, f32[2,1280,128]{2,1,0:T(8,128)} %broadcast_in_dim.27.refs_1_.refs_13_, ...), custom_call_target="tpu_custom_call" | custom-call | flops 419430400 | bytes 20971520 | tf_op jit(solution)/shard_map/pallas_call | solution.py:254
  53.3 1.3 broadcast_in_dim.28.p_ref
  54.6 17.7 %shard_map.257 = (bf16[8,640,256]{2,1,0:T(8,128)(2,1)}, bf16[2,640,128]{2,1,0:T(8,128)(2,1)}, bf16[2,640,128]{2,1,0:T(8,128)(2,1)}, bf16[8,640,256]{2,1,0:T(8,12...) custom-call(s32[3]{0:T(128)} %pad_add_fusion.pre, bf16[16,1280,256]{2,1,0:T(8,128)(2,1)} %get-tuple-element.54.first_ref, ...), custom_call_target="tpu_custom_call" | custom-call | flops 5033164800 | bytes 13107200 | tf_op jit(solution)/shard_map/pallas_call | solution.py:316
  72.3 2.7 collective-permute-start.2
  75.0 1.3 collective-permute-start.3
  77.3 1.3 copy.34
  78.6 1.0 dynamic-slice_bitcast_fusion.wo_ref
  79.6 9.4 %shard_map.256 = (bf16[640,3200]{1,0:T(8,128)(2,1)}, bf16[640,3200]{1,0:T(8,128)(2,1)}) custom-call(s32[3]{0:T(128)} %pad_add_fusion.pre, bf16[5,640,640]{2,1,0:T(8,128)(2,1)} %get-tuple-element.60.w_ref), custom_call_target="tpu_custom_call" | custom-call | flops 2621440000 | bytes 12288000 | tf_op jit(solution)/shard_map/pallas_call | solution.py:736
  89.9 1.3 broadcast_in_dim.29.p_ref
  91.2 30.5 %shard_map.258 = (bf16[16,640,256]{2,1,0:T(8,128)(2,1)}, bf16[8,640,256]{2,1,0:T(8,128)(2,1)}, bf16[8,640,256]{2,1,0:T(8,128)(2,1)}, f32[8,1,256]{2,1,0:T(1,128)}, bf16[8,640,256]{2,1,0:T(8,128)(2,1)}) custom-call(s32[3]{0:T(128)} %pad_add_fusion.pre, bf16[8,640,256]{2,1,0:T(8,128)(2,1)} %get-tuple-element.63.mid_ref.refs_3_, ...), custom_call_target="tpu_custom_call" | custom-call | flops 13086228480 | bytes 15728640 | tf_op jit(solution)/shard_map/pallas_call | solution.py:417
  121.8 0.9 broadcast_in_dim.31.refs_7_
  122.6 21.0 %shard_map.260 = (bf16[8,640,256]{2,1,0:T(8,128)(2,1)}, bf16[2,640,128]{2,1,0:T(8,128)(2,1)}, bf16[2,640,128]{2,1,0:T(8,128)(2,1)}, f32[640,128]{1,0:T(8,128)}, ...) custom-call(s32[3]{0:T(128)} %pad_add_fusion.pre, ...), custom_call_target="tpu_custom_call" | custom-call | flops 5033164800 | bytes 13107200 | tf_op jit(solution)/shard_map/pallas_call | solution.py:494
  143.6 3.1 collective-permute-start.5
  146.7 1.4 collective-permute-start.6
  148.1 15.8 %shard_map.255 = (bf16[8,640,256]{2,1,0:T(8,128)(2,1)}, bf16[2,640,128]{2,1,0:T(8,128)(2,1)}, bf16[2,640,128]{2,1,0:T(8,128)(2,1)}) custom-call(s32[3]{0:T(128)} %pad_add_fusion.pre, bf16[16,1280,256]{2,1,0:T(8,128)(2,1)} %get-tuple-element.54.first_ref, s32[16,1,256]{2,1,0:T(1,128)} %reshape.82.mask_ref, bf16[640,1280]{1,0:T(8,128)(2,1)} %get-tuple-element.55.w_ref, ...), custom_call_target="tpu_custom_call" | custom-call | flops 5033164800 | bytes 13107200 | tf_op jit(solution)/shard_map/pallas_call | solution.py:316
  163.9 3.6 collective-permute-start
  167.6 1.5 collective-permute-start.1
  169.1 2.2 copy.36
  171.4 0.9 broadcast_in_dim.32.refs_12_
  172.4 71.0 %shard_map.261 = (f32[16,640,256]{2,1,0:T(8,128)}, bf16[8,640,256]{2,1,0:T(8,128)(2,1)}, f32[3200,640]{1,0:T(8,128)}, f32[640,1280]{1,0:T(8,128)}, f32[640,128]{...) custom-call(s32[3]{0:T(128)} %pad_add_fusion.pre, ...), custom_call_target="tpu_custom_call" | custom-call | flops 30534533120 | bytes 41943040 | tf_op jit(solution)/shard_map/pallas_call | solution.py:673
  243.4 1.6 collective-permute-start.7
  245.8 29.4 %shard_map.259 = bf16[16,640,256]{2,1,0:T(8,128)(2,1)} custom-call(s32[3]{0:T(128)} %pad_add_fusion.pre, bf16[8,640,256]{2,1,0:T(8,128)(2,1)} %get-tuple-element.57.mid_ref, bf16[2,640,128]{2,1,0:T(8,128)(2,1)} %copy-done.11, bf16[2,640,128]{2,1,0:T(8,128)(2,1)} %copy-done.12, bf16[16,1280,256]{2,1,0:T(8,128)(2,1)} %refs_7_.1, ...), custom_call_target="tpu_custom_call", output_to_operand_aliasing={{}: (9, {})} | custom-call | flops 13086228480 | bytes 15728640 | tf_op jit(solution)/shard_map/pallas_call | solution.py:417
  276.2 1.1 reduce_sum.81
  277.5 1.1 reduce_sum.82
  280.3 111.8 %shard_map.263 = bf16[3072,640]{1,0:T(8,128)(2,1)} custom-call(f32[5,640,640]{2,1,0:T(8,128)} %bitcast.14, f32[640,1280]{1,0:T(8,128)} %get-tuple-element.83.refs_1_, f32[640,1280]{1,0:T(8,128)} %get-tuple-element.84.refs_2_, f32[2,16,640]{2,1,0:T(8,128)} %maximum_maximum_fusion.refs_3_), custom_call_target="tpu_custom_call" | custom-call | bytes 23592960 | tf_op jit(solution)/shard_map/pallas_call | solution.py:885
  392.2 1.8 slice.103
  394.8 2.2 convert.2
  398.3 1.5 fusion
  399.8 1.9 maximum_convert_fusion
  401.7 7.9 %shard_map.262 = f32[16,640,256]{2,1,0:T(8,128)} custom-call(s32[3]{0:T(128)} %pad_add_fusion.pre, bf16[8,640,256]{2,1,0:T(8,128)(2,1)} %collective-permute-done.7.part_ref, bf16[16,640,256]{2,1,0:T(8,128)(2,1)} %dy_ref.1, f32[16,640,256]{2,1,0:T(8,128)} %get-tuple-element.81._), custom_call_target="tpu_custom_call", output_to_operand_aliasing={{}: (3, {})} | custom-call | flops 2621440 | bytes 10485760 | tf_op jit(solution)/shard_map/pallas_call | solution.py:708
  (86 shorter events, 16.8 us)
Async XLA Ops:
  11.7 39.5 %copy-start.9 = (s32[16,256]{1,0:T(8,128)S(1)}, s32[16,256]{1,0:T(8,128)}, u32[]{:S(2)}) copy-start(s32[16,256]{1,0:T(8,128)} %param.16) | copy-start | bytes 49156
  50.5 71.3 %collective-permute-start.4 = (bf16[8,640,256]{2,1,0:T(8,128)(2,1)}, bf16[8,640,256]{2,1,0:T(8,128)(2,1)}, u32[]{:S(2)}, u32[]{:S(2)}) collective-permute-start(bf16[8,640,256]{2,1,0:T(8,128)(2,1)} %constant_dynamic-slice_fusion), channel_id=1, source_target_pairs={{0,1},{1,0},{2,3},{3,2},{4,5},{5,4},{6,7},{7,6},{8,9},{9,8},{10,11... | collective-permute-start | bytes 7864328 | tf_op jit(solution)/shard_map/ppermute | solution.py:906
  54.6 22.7 %copy-start.1 = (bf16[640,1280]{1,0:T(8,128)(2,1)S(1)}, bf16[640,1280]{1,0:T(8,128)(2,1)}, u32[]{:S(2)}) copy-start(bf16[640,1280]{1,0:T(8,128)(2,1)} %get-tuple-element.62.refs_2_) | copy-start | bytes 4915204
  72.3 16.7 %collective-permute-start.2 = (bf16[2,640,128]{2,1,0:T(8,128)(2,1)}, bf16[2,640,128]{2,1,0:T(8,128)(2,1)}, u32[]{:S(2)}, u32[]{:S(2)}) collective-permute-start(bf16[2,640,128]{2,1,0:T(8,128)(2,1)} %get-tuple-element.64), channel_id=1, source_target_pairs={{0,2},{2,4},{4,6},{6,8},{8,10},{10,12},{12,14},{14,16},{16,18},{18... | collective-permute-start | bytes 983048 | tf_op jit(solution)/shard_map/ppermute | solution.py:912
  75.0 14.1 %collective-permute-start.3 = (bf16[2,640,128]{2,1,0:T(8,128)(2,1)}, bf16[2,640,128]{2,1,0:T(8,128)(2,1)}, u32[]{:S(2)}, u32[]{:S(2)}) collective-permute-start(bf16[2,640,128]{2,1,0:T(8,128)(2,1)} %get-tuple-element.65), channel_id=1, source_target_pairs={{2,0},{4,2},{6,4},{8,6},{10,8},{12,10},{14,12},{16,14},{18,16},{20... | collective-permute-start | bytes 983048 | tf_op jit(solution)/shard_map/ppermute | solution.py:912
  79.6 9.4 %copy-start.10 = (f32[640]{0:T(1024)S(1)}, f32[640]{0:T(1024)}, u32[]{:S(2)}) copy-start(f32[640]{0:T(1024)} %param.29) | copy-start | bytes 7684
  143.6 27.8 %collective-permute-start.5 = (bf16[2,640,128]{2,1,0:T(8,128)(2,1)}, bf16[2,640,128]{2,1,0:T(8,128)(2,1)S(1)}, u32[]{:S(2)}, u32[]{:S(2)}) collective-permute-start(bf16[2,640,128]{2,1,0:T(8,128)(2,1)} %get-tuple-element.74), channel_id=1, source_target_pairs={{0,2},{2,4},{4,6},{6,8},{8,10},{10,12},{12,14},{14,16},{16,18},{18... | collective-permute-start | bytes 983048 | tf_op jit(solution)/shard_map/ppermute | solution.py:912
  146.7 22.4 %copy-start = (bf16[640,1280]{1,0:T(8,128)(2,1)S(1)}, bf16[640,1280]{1,0:T(8,128)(2,1)}, u32[]{:S(2)}) copy-start(bf16[640,1280]{1,0:T(8,128)(2,1)} %get-tuple-element.55.w_ref) | copy-start | bytes 4915204
  146.7 24.7 %collective-permute-start.6 = (bf16[2,640,128]{2,1,0:T(8,128)(2,1)}, bf16[2,640,128]{2,1,0:T(8,128)(2,1)S(1)}, u32[]{:S(2)}, u32[]{:S(2)}) collective-permute-start(bf16[2,640,128]{2,1,0:T(8,128)(2,1)} %get-tuple-element.75), channel_id=1, source_target_pairs={{2,0},{4,2},{6,4},{8,6},{10,8},{12,10},{14,12},{16,14},{18,16},{20... | collective-permute-start | bytes 983048 | tf_op jit(solution)/shard_map/ppermute | solution.py:912
  163.9 81.0 %collective-permute-start = (bf16[2,640,128]{2,1,0:T(8,128)(2,1)}, bf16[2,640,128]{2,1,0:T(8,128)(2,1)S(1)}, u32[]{:S(2)}, u32[]{:S(2)}) collective-permute-start(bf16[2,640,128]{2,1,0:T(8,128)(2,1)} %get-tuple-element.58), channel_id=1, source_target_pairs={{0,2},{2,4},{4,6},{6,8},{8,10},{10,12},{12,14},{14,16},{16,18},{18... | collective-permute-start | bytes 983048 | tf_op jit(solution)/shard_map/ppermute | solution.py:912
  167.6 77.4 %collective-permute-start.1 = (bf16[2,640,128]{2,1,0:T(8,128)(2,1)}, bf16[2,640,128]{2,1,0:T(8,128)(2,1)S(1)}, u32[]{:S(2)}, u32[]{:S(2)}) collective-permute-start(bf16[2,640,128]{2,1,0:T(8,128)(2,1)} %get-tuple-element.59), channel_id=1, source_target_pairs={{2,0},{4,2},{6,4},{8,6},{10,8},{12,10},{14,12},{16,14},{18,16},{20... | collective-permute-start | bytes 983048 | tf_op jit(solution)/shard_map/ppermute | solution.py:912
  171.4 0.9 copy-start.13
  171.4 0.9 copy-start.14
  243.4 158.4 %collective-permute-start.7 = (bf16[8,640,256]{2,1,0:T(8,128)(2,1)}, bf16[8,640,256]{2,1,0:T(8,128)(2,1)}, u32[]{:S(2)}, u32[]{:S(2)}) collective-permute-start(bf16[8,640,256]{2,1,0:T(8,128)(2,1)} %get-tuple-element.80), channel_id=1, source_target_pairs={{0,1},{1,0},{2,3},{3,2},{4,5},{5,4},{6,7},{7,6},{8,9},{9,8},{10,11... | collective-permute-start | bytes 7864328 | tf_op jit(solution)/shard_map/ppermute | solution.py:906
  245.0 0.7 copy-start.11
  245.0 0.8 copy-start.12
  245.8 29.4 %copy-start.7 = (f32[640,128]{1,0:T(8,128)S(1)}, f32[640,128]{1,0:T(8,128)}, u32[]{:S(2)}) copy-start(f32[640,128]{1,0:T(8,128)} %get-tuple-element.88) | copy-start | bytes 983044
  245.8 29.7 %copy-start.6 = (f32[640,128]{1,0:T(8,128)S(1)}, f32[640,128]{1,0:T(8,128)}, u32[]{:S(2)}) copy-start(f32[640,128]{1,0:T(8,128)} %get-tuple-element.89) | copy-start | bytes 983044
  245.8 29.9 %copy-start.5 = (f32[640,128]{1,0:T(8,128)S(1)}, f32[640,128]{1,0:T(8,128)}, u32[]{:S(2)}) copy-start(f32[640,128]{1,0:T(8,128)} %get-tuple-element.90) | copy-start | bytes 983044
  245.8 30.2 %copy-start.2 = (f32[1280,128]{1,0:T(8,128)S(1)}, f32[1280,128]{1,0:T(8,128)}, u32[]{:S(2)}) copy-start(f32[1280,128]{1,0:T(8,128)} %get-tuple-element.93) | copy-start | bytes 1966084
  245.8 32.9 %copy-start.8 = (f32[640,128]{1,0:T(8,128)S(1)}, f32[640,128]{1,0:T(8,128)}, u32[]{:S(2)}) copy-start(f32[640,128]{1,0:T(8,128)} %get-tuple-element.87) | copy-start | bytes 983044
  275.2 3.9 copy-start.4
  275.2 4.2 %copy-start.3 = (f32[1280,128]{1,0:T(8,128)S(1)}, f32[1280,128]{1,0:T(8,128)}, u32[]{:S(2)}) copy-start(f32[1280,128]{1,0:T(8,128)} %get-tuple-element.92) | copy-start | bytes 1966084

commit v3 on v2

v3 whole, which is shorter than its diff:
```python
import functools
import math

import jax
import jax.numpy as jnp
from jax import lax
from jax.experimental import pallas as pl
from jax.experimental.pallas import tpu as pltpu
from jax.sharding import PartitionSpec as P

D = 1280
INNER = 640
KERNEL = 5
DILATION = 16
REACH = KERNEL // 2 * DILATION
EPS = 1e-05
HALF_ROOT = math.sqrt(0.5)
DENSITY = 1.0 / math.sqrt(2.0 * math.pi)
F32 = jnp.float32
BF16 = jnp.bfloat16
LANES = 128
VMEM_BYTES = 60 * 1024 * 1024


TWO = 2


def rows_of(width):
    return next(r for r in (64, 32, 16) if width % r == 0)


def straight(width, length, body, init):
    rows = next(r for r in (64, 32, 16) if width % r == 0 and r * length <= 64 * 256 or r == 16)
    for i in range(width // rows):
        init = body(pl.ds(i * rows, rows), init)
    return init


def fold_rows(v):
    return v.reshape(v.shape[0] // 8, 8, v.shape[1]).sum(0)


def fold_lanes(v):
    out = v[:, :LANES]
    for j in range(1, v.shape[1] // LANES):
        out = out + v[:, j * LANES : (j + 1) * LANES]
    return out


def spread(p, length):
    return jnp.concatenate([p] * (length // LANES), axis=1)


def loop(width, body, init):
    rows = rows_of(width)

    def step(i, carry):
        return body(pl.ds(pl.multiple_of(i * rows, rows), rows), carry)

    return lax.fori_loop(0, width // rows, step, init)


def norm_stats(load, width, length, rolled=False):
    def over(body, init):
        return loop(width, body, init) if rolled else straight(width, length, body, init)

    zero = jnp.zeros((8, length), F32)
    total = over(lambda sl, a: a + fold_rows(load(sl)), zero)
    mean = total.sum(0, keepdims=True) / width

    def square(sl, a):
        c = load(sl) - mean
        return a + fold_rows(c * c)

    total = over(square, zero)
    return mean, lax.rsqrt(total.sum(0, keepdims=True) / width + EPS)


def cdf(p):
    return 0.5 + 0.5 * lax.erf(p * HALF_ROOT)


def slope(p, phi):
    return phi + p * (DENSITY * jnp.exp(p * p * -0.5))


def call(kernel, grid, in_specs, out_specs, out_shape, scratch=(), prefetch=1, aliases=None, cost=None):
    return pl.pallas_call(
        kernel,
        grid_spec=pltpu.PrefetchScalarGridSpec(
            num_scalar_prefetch=prefetch,
            grid=grid,
            in_specs=in_specs,
            out_specs=out_specs,
            scratch_shapes=list(scratch),
        ),
        out_shape=out_shape,
        input_output_aliases=aliases or {},
        cost_estimate=cost,
        compiler_params=pltpu.CompilerParams(vmem_limit_bytes=VMEM_BYTES),
    )


def cost_of(macs, bytes_accessed):
    return pl.CostEstimate(flops=int(2 * macs), bytes_accessed=int(bytes_accessed), transcendentals=0)


def whole(shape):
    return pl.BlockSpec(shape, lambda i, pre: (0,) * len(shape), pipeline_mode=pl.Buffered(1))


def sds(shape, dtype):
    return jax.ShapeDtypeStruct(shape, dtype)


def weight_copies(own_refs, full_refs, sems):
    seq, ch = lax.axis_index("seq"), lax.axis_index("ch")
    core, row = seq % 2, (seq // 2) % 2
    send_sem, recv_sem = sems
    across, along, beside = {"ch": 1 - ch}, {"seq": seq + 2 - 4 * row}, {"seq": seq + 1 - 2 * core}

    def part(ref, at, size):
        at = pl.multiple_of(at, 16)
        return ref.at[:, pl.ds(at, size), :] if len(ref.shape) == 3 else ref.at[pl.ds(at, size), :]

    (w_in, conv, w_out), (w_in_full, conv_full, w_out_full) = own_refs, full_refs
    items = [
        (w_in, w_in_full),
        (conv.at[pl.ds(0, 2)], conv_full.at[pl.ds(0, 2)]),
        (conv.at[pl.ds(2, 3)], conv_full.at[pl.ds(2, 3)]),
        (w_out, w_out_full),
    ]
    local, first_hop, second_hop, third_hop = [], [], [], []
    for k, (own, full) in enumerate(items):
        half = own.shape[-2]
        size = half // 4

        def remote(src, dst, slot, device):
            return pltpu.make_async_remote_copy(
                src_ref=src,
                dst_ref=dst,
                send_sem=send_sem.at[k, slot],
                recv_sem=recv_sem.at[k, slot],
                device_id=device,
                device_id_type=pl.DeviceIdType.MESH,
            )

        quarter = (row * 2 + core) * size
        local.append(remote(own, part(full, ch * half, half), 4, beside))
        first_hop.append(remote(part(own, quarter, size), part(full, ch * half + quarter, size), 0, across))
        landed = (1 - ch) * half
        mine = part(full, landed + quarter, size)
        second_hop.append(remote(mine, mine, 1, along))
        both = []
        for j, r in enumerate((row, 1 - row)):
            piece = part(full, landed + (r * 2 + core) * size, size)
            both.append(remote(piece, piece, 2 + j, beside))
        third_hop.append(both)
    return local, first_hop, second_hop, third_hop


def first_kernel(comm, pre, x_ref, p_ref, *rest):
    if comm:
        own_refs, own_vec, first_ref, stat_ref = rest[:3], rest[3], rest[4], rest[5]
        full_refs, full_vec = rest[6:9], rest[9]
        exchange(own_refs, own_vec, full_refs, full_vec, rest[10:12], rest[12:])
    else:
        first_ref, stat_ref = rest
    length = x_ref.shape[2]
    mean, scale = norm_stats(lambda sl: x_ref[0, sl, :].astype(F32), D, length, True)
    stat_ref[0, 0:1, :] = mean
    stat_ref[0, 1:2, :] = scale

    def body(sl, carry):
        hat = (x_ref[0, sl, :].astype(F32) - mean) * scale
        point = hat * spread(p_ref[0, sl, :], length) + spread(p_ref[1, sl, :], length)
        first_ref[0, sl, :] = (point * cdf(point)).astype(BF16)
        return carry

    loop(D, body, 0)


def exchange(own_refs, own_vec, full_refs, full_vec, sems, vec_sems):
    step, steps = pl.program_id(0), pl.num_programs(0)
    seq, ch = lax.axis_index("seq"), lax.axis_index("ch")
    core, row = seq % 2, (seq // 2) % 2
    local, first_hop, second_hop, third_hop = weight_copies(own_refs, full_refs, sems)
    vec_local = pltpu.make_async_copy(own_vec, full_vec.at[ch], vec_sems[0])
    vec_remote = pltpu.make_async_remote_copy(
        src_ref=own_vec,
        dst_ref=full_vec.at[ch],
        send_sem=vec_sems[1],
        recv_sem=vec_sems[2],
        device_id={"ch": 1 - ch},
        device_id_type=pl.DeviceIdType.MESH,
    )

    @pl.when(step == 0)
    def _():
        barrier = pltpu.get_barrier_semaphore()
        for device in ({"ch": 1 - ch}, {"seq": seq + 2 - 4 * row}, {"seq": seq + 1 - 2 * core}):
            pl.semaphore_signal(barrier, inc=1, device_id=device, device_id_type=pl.DeviceIdType.MESH)
        pl.semaphore_wait(barrier, 3)
        vec_remote.start()
        first_hop[0].start()
        vec_local.start()
        for copy in local:
            copy.start()

    for k in range(4):

        if k > 0:

            @pl.when(step == (0, 1, 4, 7)[k])
            def _():
                first_hop[k].start()

        @pl.when(step == (4, 7, 10, 12)[k])
        def _():
            first_hop[k].wait()
            second_hop[k].start()
            third_hop[k][0].start()

        @pl.when(step == (7, 10, 14, 15)[k])
        def _():
            second_hop[k].wait()
            third_hop[k][1].start()

    @pl.when(step == steps - 1)
    def _():
        vec_remote.wait()
        vec_local.wait()
        for k in range(4):
            local[k].wait()
            third_hop[k][0].wait()
            third_hop[k][1].wait()


def first_call(pre, tokens, p1, weights, vec):
    seqs, _, length = tokens.shape
    comm = weights is not None
    any_spec = pl.BlockSpec(memory_space=pl.ANY)
    in_specs = [pl.BlockSpec((1, D, length), lambda i, pre: ((pre[0] + i) % seqs, 0, 0)), whole((2, D, LANES))]
    out_specs = [
        pl.BlockSpec((1, D, length), lambda i, pre: (i, 0, 0)),
        pl.BlockSpec((1, 2, length), lambda i, pre: (i, 0, 0)),
    ]
    shapes = [sds((seqs, D, length), BF16), sds((seqs, 2, length), F32)]
    args, scratch = [pre, tokens, p1], []
    if comm:
        in_specs += [any_spec] * 4
        out_specs += [any_spec] * 4
        shapes += [sds(w.shape[:-2] + (2 * w.shape[-2], w.shape[-1]), BF16) for w in weights]
        shapes.append(sds((2,) + vec.shape, F32))
        args += list(weights) + [vec]
        dma = pltpu.SemaphoreType.DMA
        scratch = [dma((4, 5)), dma((4, 5)), dma, dma, dma]

    def kernel(*refs):
        first_kernel(comm, *refs)

    if comm:

        def at(i):
            return ((lax.axis_index("ch") * (seqs // 2) + i) % seqs, 0, 0)

        return pl.pallas_call(
            lambda *refs: first_kernel(True, None, *refs),
            grid=(seqs,),
            in_specs=[
                pl.BlockSpec((1, D, length), at),
                pl.BlockSpec((2, D, LANES), lambda i: (0, 0, 0), pipeline_mode=pl.Buffered(1)),
            ]
            + [any_spec] * 4,
            out_specs=tuple(
                [pl.BlockSpec((1, D, length), lambda i: (i, 0, 0)), pl.BlockSpec((1, 2, length), lambda i: (i, 0, 0))]
                + [any_spec] * 4
            ),
            out_shape=tuple(shapes),
            scratch_shapes=scratch,
            cost_estimate=cost_of(seqs * D * length * 40, seqs * D * length * 4),
            compiler_params=pltpu.CompilerParams(
                vmem_limit_bytes=VMEM_BYTES, collective_id=1, has_side_effects=True
            ),
        )(*args[1:])
    return call(kernel, (seqs,), in_specs, tuple(out_specs), tuple(shapes))(*args)


def put_edges(group, ref, lead_ref, trail_ref):
    length = ref.shape[2]
    place = pl.program_id(0) % (group // TWO)
    for k in range(group // TWO):

        @pl.when(place == k)
        def _():
            for j in range(TWO):
                lanes = slice((k * TWO + j) * REACH, (k * TWO + j + 1) * REACH)
                lead_ref[0, :, lanes] = ref[j, :, :REACH]
                trail_ref[0, :, lanes] = ref[j, :, length - REACH :]


def middle_kernel(group, keep, pre, first_ref, mask_ref, w_ref, p_ref, mid_ref, lead_ref, trail_ref, *rest):
    nar_refs = rest[-TWO:]
    length = first_ref.shape[2]
    for j in range(TWO):
        nar = jnp.dot(w_ref[...], first_ref[j], preferred_element_type=F32)
        nar_refs[j][...] = nar + spread(p_ref[0], length)
    for j in range(TWO):
        nar_ref = nar_refs[j]
        mean, scale = norm_stats(lambda sl: nar_ref[sl, :], INNER, length)
        mask = mask_ref[j].astype(F32)

        def body(sl, carry):
            hat = (nar_ref[sl, :] - mean) * scale
            point = hat * spread(p_ref[1, sl, :], length) + spread(p_ref[2, sl, :], length)
            phi = cdf(point)
            mid_ref[j, sl, :] = (point * phi * mask).astype(BF16)
            if keep:
                rest[0][j, sl, :] = hat.astype(BF16)
                rest[1][j, sl, :] = slope(point, phi) * mask
            return carry

        straight(INNER, length, body, 0)
        if keep:
            rest[2][j] = scale
    put_edges(group, mid_ref, lead_ref, trail_ref)


def middle_call(pre, first, mask, w_in, p2, count, offset, group, keep):
    _, _, length = first.shape
    seqs = mask.shape[0]
    edge = pl.BlockSpec((1, INNER, group * REACH), lambda i, pre: (i // (group // TWO), 0, 0))
    edge_shape = sds((count // group, INNER, group * REACH), BF16)
    own = pl.BlockSpec((TWO, INNER, length), lambda i, pre: (i, 0, 0))
    outs = [own, edge, edge]
    shapes = [sds((count, INNER, length), BF16), edge_shape, edge_shape]
    if keep:
        outs += [own, own, pl.BlockSpec((TWO, 1, length), lambda i, pre: (i, 0, 0))]
        shapes += [
            sds((count, INNER, length), BF16),
            sds((count, INNER, length), F32),
            sds((count, 1, length), F32),
        ]
    return call(
        functools.partial(middle_kernel, group, keep),
        (count // TWO,),
        [
            pl.BlockSpec((TWO, D, length), lambda i, pre: (offset // TWO + i, 0, 0)),
            pl.BlockSpec((TWO, 1, length), lambda i, pre: (((pre[0] + offset) // TWO + i) % (seqs // TWO), 0, 0)),
            whole((INNER, D)),
            whole((3, INNER, LANES)),
        ],
        tuple(outs),
        tuple(shapes),
        scratch=[pltpu.VMEM((INNER, length), F32)] * TWO,
        cost=cost_of(count * INNER * D * length * 1.5, count * (D + INNER * 3) * length * 2),
    )(pre, first, mask.reshape(seqs, 1, length), w_in, p2)


def gather_windows(group, body_ref, before_ref, after_ref, pad_ref, cat_refs, order):
    width, length = body_ref.shape[1], body_ref.shape[2]
    place = pl.program_id(0) % (group // TWO)
    for k in range(group // TWO):

        @pl.when(place == k)
        def _():
            for j in range(TWO):
                lanes = slice((k * TWO + j) * REACH, (k * TWO + j + 1) * REACH)
                pad_ref[j, :, LANES - REACH : LANES] = before_ref[0, :, lanes]
                pad_ref[j, :, LANES + length : LANES + length + REACH] = after_ref[0, :, lanes]

    for j in range(TWO):
        pad_ref[j, :, LANES : LANES + length] = body_ref[j]
        for tap in range(KERNEL):
            start = LANES + order * (tap - KERNEL // 2) * DILATION
            cat_refs[j][tap * width : (tap + 1) * width, :] = pad_ref[j, :, start : start + length]


def last_kernel(
    group, keep, pre, mid_ref, before_ref, after_ref, x_ref, wc_ref, wo_ref, p_ref, b_ref, *rest
):
    if keep:
        mixed_ref, hat_ref, gp_ref, scale_ref, last_out = rest[:5]
        last_refs = [last_out.at[j] for j in range(TWO)]
    else:
        mixed_ref = rest[1]
        last_refs = rest[-TWO:]
        rest = rest[:-TWO]
    pad_ref, cat_refs, conv_refs = rest[-1 - 2 * TWO], rest[-2 * TWO : -TWO], rest[-TWO:]
    length = mid_ref.shape[2]
    gather_windows(group, mid_ref, before_ref, after_ref, pad_ref, cat_refs, 1)
    for j in range(TWO):
        conv = jnp.dot(wc_ref[...], cat_refs[j][...], preferred_element_type=F32)
        conv_refs[j][...] = conv + spread(p_ref[0], length)
    for j in range(TWO):
        conv_ref, last_ref = conv_refs[j], last_refs[j]
        mean, scale = norm_stats(lambda sl: conv_ref[sl, :], INNER, length)

        def body(sl, carry):
            hat = (conv_ref[sl, :] - mean) * scale
            point = hat * spread(p_ref[1, sl, :], length) + spread(p_ref[2, sl, :], length)
            phi = cdf(point)
            last_ref[sl, :] = (point * phi).astype(BF16)
            if keep:
                hat_ref[j, sl, :] = hat.astype(BF16)
                gp_ref[j, sl, :] = slope(point, phi)
            return carry

        straight(INNER, length, body, 0)
        if keep:
            scale_ref[j] = scale
        branch = jnp.dot(wo_ref[...], last_ref[...], preferred_element_type=F32)
        mixed_ref[j] = (x_ref[j].astype(F32) + branch + spread(b_ref[...], length)).astype(BF16)


def last_call(pre, mid, before, after, tokens, wc, wo_t, p2, b_out, count, offset, group, keep, mixed):
    _, _, length = mid.shape
    seqs, share = tokens.shape[0], wo_t.shape[0]
    edge = pl.BlockSpec((1, INNER, group * REACH), lambda i, pre: (i // (group // TWO), 0, 0))
    own = pl.BlockSpec((TWO, INNER, length), lambda i, pre: (i, 0, 0))

    def pair_at(i, pre):
        return ((pre[0] + offset) // TWO + i) % (seqs // TWO)

    outs = [pl.BlockSpec((TWO, share, length), lambda i, pre: (pair_at(i, pre), 0, 0))]
    shapes = [sds((seqs, share, length), BF16)]
    in_specs = [
        own,
        edge,
        edge,
        pl.BlockSpec((TWO, share, length), lambda i, pre: (pair_at(i, pre), pre[1], 0)),
        whole((INNER, KERNEL * INNER)),
        whole((share, INNER)),
        whole((3, INNER, LANES)),
        whole((share, LANES)),
    ]
    args = [pre, mid, before, after, tokens, wc, wo_t, p2, b_out]
    aliases = None
    scratch = [pltpu.VMEM((TWO, INNER, length + 2 * LANES), BF16)]
    scratch += [pltpu.VMEM((KERNEL * INNER, length), BF16)] * TWO
    scratch += [pltpu.VMEM((INNER, length), F32)] * TWO
    if keep:
        outs += [own, own, pl.BlockSpec((TWO, 1, length), lambda i, pre: (i, 0, 0)), own]
        saved = sds((count, INNER, length), BF16)
        shapes += [saved, sds((count, INNER, length), F32), sds((count, 1, length), F32), saved]
    else:
        scratch += [pltpu.VMEM((INNER, length), BF16)] * TWO
        in_specs.append(pl.BlockSpec(memory_space=pl.ANY))
        args.append(mixed)
        aliases = {len(args) - 1: 0}
    return call(
        functools.partial(last_kernel, group, keep),
        (count // TWO,),
        in_specs,
        tuple(outs),
        tuple(shapes),
        scratch=scratch,
        aliases=aliases,
        cost=cost_of(count * INNER * (KERNEL * INNER + share) * length * 1.3, count * share * 6 * length * 2),
    )(*args)


def side(ref, sl):
    return jnp.concatenate([ref[j, sl, :].astype(F32) for j in range(TWO)], axis=1)


def across(ref, row):
    return jnp.concatenate([ref[j, row : row + 1, :] for j in range(TWO)], axis=1)


def norm_back(d_ref, gp_ref, hat_ref, scale, gain_ref, gg_ref, gb_ref, sum_ref, put):
    wide = d_ref.shape[1]
    zero = jnp.zeros((8, wide), F32)

    def body(sl, carry):
        d_pre = d_ref[sl, :] * side(gp_ref, sl)
        hat = side(hat_ref, sl)
        gg_ref[sl, :] += fold_lanes(d_pre * hat)
        gb_ref[sl, :] += fold_lanes(d_pre)
        e = d_pre * spread(gain_ref[0, sl, :], wide)
        d_ref[sl, :] = e
        return carry[0] + fold_rows(e), carry[1] + fold_rows(e * hat)

    total, dot = straight(INNER, wide, body, (zero, zero))
    total = total.sum(0, keepdims=True) * (scale / INNER)
    dot = dot.sum(0, keepdims=True) * (scale / INNER)

    def finish(sl, carry):
        v = (d_ref[sl, :] * scale - total - side(hat_ref, sl) * dot).astype(BF16)
        put(sl, v)
        sum_ref[sl, :] += fold_lanes(v.astype(F32))
        return carry

    straight(INNER, wide, finish, 0)


def rear_kernel(group, chs, pre, *refs):
    dy_refs = refs[:chs]
    w_ref, hat_ref, gp_ref, last_ref, scale_ref, p_ref = refs[chs : chs + 6]
    dconv_ref, lead_ref, trail_ref, gg_ref, gb_ref, gc_ref, gw_ref, go_ref = refs[chs + 6 : chs + 14]
    dy_ref, d_ref = refs[chs + 14 :]
    share, length = dy_refs[0].shape[1], dy_refs[0].shape[2]

    @pl.when(pl.program_id(0) == 0)
    def _():
        for ref in (gg_ref, gb_ref, gc_ref, gw_ref, go_ref):
            ref[...] = jnp.zeros_like(ref)

    for r in range(chs):
        at = pl.multiple_of(((pre[1] + chs - r) % chs) * share, share)
        for j in range(TWO):
            dy_ref[pl.ds(at, share), j * length : (j + 1) * length] = dy_refs[r][j]
    d_ref[...] = jnp.dot(w_ref[...], dy_ref[...], preferred_element_type=F32)
    last = jnp.concatenate([last_ref[j] for j in range(TWO)], axis=1)
    gw_ref[...] += lax.dot_general(last, dy_ref[...], (((1,), (1,)), ((), ())), preferred_element_type=F32)
    go_ref[...] += fold_lanes(dy_ref[...].astype(F32))

    def put(sl, v):
        for j in range(TWO):
            dconv_ref[j, sl, :] = v[:, j * length : (j + 1) * length]

    norm_back(d_ref, gp_ref, hat_ref, across(scale_ref, 0), p_ref, gg_ref, gb_ref, gc_ref, put)
    put_edges(group, dconv_ref, lead_ref, trail_ref)


def const(shape):
    return pl.BlockSpec(shape, lambda i, pre: (0,) * len(shape), pipeline_mode=pl.Buffered(1))


def rear_call(pre, cot, others, w_out, hat, gp, last, scale, p2, group):
    seqs, share, length = cot.shape
    count = hat.shape[0]
    chs = 1 + len(others)
    edge = pl.BlockSpec((1, INNER, group * REACH), lambda i, pre: (i // (group // TWO), 0, 0))
    edge_shape = sds((count // group, INNER, group * REACH), BF16)
    own = pl.BlockSpec((TWO, INNER, length), lambda i, pre: (i, 0, 0))
    sums = [(INNER, LANES)] * 3 + [(INNER, D), (D, LANES)]
    return call(
        functools.partial(rear_kernel, group, chs),
        (count // TWO,),
        [pl.BlockSpec((TWO, share, length), lambda i, pre: (pre[0] // TWO + i, 0, 0))]
        + [pl.BlockSpec((TWO, share, length), lambda i, pre: (i, 0, 0))] * (chs - 1)
        + [
            whole((INNER, D)),
            own,
            own,
            own,
            pl.BlockSpec((TWO, 1, length), lambda i, pre: (i, 0, 0)),
            whole((1, INNER, LANES)),
        ],
        tuple([own, edge, edge] + [const(v) for v in sums]),
        tuple([sds((count, INNER, length), BF16), edge_shape, edge_shape] + [sds(v, F32) for v in sums]),
        scratch=[pltpu.VMEM((D, TWO * length), BF16), pltpu.VMEM((INNER, TWO * length), F32)],
        cost=cost_of(count * INNER * D * length * 2.5, count * INNER * 5 * length * 2),
    )(pre, cot, *others, w_out, hat, gp, last, scale, p2)


def front_kernel(group, chs, pre, *refs):
    dconv_ref, before_ref, after_ref, mid_ref, hat_ref, gp_ref, scale_ref = refs[:7]
    x_ref, stat_ref, dy_ref, wc_ref, wi_ref, p2_ref, p1_ref = refs[7:14]
    refs = refs[14:]
    gt_ref = refs[0]
    send_refs = refs[1:chs]
    gcw_ref, gwi_ref, gg2_ref, gb2_ref, gbi_ref, gg1_ref, gb1_ref = refs[chs : chs + 7]
    pad_ref, cat_ref, d_ref, dn_ref, df_ref, first_ref = refs[chs + 7 :]
    share, length = dy_ref.shape[1], dy_ref.shape[2]
    wide = TWO * length

    @pl.when(pl.program_id(0) == 0)
    def _():
        for ref in (gcw_ref, gwi_ref, gg2_ref, gb2_ref, gbi_ref, gg1_ref, gb1_ref):
            ref[...] = jnp.zeros_like(ref)

    cats = [cat_ref.at[:, j * length : (j + 1) * length] for j in range(TWO)]
    gather_windows(group, dconv_ref, before_ref, after_ref, pad_ref, cats, -1)
    d_ref[...] = jnp.dot(wc_ref[...], cat_ref[...], preferred_element_type=F32)
    mid = jnp.concatenate([mid_ref[j] for j in range(TWO)], axis=1)
    gcw_ref[...] += lax.dot_general(cat_ref[...], mid, (((1,), (1,)), ((), ())), preferred_element_type=F32)

    def put(sl, v):
        dn_ref[sl, :] = v

    norm_back(d_ref, gp_ref, hat_ref, across(scale_ref, 0), p2_ref, gg2_ref, gb2_ref, gbi_ref, put)
    df_ref[...] = jnp.dot(wi_ref[...], dn_ref[...], preferred_element_type=F32)
    mean_in, scale_in = across(stat_ref, 0), across(stat_ref, 1)
    zero = jnp.zeros((8, wide), F32)

    def inner(sl, carry):
        hat = (side(x_ref, sl) - mean_in) * scale_in
        gain = spread(p1_ref[0, sl, :], wide)
        point = hat * gain + spread(p1_ref[1, sl, :], wide)
        phi = cdf(point)
        first_ref[sl, :] = (point * phi).astype(BF16)
        d_pre = df_ref[sl, :] * slope(point, phi)
        gg1_ref[sl, :] += fold_lanes(d_pre * hat)
        gb1_ref[sl, :] += fold_lanes(d_pre)
        e = d_pre * gain
        df_ref[sl, :] = e
        return carry[0] + fold_rows(e), carry[1] + fold_rows(e * hat)

    total, dot = straight(D, wide, inner, (zero, zero))
    total = total.sum(0, keepdims=True) * (scale_in / D)
    dot = dot.sum(0, keepdims=True) * (scale_in / D)
    gwi_ref[...] += lax.dot_general(
        dn_ref[...], first_ref[...], (((1,), (1,)), ((), ())), preferred_element_type=F32
    )
    for r in range(chs):
        base = ((pre[1] + r) % chs) * share

        def out(to, carry):
            rows = pl.ds(pl.multiple_of(base + to.start, 16), to.size)
            hat = (side(x_ref, rows) - mean_in) * scale_in
            v = df_ref[rows, :] * scale_in - total - hat * dot
            for j in range(TWO):
                half = v[:, j * length : (j + 1) * length]
                if r == 0:
                    gt_ref[j, to, :] = half + dy_ref[j, to, :].astype(F32)
                else:
                    send_refs[r - 1][j, to, :] = half.astype(BF16)
            return carry

        straight(share, wide, out, 0)


def front_call(pre, dconv, before, after, mid, hat, gp, scale, tokens, stat, cot, wc_t, wi_t, p2, p1, chs, group):
    seqs, share, length = cot.shape
    count = dconv.shape[0]
    edge = pl.BlockSpec((1, INNER, group * REACH), lambda i, pre: (i // (group // TWO), 0, 0))
    own = pl.BlockSpec((TWO, INNER, length), lambda i, pre: (i, 0, 0))

    def seq_block(rows):
        return pl.BlockSpec((TWO, rows, length), lambda i, pre: (pre[0] // TWO + i, 0, 0))

    inner_part, outer_part = (INNER, LANES), (D, LANES)
    sums = [(KERNEL * INNER, INNER), (INNER, D), inner_part, inner_part, inner_part, outer_part, outer_part]
    wide = TWO * length
    return call(
        functools.partial(front_kernel, group, chs),
        (count // TWO,),
        [
            own,
            edge,
            edge,
            own,
            own,
            own,
            pl.BlockSpec((TWO, 1, length), lambda i, pre: (i, 0, 0)),
            seq_block(D),
            pl.BlockSpec((TWO, 2, length), lambda i, pre: (i, 0, 0)),
            seq_block(share),
            whole((INNER, KERNEL * INNER)),
            whole((D, INNER)),
            whole((1, INNER, LANES)),
            whole((2, D, LANES)),
        ],
        tuple(
            [seq_block(share)]
            + [pl.BlockSpec((TWO, share, length), lambda i, pre: (i, 0, 0))] * (chs - 1)
            + [const(v) for v in sums]
        ),
        tuple(
            [sds((seqs, share, length), F32)]
            + [sds((count, share, length), BF16)] * (chs - 1)
            + [sds(v, F32) for v in sums]
        ),
        scratch=[
            pltpu.VMEM((TWO, INNER, length + 2 * LANES), BF16),
            pltpu.VMEM((KERNEL * INNER, wide), BF16),
            pltpu.VMEM((INNER, wide), F32),
            pltpu.VMEM((INNER, wide), BF16),
            pltpu.VMEM((D, wide), F32),
            pltpu.VMEM((D, wide), BF16),
        ],
        cost=cost_of(count * INNER * (2 * KERNEL * INNER + 2 * D) * length * 1.3, count * D * 8 * length * 2),
    )(pre, dconv, before, after, mid, hat, gp, scale, tokens, stat, cot, wc_t, wi_t, p2, p1)


def add_kernel(pre, part_ref, dy_ref, _, gt_ref):
    gt_ref[...] = part_ref[...].astype(F32) + dy_ref[...].astype(F32)


def add_call(pre, part, cot, gt, start):
    seqs, share, length = cot.shape
    count = part.shape[0]
    at = lambda i, pre: (pre[start] + i, 0, 0)
    return call(
        add_kernel,
        (count,),
        [
            pl.BlockSpec((1, share, length), lambda i, pre: (i, 0, 0)),
            pl.BlockSpec((1, share, length), at),
            pl.BlockSpec(memory_space=pl.ANY),
        ],
        pl.BlockSpec((1, share, length), at),
        sds((seqs, share, length), F32),
        aliases={3: 0},
        cost=cost_of(count * share * length, count * share * length * 8),
    )(pre, part, cot, gt)


def turn_kernel(pre, w_ref, flat_ref, turned_ref):
    unit = (
        lax.broadcasted_iota(jnp.int32, (INNER, INNER), 0) == lax.broadcasted_iota(jnp.int32, (INNER, INNER), 1)
    ).astype(F32).astype(BF16)
    flat_ref[...] = w_ref[0]
    turned_ref[...] = lax.dot_general(
        unit, w_ref[0], (((1,), (1,)), ((), ())), preferred_element_type=F32
    ).astype(BF16)


def turn_call(pre, conv):
    block = pl.BlockSpec((INNER, INNER), lambda k, pre: (0, k))
    shape = sds((INNER, KERNEL * INNER), BF16)
    return call(
        turn_kernel,
        (KERNEL,),
        [pl.BlockSpec((1, INNER, INNER), lambda k, pre: (k, 0, 0))],
        (block, block),
        (shape, shape),
        cost=cost_of(KERNEL * INNER**3, KERNEL * INNER * INNER * 6),
    )(pre, conv)


def reduce_ticks(stages, starts, half_rows, refs):
    gcw_ref, gwi_ref, gwo_ref, small_ref, out_ref = refs[:5]
    acc, send, recv, swap, res, load_sem, send_sem, recv_sem = refs[5:]
    seq, ch = lax.axis_index("seq"), lax.axis_index("ch")
    streams, levels = len(stages), len(stages[0])
    rows = acc.shape[1] // streams
    size = [rows >> (t + 1) for t in range(levels)]
    at = [rows - (rows >> t) for t in range(levels)]

    def bit(b):
        return (seq // (1 << b)) % 2

    def partner(b):
        return {"seq": seq + (1 - 2 * bit(b)) * (1 << b)}

    low = []
    for q in range(streams):
        place = [q * rows]
        for t in range(levels):
            place.append(place[-1] + bit(stages[q][t]) * size[t])
        low.append(place)

    def loads():
        out = []
        for h in range(2):
            mine = pl.ds(h * half_rows, half_rows)
            pieces = [gcw_ref.at[k, mine, :] for k in range(KERNEL)]
            for ref in (gwi_ref, gwo_ref):
                pieces += [ref.at[mine, pl.ds(j * INNER, INNER)] for j in range(D // INNER)]
            for j, piece in enumerate(pieces):
                out.append((piece, acc.at[h, pl.ds(j * half_rows, half_rows), :]))
            used = len(pieces) * half_rows
            out.append((small_ref.at[h], acc.at[h, pl.ds(used, small_ref.shape[1]), :]))
        return [pltpu.make_async_copy(a, b, load_sem.at[j]) for j, (a, b) in enumerate(out)]

    def begin():
        used = half_rows * (KERNEL + 2 * D // INNER) + small_ref.shape[1]
        for h in range(2):
            acc[h, used:, :] = jnp.zeros((acc.shape[1] - used, INNER), F32)
        for copy in loads():
            copy.start()
        barrier = pltpu.get_barrier_semaphore()
        for device in [partner(b) for b in sorted(stages[0])] + [{"ch": 1 - ch}]:
            pl.semaphore_signal(barrier, inc=1, device_id=device, device_id_type=pl.DeviceIdType.MESH)
        pl.semaphore_wait(barrier, levels + 1)

    def remote(src, dst, q, k, device):
        slot = q * (2 * levels + 1) + k
        return pltpu.make_async_remote_copy(
            src_ref=src,
            dst_ref=dst,
            send_sem=send_sem.at[slot],
            recv_sem=recv_sem.at[slot],
            device_id=device,
            device_id_type=pl.DeviceIdType.MESH,
        )

    def sliced(count, body):
        step = next(r for r in (96, 48, 32, 16) if count % r == 0)

        def one(i, carry):
            body(pl.multiple_of(i * step, 16), step)
            return carry

        lax.fori_loop(0, count // step, one, 0)

    def spot(base, i, step):
        return pl.ds(pl.multiple_of(base + i, 16), step)

    def copy_of(q, k):
        if k < levels:
            window = pl.ds(at[k], size[k])
            return remote(send.at[q, :, window, :], recv.at[q, :, window, :], q, k, partner(stages[q][k]))
        if k == levels:
            return remote(swap.at[0, q], swap.at[1, q], q, k, {"ch": 1 - ch})
        t = 2 * levels - k
        place = pl.ds(pl.multiple_of(low[q][t + 1], 16), size[t])
        return remote(res.at[place, :], res.at[place, :], q, k, partner(stages[q][t]))

    def start(q, k):
        if k < levels:
            away = low[q][k] + (1 - bit(stages[q][k])) * size[k]
            for h in range(2):

                def pack(i, step, h=h):
                    send[q, h, spot(at[k], i, step), :] = acc[h, spot(away, i, step), :].astype(BF16)

                sliced(size[k], pack)
        elif k == levels:
            place = spot(low[q][levels], 0, size[-1])
            swap[0, q] = acc[1 - ch, place, :].astype(BF16)
        copy_of(q, k).start()

    def finish(q, k):
        copy_of(q, k).wait()
        if k < levels:
            for h in range(2):

                def add(i, step, h=h):
                    place = spot(low[q][k + 1], i, step)
                    acc[h, place, :] += recv[q, h, spot(at[k], i, step), :].astype(F32)

                sliced(size[k], add)
        elif k == levels:
            place = spot(low[q][levels], 0, size[-1])
            res[place, :] = (acc[ch, place, :] + swap[1, q].astype(F32)).astype(BF16)

    def tick(now):
        if now == 0:
            for copy in loads():
                copy.wait()
        for q in range(streams):
            k = now - starts[q]
            if 1 <= k <= 2 * levels + 1:
                finish(q, k - 1)
            if 0 <= k <= 2 * levels:
                start(q, k)

    def end():
        done = pltpu.make_async_copy(res, out_ref, load_sem.at[0])
        done.start()
        done.wait()

    return (
        [begin]
        + [functools.partial(tick, now) for now in range(max(starts) + 2 * levels + 2)]
        + [end]
    )


def reduce_plan(small, seq_count):
    half_rows = INNER // 2
    levels = seq_count.bit_length() - 1
    order = list(range(levels))
    one, two = tuple(order), tuple(order[:1] + order[2:] + order[1:2])
    stages, starts = streams_of(one, two)
    streams = len(stages)
    used = half_rows * (KERNEL + 2 * D // INNER) + small.shape[1]
    unit = streams * seq_count * 16
    rows = -(-used // unit) * unit
    each = rows // streams
    slots = streams * (2 * levels + 1)
    dma = pltpu.SemaphoreType.DMA
    scratch = [
        pltpu.VMEM((2, rows, INNER), F32),
        pltpu.VMEM((streams, 2, each - each // seq_count, INNER), BF16),
        pltpu.VMEM((streams, 2, each - each // seq_count, INNER), BF16),
        pltpu.VMEM((2, streams, each // seq_count, INNER), BF16),
        pltpu.VMEM((rows, INNER), BF16),
        dma((2 * (KERNEL + 2 * D // INNER + 1),)),
        dma((slots,)),
        dma((slots,)),
    ]
    return stages, starts, half_rows, rows, scratch


def streams_of(one, two):
    return (one, one, two, one), (0, 1, 0, 2)


def tail_kernel(plan, group, mid_ref, before_ref, after_ref, x_ref, wc_ref, wo_ref, p_ref, b_ref, *rest):
    mixed_in, sums, mixed_ref, total_ref = rest[0], rest[1:5], rest[5], rest[6]
    ticks = reduce_ticks(*plan, (*sums, total_ref, *rest[7:15]))
    step = pl.program_id(0)
    last = 3
    for i in range(last + 1):

        @pl.when(step == i)
        def _():
            ticks[i]()

    last_kernel(
        group, False, None, mid_ref, before_ref, after_ref, x_ref, wc_ref, wo_ref, p_ref, b_ref,
        mixed_in, mixed_ref, *rest[15:],
    )

    @pl.when(step == last)
    def _():
        for tick in ticks[last + 1 :]:
            tick()


def tail_call(mid, before, after, tokens, wc, wo_t, p2, b_out, mixed, sums, group):
    count, _, length = mid.shape
    seqs, share = tokens.shape[0], wo_t.shape[0]
    stages, starts, half_rows, rows, scratch = reduce_plan(sums[3], lax.axis_size("seq"))
    any_spec = pl.BlockSpec(memory_space=pl.ANY)

    def pair_at(i):
        return ((lax.axis_index("ch") + 1) * (seqs // 2 // TWO) + i) % (seqs // TWO)

    def fixed(shape):
        return pl.BlockSpec(shape, lambda i: (0,) * len(shape), pipeline_mode=pl.Buffered(1))

    edge = pl.BlockSpec((1, INNER, group * REACH), lambda i: (i // (group // TWO), 0, 0))
    return pl.pallas_call(
        functools.partial(tail_kernel, (stages, starts, half_rows), group),
        grid=(count // TWO,),
        in_specs=[
            pl.BlockSpec((TWO, INNER, length), lambda i: (i, 0, 0)),
            edge,
            edge,
            pl.BlockSpec((TWO, share, length), lambda i: (pair_at(i), lax.axis_index("ch"), 0)),
            fixed((INNER, KERNEL * INNER)),
            fixed((share, INNER)),
            fixed((3, INNER, LANES)),
            fixed((share, LANES)),
        ]
        + [any_spec] * 5,
        out_specs=(pl.BlockSpec((TWO, share, length), lambda i: (pair_at(i), 0, 0)), any_spec),
        out_shape=(sds((seqs, share, length), BF16), sds((rows, INNER), BF16)),
        scratch_shapes=scratch
        + [pltpu.VMEM((TWO, INNER, length + 2 * LANES), BF16)]
        + [pltpu.VMEM((KERNEL * INNER, length), BF16)] * TWO
        + [pltpu.VMEM((INNER, length), F32)] * TWO
        + [pltpu.VMEM((INNER, length), BF16)] * TWO,
        input_output_aliases={8: 0},
        cost_estimate=cost_of(count * INNER * (KERNEL * INNER + share) * length * 4, rows * INNER * 12),
        compiler_params=pltpu.CompilerParams(vmem_limit_bytes=VMEM_BYTES, collective_id=2, has_side_effects=True),
    )(mid, before, after, tokens, wc, wo_t, p2, b_out, mixed, *sums)


def reduce_kernel(plan, *refs):
    for tick in reduce_ticks(*plan, refs):
        tick()


def reduce_call(sums, seq_count):
    stages, starts, half_rows, rows, scratch = reduce_plan(sums[3], seq_count)
    any_spec = pl.BlockSpec(memory_space=pl.ANY)
    return pl.pallas_call(
        functools.partial(reduce_kernel, (stages, starts, half_rows)),
        in_specs=[any_spec] * 4,
        out_specs=any_spec,
        out_shape=sds((rows, INNER), BF16),
        scratch_shapes=scratch,
        compiler_params=pltpu.CompilerParams(vmem_limit_bytes=VMEM_BYTES, collective_id=2, has_side_effects=True),
    )(*sums)


def rotate(value, axis, count, by):
    return lax.ppermute(value, axis, [(i, (i + by) % count) for i in range(count)])


def shift(value, by):
    count = lax.axis_size("seq")
    pairs = [(i, i + by) for i in range(count) if 0 <= i + by < count]
    return lax.ppermute(value, "seq", pairs)


def rims(lead, trail):
    return shift(trail, 1), shift(lead, -1)


def own_slice(value, width, dim):
    return lax.dynamic_slice_in_dim(value, lax.axis_index("ch") * width, width, dim)


def lane_copies(vectors):
    return jnp.broadcast_to(vectors[..., None], vectors.shape + (LANES,))


def body(
    tokens,
    pad_mask,
    cotangent,
    ln1_gain,
    first_norm_bias,
    w_in,
    b_in,
    ln2_gain,
    ln2_bias,
    conv_w,
    conv_b,
    ln3_gain,
    ln3_bias,
    w_out,
    b_out,
):
    chs = lax.axis_size("ch")
    ch = lax.axis_index("ch")
    seqs, _, length = tokens.shape
    share = b_out.shape[0]
    part = b_in.shape[0]
    n = seqs // chs
    group = min(4, n)
    starts = [((ch + chs - r) % chs) * n for r in range(1, chs)]
    pre = jnp.stack([ch * n, ch] + starts).astype(jnp.int32)
    pair = chs == 2

    p1 = lane_copies(jnp.stack([ln1_gain, first_norm_bias]))
    bo = lane_copies(b_out)
    vec = jnp.stack([b_in, ln2_gain, ln2_bias, conv_b, ln3_gain, ln3_bias, b_in, b_in])
    if pair:
        first, stat, w_in_full, conv_full, w_out_full, vec_full = first_call(
            pre, tokens, p1, (w_in, conv_w, w_out), vec
        )
        inner = vec_full.transpose(1, 0, 2).reshape(8, INNER)[:6]
    else:
        first, stat = first_call(pre, tokens, p1, None, None)
        w_in_full = lax.all_gather(w_in, "ch", axis=0, tiled=True)
        conv_full = lax.all_gather(conv_w, "ch", axis=1, tiled=True)
        w_out_full = lax.all_gather(w_out, "ch", axis=0, tiled=True)
        inner = lax.all_gather(vec, "ch", axis=1, tiled=True)[:6]

    others = []
    for r in range(1, chs):
        block = lax.dynamic_slice_in_dim(cotangent, ((ch + r) % chs) * n, n, 0)
        block, _ = lax.optimization_barrier((block, stat))
        others.append(rotate(block, "ch", chs, r))
    p2 = lane_copies(inner)
    wc, wc_t = turn_call(pre, conv_full)
    wi_t = w_in_full.T
    wo_t = lax.dynamic_slice_in_dim(w_out_full, ch * share, share, 1).T

    mid_own, lead, trail, hat_mid, gp_mid, scale_mid = middle_call(
        pre, first, pad_mask, w_in_full, p2[0:3], n, 0, group, True
    )
    before, after = rims(lead, trail)
    mid_oth, lead, trail = middle_call(pre, first, pad_mask, w_in_full, p2[0:3], seqs - n, n, group, False)
    before_oth, after_oth = rims(lead, trail)
    mixed, hat_out, gp_out, scale_out, last_own = last_call(
        pre, mid_own, before, after, tokens, wc, wo_t, p2[3:6], bo, n, 0, group, True, None
    )
    dconv, lead, trail, gg3, gb3, gcb, gwo, gbo = rear_call(
        pre, cotangent, others, w_out_full, hat_out, gp_out, last_own, scale_out, p2[4:5], group
    )
    lead, trail = rims(lead, trail)
    gt, *rest = front_call(
        pre, dconv, lead, trail, mid_own, hat_mid, gp_mid, scale_mid, tokens, stat, cotangent,
        wc_t, wi_t, p2[1:2], p1, chs, group,
    )
    sends = [rotate(v, "ch", chs, r + 1) for r, v in enumerate(rest[: chs - 1])]
    gcw, gwi, gg2, gb2, gbi, gg1, gb1 = rest[chs - 1 :]
    gcw = gcw.reshape(KERNEL, INNER, INNER)
    inner_sums = jnp.stack([v.sum(1) for v in (gbi, gg2, gb2, gcb, gg3, gb3)])
    outer_sums = jnp.stack([v.sum(1) for v in (gg1, gb1, gbo)])

    if pair:
        small = jnp.concatenate(
            [
                inner_sums.reshape(6, 2, part).transpose(1, 0, 2).reshape(2, 3, INNER),
                outer_sums.reshape(3, 2, share).transpose(1, 0, 2),
                jnp.zeros((2, 10, INNER), F32),
            ],
            axis=1,
        )
        mixed, total = tail_call(
            mid_oth, before_oth, after_oth, tokens, wc, wo_t, p2[3:6], bo, mixed, (gcw, gwi, gwo, small), group
        )
        gcw = total[: KERNEL * part].reshape(KERNEL, part, INNER).astype(F32)
        base = KERNEL * part
        wide = []
        for k in range(2):
            blocks = [total[base + (2 * k + j) * part : base + (2 * k + j + 1) * part] for j in range(2)]
            wide.append(jnp.concatenate(blocks, axis=1).astype(F32))
        gwi, gwo = wide
        base += 4 * part
        inner_sums = total[base : base + 3].reshape(6, part).astype(F32)
        outer_sums = total[base + 3 : base + 6].astype(F32)
    else:
        mixed, = last_call(
            pre, mid_oth, before_oth, after_oth, tokens, wc, wo_t, p2[3:6], bo, seqs - n, n, group, False, mixed
        )
        gcw, gwi, gwo, inner_sums, outer_sums = lax.psum((gcw, gwi, gwo, inner_sums, outer_sums), ("seq", "ch"))
        gcw = own_slice(gcw, part, 1)
        gwi = own_slice(gwi, part, 0)
        gwo = own_slice(gwo, part, 0)
        inner_sums = own_slice(inner_sums, part, 1)
        outer_sums = own_slice(outer_sums, share, 1)
    for r in range(chs - 1):
        gt = add_call(pre, sends[r], cotangent, gt, 2 + r)
    return (
        mixed,
        gt,
        outer_sums[0],
        outer_sums[1],
        gwi,
        inner_sums[0],
        inner_sums[1],
        inner_sums[2],
        gcw,
        inner_sums[3],
        inner_sums[4],
        inner_sums[5],
        gwo,
        outer_sums[2],
    )


def solution(mesh):
    in_specs = (
        P(None, None, "seq"),
        P(None, "seq"),
        P(None, "ch", "seq"),
        P(),
        P(),
        P("ch", None),
        P("ch"),
        P("ch"),
        P("ch"),
        P(None, "ch", None),
        P("ch"),
        P("ch"),
        P("ch"),
        P("ch", None),
        P("ch"),
    )
    out_specs = (
        P(None, "ch", "seq"),
        P(None, "ch", "seq"),
        P("ch"),
        P("ch"),
        P("ch", None),
        P("ch"),
        P("ch"),
        P("ch"),
        P(None, "ch", None),
        P("ch"),
        P("ch"),
        P("ch"),
        P("ch", None),
        P("ch"),
    )
    return jax.shard_map(body, mesh=mesh, in_specs=in_specs, out_specs=out_specs, check_vma=False)
```

time: 411 us -> 350 us (0.85)
  Pallas kernels: 353 us -> 284 us
  local copies, waits for them, and re-layouts: 29.5 us -> 34 us
    pallas_call x7 -> x6, Pallas kernels: 297 us -> 228 us  [the longest x1 106 us: tail_call(): pl.pallas_call(functools.partial(tail_kernel, (stages, starts, half_rows)...]
    unnamed x30 -> x17, local copies, waits for them, and re-layouts: 0.87 us -> 5.34 us
  transfers between devices with their start and end apart: 8 -> 8, of which waited for: 0 -> 0; matrix products, arithmetic and copies ran while one was open for 7% -> 9% of each run, Pallas kernels for 70% -> 63%
where the time goes in v3:
time: 350 us; the launch traced here: 349 us
  Pallas kernels  284 us (81%)
  local copies, waits for them, and re-layouts  34 us (10%)
  starting transfers between devices  16.9 us (5%)
  other arithmetic  13.2 us (4%)
    pallas_call x1, Pallas kernels, tail_call(): pl.pallas_call(functools.partial(tail_kernel, (stages, starts, half_rows)...  106 us
    pallas_call x1, Pallas kernels, front_call(): call(functools.partial(front_kernel, group, chs), (count // TWO,), [own,...  53.5 us
    pallas_call x1, Pallas kernels, first_call(): pl.pallas_call(lambda *refs: first_kernel(True, None, *refs), grid=(seqs,...  38.8 us
    pallas_call x2, Pallas kernels, middle_call(): call(functools.partial(middle_kernel, group, keep), (count // TWO,), [pl....  26.1 us
    pallas_call x1, Pallas kernels, last_call(): call(functools.partial(last_kernel, group, keep), (count // TWO,), in_spe...  24.4 us
    pallas_call x1, Pallas kernels, rear_call(): call(functools.partial(rear_kernel, group, chs), (count // TWO,), [pl.Blo...  18.4 us
    ppermute x6, starting transfers between devices, shift(): return lax.ppermute(value, 'seq', pairs)  14.8 us
    pallas_call x1, Pallas kernels, turn_call(): call(turn_kernel, (KERNEL,), [pl.BlockSpec((1, INNER, INNER), lambda k, p...  9.36 us
  transfers between devices with their start and end apart: 8, of which 0 were waited for; matrix products, arithmetic and copies ran while one was open for 9% of the time, Pallas kernels for 63%

profile of v3, /device:TPU:0, one launch (start us, length us, event | category | flops | bytes accessed | tf_op | source)
XLA Modules:
  0.0 349.0 jit_solution(16428081009620535794)
XLA Ops:
  6.2 3.5 constant_dynamic-slice_fusion
  10.3 1.5 broadcast_in_dim.27.refs_1_.refs_13_
  11.7 38.8 %shard_map.254 = (bf16[16,1280,256]{2,1,0:T(8,128)(2,1)}, f32[16,2,256]{2,1,0:T(2,128)}, bf16[640,1280]{1,0:T(8,128)(2,1)}, bf16[5,640,640]{2,1,0:T(8,128)(2,1)}...) custom-call(bf16[16,1280,256]{2,1,0:T(8,128)(2,1)} %x_ref.3, f32[2,1280,128]{2,1,0:T(8,128)} %broadcast_in_dim.27.refs_1_.refs_13_, ...), custom_call_target="tpu_custom_call" | custom-call | flops 419430400 | bytes 20971520 | tf_op jit(solution)/shard_map/pallas_call | solution.py:267
  53.4 1.3 broadcast_in_dim.28.p_ref
  54.6 14.3 %shard_map.257 = (bf16[8,640,256]{2,1,0:T(8,128)(2,1)}, bf16[2,640,128]{2,1,0:T(8,128)(2,1)}, bf16[2,640,128]{2,1,0:T(8,128)(2,1)}, bf16[8,640,256]{2,1,0:T(8,12...) custom-call(s32[3]{0:T(128)} %pad_add_fusion.pre, bf16[16,1280,256]{2,1,0:T(8,128)(2,1)} %get-tuple-element.56.first_ref, ...), custom_call_target="tpu_custom_call" | custom-call | flops 5033164800 | bytes 13107200 | tf_op jit(solution)/shard_map/pallas_call | solution.py:344
  68.9 2.7 collective-permute-start.2
  71.6 1.5 collective-permute-start.3
  74.1 1.3 copy.34
  76.4 9.4 %shard_map.256 = (bf16[640,3200]{1,0:T(8,128)(2,1)}, bf16[640,3200]{1,0:T(8,128)(2,1)}) custom-call(s32[3]{0:T(128)} %pad_add_fusion.pre, bf16[5,640,640]{2,1,0:T(8,128)(2,1)} %get-tuple-element.62.w_ref), custom_call_target="tpu_custom_call" | custom-call | flops 2621440000 | bytes 12288000 | tf_op jit(solution)/shard_map/pallas_call | solution.py:714
  86.7 1.3 broadcast_in_dim.29.p_ref
  88.0 24.4 %shard_map.258 = (bf16[16,640,256]{2,1,0:T(8,128)(2,1)}, bf16[8,640,256]{2,1,0:T(8,128)(2,1)}, f32[8,640,256]{2,1,0:T(8,128)}, f32[8,1,256]{2,1,0:T(1,128)}, bf16[8,640,256]{2,1,0:T(8,128)(2,1)}) custom-call(s32[3]{0:T(128)} %pad_add_fusion.pre, bf16[8,640,256]{2,1,0:T(8,128)(2,1)} %get-tuple-element.65.mid_ref.refs_3_, ...), custom_call_target="tpu_custom_call" | custom-call | flops 13086228480 | bytes 15728640 | tf_op jit(solution)/shard_map/pallas_call | solution.py:451
  113.2 18.4 %shard_map.259 = (bf16[8,640,256]{2,1,0:T(8,128)(2,1)}, bf16[2,640,128]{2,1,0:T(8,128)(2,1)}, bf16[2,640,128]{2,1,0:T(8,128)(2,1)}, f32[640,128]{1,0:T(8,128)}, ...) custom-call(s32[3]{0:T(128)} %pad_add_fusion.pre, ...), custom_call_target="tpu_custom_call" | custom-call | flops 8388608000 | bytes 13107200 | tf_op jit(solution)/shard_map/pallas_call | solution.py:538
  131.6 3.8 %collective-permute-start.5 = (bf16[2,640,128]{2,1,0:T(8,128)(2,1)}, bf16[2,640,128]{2,1,0:T(8,128)(2,1)}, u32[]{:S(2)}, u32[]{:S(2)}) collective-permute-start(bf16[2,640,128]{2,1,0:T(8,128)(2,1)} %get-tuple-element.76), channel_id=1, source_target_pairs={{0,2},{2,4},{4,6},{6,8},{8,10},{10,12},{12,14},{14,16},{16,18},{18... | collective-permute-start | bytes 983048 | tf_op jit(solution)/shard_map/ppermute | solution.py:971
  135.4 1.4 collective-permute-start.6
  136.9 11.8 %shard_map.255 = (bf16[8,640,256]{2,1,0:T(8,128)(2,1)}, bf16[2,640,128]{2,1,0:T(8,128)(2,1)}, bf16[2,640,128]{2,1,0:T(8,128)(2,1)}) custom-call(s32[3]{0:T(128)} %pad_add_fusion.pre, bf16[16,1280,256]{2,1,0:T(8,128)(2,1)} %get-tuple-element.56.first_ref, s32[16,1,256]{2,1,0:T(1,128)} %reshape.82.mask_ref, bf16[640,1280]{1,0:T(8,128)(2,1)} %get-tuple-element.57.w_ref, ...), custom_call_target="tpu_custom_call" | custom-call | flops 5033164800 | bytes 13107200 | tf_op jit(solution)/shard_map/pallas_call | solution.py:344
  148.7 3.9 %collective-permute-start = (bf16[2,640,128]{2,1,0:T(8,128)(2,1)}, bf16[2,640,128]{2,1,0:T(8,128)(2,1)}, u32[]{:S(2)}, u32[]{:S(2)}) collective-permute-start(bf16[2,640,128]{2,1,0:T(8,128)(2,1)} %get-tuple-element.60), channel_id=1, source_target_pairs={{0,2},{2,4},{4,6},{6,8},{8,10},{10,12},{12,14},{14,16},{16,18},{18... | collective-permute-start | bytes 983048 | tf_op jit(solution)/shard_map/ppermute | solution.py:971
  152.6 1.5 collective-permute-start.1
  154.1 2.2 copy.36
  158.4 53.5 %shard_map.260 = (f32[16,640,256]{2,1,0:T(8,128)}, bf16[8,640,256]{2,1,0:T(8,128)(2,1)}, f32[3200,640]{1,0:T(8,128)}, f32[640,1280]{1,0:T(8,128)}, f32[640,128]{...) custom-call(s32[3]{0:T(128)} %pad_add_fusion.pre, ...), custom_call_target="tpu_custom_call" | custom-call | flops 30534533120 | bytes 41943040 | tf_op jit(solution)/shard_map/pallas_call | solution.py:637
  211.9 1.1 reduce_sum.81
  213.1 1.1 reduce_sum.82
  214.3 1.1 reduce_sum.83
  215.7 1.3 reduce_sum.87
  217.0 1.3 reduce_sum.88
  218.4 1.5 collective-permute-start.7
  220.6 105.5 %shard_map.261 = (bf16[16,640,256]{2,1,0:T(8,128)(2,1)}, bf16[3072,640]{1,0:T(8,128)(2,1)}) custom-call(bf16[8,640,256]{2,1,0:T(8,128)(2,1)} %get-tuple-element.59.mid_ref, bf16[2,640,128]{2,1,0:T(8,128)(2,1)} %collective-permute-done.before_ref, bf16[2,640,128]{2,1,0:T(8,128)(2,1)} %collective-permute-done.1.after_ref, ...), custom_call_target="tpu_custom_call", output_to_operand_aliasing={{0}: (8, {})} | custom-call | flops 40265318400 | bytes 23592960 | tf_op jit(solution)/shard_map/pallas_call | solution.py:919
  326.2 1.8 slice.103
  328.8 2.2 convert.2
  332.3 1.5 fusion
  333.8 1.9 maximum_convert_fusion
  335.7 7.9 %shard_map.262 = f32[16,640,256]{2,1,0:T(8,128)} custom-call(s32[3]{0:T(128)} %pad_add_fusion.pre, bf16[8,640,256]{2,1,0:T(8,128)(2,1)} %collective-permute-done.7.part_ref, bf16[16,640,256]{2,1,0:T(8,128)(2,1)} %dy_ref.1, f32[16,640,256]{2,1,0:T(8,128)} %get-tuple-element.96._), custom_call_target="tpu_custom_call", output_to_operand_aliasing={{}: (3, {})} | custom-call | flops 2621440 | bytes 10485760 | tf_op jit(solution)/shard_map/pallas_call | solution.py:686
  343.7 5.3 %copy.40 = bf16[16,640,256]{2,1,0:T(8,128)(2,1)} copy(bf16[16,640,256]{2,1,0:T(8,128)(2,1)} %get-tuple-element.133) | data formatting | bytes 10485760
  (72 shorter events, 18.0 us)
Async XLA Ops:
  11.7 39.5 %copy-start.6 = (s32[16,256]{1,0:T(8,128)S(1)}, s32[16,256]{1,0:T(8,128)}, u32[]{:S(2)}) copy-start(s32[16,256]{1,0:T(8,128)} %param.16) | copy-start | bytes 49156
  50.5 61.8 %collective-permute-start.4 = (bf16[8,640,256]{2,1,0:T(8,128)(2,1)}, bf16[8,640,256]{2,1,0:T(8,128)(2,1)}, u32[]{:S(2)}, u32[]{:S(2)}) collective-permute-start(bf16[8,640,256]{2,1,0:T(8,128)(2,1)} %constant_dynamic-slice_fusion), channel_id=1, source_target_pairs={{0,1},{1,0},{2,3},{3,2},{4,5},{5,4},{6,7},{7,6},{8,9},{9,8},{10,11... | collective-permute-start | bytes 7864328 | tf_op jit(solution)/shard_map/ppermute | solution.py:965
  54.6 19.5 %copy-start.1 = (bf16[640,1280]{1,0:T(8,128)(2,1)S(1)}, bf16[640,1280]{1,0:T(8,128)(2,1)}, u32[]{:S(2)}) copy-start(bf16[640,1280]{1,0:T(8,128)(2,1)} %get-tuple-element.64.refs_2_) | copy-start | bytes 4915204
  68.9 16.9 %collective-permute-start.2 = (bf16[2,640,128]{2,1,0:T(8,128)(2,1)}, bf16[2,640,128]{2,1,0:T(8,128)(2,1)}, u32[]{:S(2)}, u32[]{:S(2)}) collective-permute-start(bf16[2,640,128]{2,1,0:T(8,128)(2,1)} %get-tuple-element.66), channel_id=1, source_target_pairs={{0,2},{2,4},{4,6},{6,8},{8,10},{10,12},{12,14},{14,16},{16,18},{18... | collective-permute-start | bytes 983048 | tf_op jit(solution)/shard_map/ppermute | solution.py:971
  71.6 14.1 %collective-permute-start.3 = (bf16[2,640,128]{2,1,0:T(8,128)(2,1)}, bf16[2,640,128]{2,1,0:T(8,128)(2,1)}, u32[]{:S(2)}, u32[]{:S(2)}) collective-permute-start(bf16[2,640,128]{2,1,0:T(8,128)(2,1)} %get-tuple-element.67), channel_id=1, source_target_pairs={{2,0},{4,2},{6,4},{8,6},{10,8},{12,10},{14,12},{16,14},{18,16},{20... | collective-permute-start | bytes 983048 | tf_op jit(solution)/shard_map/ppermute | solution.py:971
  76.4 9.4 %copy-start.7 = (f32[640]{0:T(1024)S(1)}, f32[640]{0:T(1024)}, u32[]{:S(2)}) copy-start(f32[640]{0:T(1024)} %param.29) | copy-start | bytes 7684
  131.6 25.9 %collective-permute-start.5 = (bf16[2,640,128]{2,1,0:T(8,128)(2,1)}, bf16[2,640,128]{2,1,0:T(8,128)(2,1)}, u32[]{:S(2)}, u32[]{:S(2)}) collective-permute-start(bf16[2,640,128]{2,1,0:T(8,128)(2,1)} %get-tuple-element.76), channel_id=1, source_target_pairs={{0,2},{2,4},{4,6},{6,8},{8,10},{10,12},{12,14},{14,16},{16,18},{18... | collective-permute-start | bytes 983048 | tf_op jit(solution)/shard_map/ppermute | solution.py:971
  135.4 18.7 %copy-start = (bf16[640,1280]{1,0:T(8,128)(2,1)S(1)}, bf16[640,1280]{1,0:T(8,128)(2,1)}, u32[]{:S(2)}) copy-start(bf16[640,1280]{1,0:T(8,128)(2,1)} %get-tuple-element.57.w_ref) | copy-start | bytes 4915204
  135.4 22.1 %collective-permute-start.6 = (bf16[2,640,128]{2,1,0:T(8,128)(2,1)}, bf16[2,640,128]{2,1,0:T(8,128)(2,1)}, u32[]{:S(2)}, u32[]{:S(2)}) collective-permute-start(bf16[2,640,128]{2,1,0:T(8,128)(2,1)} %get-tuple-element.77), channel_id=1, source_target_pairs={{2,0},{4,2},{6,4},{8,6},{10,8},{12,10},{14,12},{16,14},{18,16},{20... | collective-permute-start | bytes 983048 | tf_op jit(solution)/shard_map/ppermute | solution.py:971
  148.7 7.8 %copy-start.5 = (f32[640,128]{1,0:T(8,128)S(1)}, f32[640,128]{1,0:T(8,128)}, u32[]{:S(2)}) copy-start(f32[640,128]{1,0:T(8,128)} %get-tuple-element.88) | copy-start | bytes 983044
  148.7 8.0 %copy-start.4 = (f32[640,128]{1,0:T(8,128)S(1)}, f32[640,128]{1,0:T(8,128)}, u32[]{:S(2)}) copy-start(f32[640,128]{1,0:T(8,128)} %get-tuple-element.89) | copy-start | bytes 983044
  148.7 8.3 %copy-start.3 = (f32[640,128]{1,0:T(8,128)S(1)}, f32[640,128]{1,0:T(8,128)}, u32[]{:S(2)}) copy-start(f32[640,128]{1,0:T(8,128)} %get-tuple-element.90) | copy-start | bytes 983044
  148.7 8.5 %copy-start.2 = (f32[1280,128]{1,0:T(8,128)S(1)}, f32[1280,128]{1,0:T(8,128)}, u32[]{:S(2)}) copy-start(f32[1280,128]{1,0:T(8,128)} %get-tuple-element.93) | copy-start | bytes 1966084
  148.7 71.9 %collective-permute-start = (bf16[2,640,128]{2,1,0:T(8,128)(2,1)}, bf16[2,640,128]{2,1,0:T(8,128)(2,1)}, u32[]{:S(2)}, u32[]{:S(2)}) collective-permute-start(bf16[2,640,128]{2,1,0:T(8,128)(2,1)} %get-tuple-element.60), channel_id=1, source_target_pairs={{0,2},{2,4},{4,6},{6,8},{8,10},{10,12},{12,14},{14,16},{16,18},{18... | collective-permute-start | bytes 983048 | tf_op jit(solution)/shard_map/ppermute | solution.py:971
  152.6 68.0 %collective-permute-start.1 = (bf16[2,640,128]{2,1,0:T(8,128)(2,1)}, bf16[2,640,128]{2,1,0:T(8,128)(2,1)}, u32[]{:S(2)}, u32[]{:S(2)}) collective-permute-start(bf16[2,640,128]{2,1,0:T(8,128)(2,1)} %get-tuple-element.61), channel_id=1, source_target_pairs={{2,0},{4,2},{6,4},{8,6},{10,8},{12,10},{14,12},{16,14},{18,16},{20... | collective-permute-start | bytes 983048 | tf_op jit(solution)/shard_map/ppermute | solution.py:971
  218.4 117.3 %collective-permute-start.7 = (bf16[8,640,256]{2,1,0:T(8,128)(2,1)}, bf16[8,640,256]{2,1,0:T(8,128)(2,1)}, u32[]{:S(2)}, u32[]{:S(2)}) collective-permute-start(bf16[8,640,256]{2,1,0:T(8,128)(2,1)} %get-tuple-element.95), channel_id=1, source_target_pairs={{0,1},{1,0},{2,3},{3,2},{4,5},{5,4},{6,7},{7,6},{8,9},{9,8},{10,11... | collective-permute-start | bytes 7864328 | tf_op jit(solution)/shard_map/ppermute | solution.py:965

commit v4 on v3

--- a/solution.py
+++ b/solution.py
@@ -105,8 +105,8 @@
     return pl.CostEstimate(flops=int(2 * macs), bytes_accessed=int(bytes_accessed), transcendentals=0)
 
 
-def whole(shape):
-    return pl.BlockSpec(shape, lambda i, pre: (0,) * len(shape), pipeline_mode=pl.Buffered(1))
+def whole(shape, at=0):
+    return pl.BlockSpec(shape, lambda i, pre: (at,) + (0,) * (len(shape) - 1), pipeline_mode=pl.Buffered(1))
 
 
 def sds(shape, dtype):
@@ -161,9 +161,14 @@
 
 def first_kernel(comm, pre, x_ref, p_ref, *rest):
     if comm:
-        own_refs, own_vec, first_ref, stat_ref = rest[:3], rest[3], rest[4], rest[5]
-        full_refs, full_vec = rest[6:9], rest[9]
-        exchange(own_refs, own_vec, full_refs, full_vec, rest[10:12], rest[12:])
+        own_refs, own_vec, cot_ref, first_ref, stat_ref = rest[:3], rest[3], rest[4], rest[5], rest[6]
+        full_refs, full_vec, away_ref = rest[7:10], rest[10], rest[11]
+        exchange(own_refs, own_vec, full_refs, full_vec, rest[12:14], rest[14:])
+
+        @pl.when(pl.program_id(0) < pl.num_programs(0) // 2)
+        def _():
+            away_ref[...] = cot_ref[...]
+
     else:
         first_ref, stat_ref = rest
     length = x_ref.shape[2]
@@ -236,7 +241,7 @@
             third_hop[k][1].wait()
 
 
-def first_call(pre, tokens, p1, weights, vec):
+def first_call(pre, tokens, p1, weights, vec, cot=None):
     seqs, _, length = tokens.shape
     comm = weights is not None
     any_spec = pl.BlockSpec(memory_space=pl.ANY)
@@ -264,6 +269,14 @@
         def at(i):
             return ((lax.axis_index("ch") * (seqs // 2) + i) % seqs, 0, 0)
 
+        n, share = seqs // 2, cot.shape[1]
+
+        def away(i):
+            return ((1 - lax.axis_index("ch")) * n + jnp.minimum(i, n - 1), 0, 0)
+
+        shapes.append(sds((n, share, length), BF16))
+        args.append(cot)
+
         return pl.pallas_call(
             lambda *refs: first_kernel(True, None, *refs),
             grid=(seqs,),
@@ -271,10 +284,12 @@
                 pl.BlockSpec((1, D, length), at),
                 pl.BlockSpec((2, D, LANES), lambda i: (0, 0, 0), pipeline_mode=pl.Buffered(1)),
             ]
-            + [any_spec] * 4,
+            + [any_spec] * 4
+            + [pl.BlockSpec((1, share, length), away)],
             out_specs=tuple(
                 [pl.BlockSpec((1, D, length), lambda i: (i, 0, 0)), pl.BlockSpec((1, 2, length), lambda i: (i, 0, 0))]
                 + [any_spec] * 4
+                + [pl.BlockSpec((1, share, length), lambda i: (jnp.minimum(i, n - 1), 0, 0))]
             ),
             out_shape=tuple(shapes),
             scratch_shapes=scratch,
@@ -357,19 +372,19 @@
     )(pre, first, mask.reshape(seqs, 1, length), w_in, p2)
 
 
-def gather_windows(group, body_ref, before_ref, after_ref, pad_ref, cat_refs, order):
-    width, length = body_ref.shape[1], body_ref.shape[2]
-    place = pl.program_id(0) % (group // TWO)
-    for k in range(group // TWO):
+def gather_windows(group, body_ref, before_ref, after_ref, pad_ref, cat_refs, order, step=None):
+    width, length, count = body_ref.shape[1], body_ref.shape[2], len(cat_refs)
+    place = (pl.program_id(0) if step is None else step) % (group // count)
+    for k in range(group // count):
 
         @pl.when(place == k)
         def _():
-            for j in range(TWO):
-                lanes = slice((k * TWO + j) * REACH, (k * TWO + j + 1) * REACH)
+            for j in range(count):
+                lanes = slice((k * count + j) * REACH, (k * count + j + 1) * REACH)
                 pad_ref[j, :, LANES - REACH : LANES] = before_ref[0, :, lanes]
                 pad_ref[j, :, LANES + length : LANES + length + REACH] = after_ref[0, :, lanes]
 
-    for j in range(TWO):
+    for j in range(count):
         pad_ref[j, :, LANES : LANES + length] = body_ref[j]
         for tap in range(KERNEL):
             start = LANES + order * (tap - KERNEL // 2) * DILATION
@@ -431,7 +446,7 @@
         pl.BlockSpec((TWO, share, length), lambda i, pre: (pair_at(i, pre), pre[1], 0)),
         whole((INNER, KERNEL * INNER)),
         whole((share, INNER)),
-        whole((3, INNER, LANES)),
+        whole((3, INNER, LANES), 1),
         whole((share, LANES)),
     ]
     args = [pre, mid, before, after, tokens, wc, wo_t, p2, b_out]
@@ -461,11 +476,18 @@
 
 
 def side(ref, sl):
-    return jnp.concatenate([ref[j, sl, :].astype(F32) for j in range(TWO)], axis=1)
+    return jnp.concatenate([ref[j, sl, :].astype(F32) for j in range(ref.shape[0])], axis=1)
 
 
 def across(ref, row):
-    return jnp.concatenate([ref[j, row : row + 1, :] for j in range(TWO)], axis=1)
+    return jnp.concatenate([ref[j, row : row + 1, :] for j in range(ref.shape[0])], axis=1)
+
+
+def row_sums(ref):
+    ones = jnp.ones((8, LANES), F32)
+    return lax.dot_general(
+        ones, ref[...], (((1,), (1,)), ((), ())), precision=lax.Precision.HIGHEST, preferred_element_type=F32
+    )
 
 
 def norm_back(d_ref, gp_ref, hat_ref, scale, gain_ref, gg_ref, gb_ref, sum_ref, put):
@@ -498,7 +520,7 @@
     dy_refs = refs[:chs]
     w_ref, hat_ref, gp_ref, last_ref, scale_ref, p_ref = refs[chs : chs + 6]
     dconv_ref, lead_ref, trail_ref, gg_ref, gb_ref, gc_ref, gw_ref, go_ref = refs[chs + 6 : chs + 14]
-    dy_ref, d_ref = refs[chs + 14 :]
+    rows_ref, dy_ref, d_ref = refs[chs + 14 :]
     share, length = dy_refs[0].shape[1], dy_refs[0].shape[2]
 
     @pl.when(pl.program_id(0) == 0)
@@ -522,6 +544,12 @@
     norm_back(d_ref, gp_ref, hat_ref, across(scale_ref, 0), p_ref, gg_ref, gb_ref, gc_ref, put)
     put_edges(group, dconv_ref, lead_ref, trail_ref)
 
+    @pl.when(pl.program_id(0) == pl.num_programs(0) - 1)
+    def _():
+        for k, ref in enumerate((gc_ref, gg_ref, gb_ref)):
+            rows_ref[:, k * INNER : (k + 1) * INNER] = row_sums(ref)
+        rows_ref[:, 3 * INNER :] = row_sums(go_ref)
+
 
 def const(shape):
     return pl.BlockSpec(shape, lambda i, pre: (0,) * len(shape), pipeline_mode=pl.Buffered(1))
@@ -534,7 +562,7 @@
     edge = pl.BlockSpec((1, INNER, group * REACH), lambda i, pre: (i // (group // TWO), 0, 0))
     edge_shape = sds((count // group, INNER, group * REACH), BF16)
     own = pl.BlockSpec((TWO, INNER, length), lambda i, pre: (i, 0, 0))
-    sums = [(INNER, LANES)] * 3 + [(INNER, D), (D, LANES)]
+    sums = [(INNER, LANES)] * 3 + [(INNER, D), (D, LANES), (8, 3 * INNER + D)]
     return call(
         functools.partial(rear_kernel, group, chs),
         (count // TWO,),
@@ -546,7 +574,7 @@
             own,
             own,
             pl.BlockSpec((TWO, 1, length), lambda i, pre: (i, 0, 0)),
-            whole((1, INNER, LANES)),
+            whole((1, INNER, LANES), 4),
         ],
         tuple([own, edge, edge] + [const(v) for v in sums]),
         tuple([sds((count, INNER, length), BF16), edge_shape, edge_shape] + [sds(v, F32) for v in sums]),
@@ -650,7 +678,7 @@
             seq_block(share),
             whole((INNER, KERNEL * INNER)),
             whole((D, INNER)),
-            whole((1, INNER, LANES)),
+            whole((1, INNER, LANES), 1),
             whole((2, D, LANES)),
         ],
         tuple(
@@ -721,244 +749,512 @@
     )(pre, conv)
 
 
-def reduce_ticks(stages, starts, half_rows, refs):
-    gcw_ref, gwi_ref, gwo_ref, small_ref, out_ref = refs[:5]
-    acc, send, recv, swap, res, load_sem, send_sem, recv_sem = refs[5:]
+ORDERS = ((0, 1, 2, 3), (0, 1, 2, 3), (0, 2, 3, 1), (0, 2, 3, 1), (0, 1, 2, 3))
+GIVE = 5
+SCHEDULE = {
+    1: [(2, 0)],
+    2: [(0, 0), (2, 1)],
+    3: [(0, 1)],
+    6: [(2, 2)],
+    9: [(5, 0), (3, 0), (0, 2), (1, 0)],
+    10: [(3, 1), (1, 1), (2, 3), (5, 1)],
+    13: [(0, 3), (2, 4)],
+    14: [(5, 2)],
+    15: [(3, 2), (1, 2)],
+    16: [(5, 3), (4, 0), (2, 5)],
+    17: [(4, 1), (2, 6), (3, 3), (4, 2), (0, 4), (5, 4), (1, 3), (2, 7)],
+    19: [(4, 3), (3, 4), (0, 5), (1, 4), (5, 5), (3, 5), (1, 5)],
+    20: [(0, 6)],
+    21: [(1, 6), (4, 4), (3, 6), (5, 6), (2, 8), (4, 5), (0, 7)],
+    22: [(4, 6), (1, 7), (4, 7), (3, 7), (0, 8), (5, 7)],
+    23: [(4, 8), (1, 8), (3, 8), (2, 9)],
+    24: [(3, 9), (4, 9), (1, 9), (5, 8), (0, 9)],
+}
+
+
+class Stream:
+    def __init__(self, order, first, rows, arrays, slot):
+        self.order, self.rows = order, rows
+        self.acc, self.send, self.recv, self.swap, self.res, self.sems = arrays
+        self.slot = slot
+        self.levels = len(order)
+        self.size = [rows >> (t + 1) for t in range(self.levels)]
+        self.at = [rows - (rows >> t) for t in range(self.levels)]
+        self.seq, self.ch = lax.axis_index("seq"), lax.axis_index("ch")
+        self.low = [first]
+        for t in range(self.levels):
+            self.low.append(self.low[-1] + self.bit(order[t]) * self.size[t])
+
+    def bit(self, b):
+        return (self.seq // (1 << b)) % 2
+
+    def partner(self, b):
+        return {"seq": self.seq + (1 - 2 * self.bit(b)) * (1 << b)}
+
+    def remote(self, src, dst, k, device):
+        return pltpu.make_async_remote_copy(
+            src_ref=src,
+            dst_ref=dst,
+            send_sem=self.sems[0].at[self.slot, k],
+            recv_sem=self.sems[1].at[self.slot, k],
+            device_id=device,
+            device_id_type=pl.DeviceIdType.MESH,
+        )
+
+    def copy(self, k):
+        if k < self.levels:
+            window = pl.ds(self.at[k], self.size[k])
+            held = self.send.at[:, pl.ds(0, self.size[k]), :]
+            return self.remote(held, self.recv.at[:, window, :], k, self.partner(self.order[k]))
+        if k == self.levels:
+            return self.remote(self.swap.at[0], self.swap.at[1], k, {"ch": 1 - self.ch})
+        t = 2 * self.levels - k
+        place = spot(self.low[t + 1], 0, self.size[t])
+        return self.remote(self.res.at[place, :], self.res.at[place, :], k, self.partner(self.order[t]))
+
+    def start(self, k):
+        if k < self.levels:
+            away = self.low[k] + (1 - self.bit(self.order[k])) * self.size[k]
+            for h in range(2):
+
+                def pack(i, step, h=h):
+                    self.send[h, spot(0, i, step), :] = self.acc[h, spot(away, i, step), :].astype(BF16)
+
+                sliced(self.size[k], pack)
+        elif k == self.levels:
+            place = spot(self.low[-1], 0, self.size[-1])
+            self.swap[0] = self.acc[1 - self.ch, place, :].astype(BF16)
+        self.copy(k).start()
+
+    def finish(self, k):
+        self.copy(k).wait()
+        if k < self.levels:
+            for h in range(2):
+
+                def add(i, step, h=h):
+                    place = spot(self.low[k + 1], i, step)
+                    self.acc[h, place, :] += self.recv[h, spot(self.at[k], i, step), :].astype(F32)
+
+                sliced(self.size[k], add)
+        elif k == self.levels:
+            place = spot(self.low[-1], 0, self.size[-1])
+            self.res[place, :] = (self.acc[self.ch, place, :] + self.swap[1].astype(F32)).astype(BF16)
+
+
+def sliced(count, body):
+    step = next(r for r in (96, 64, 48, 32, 16) if count % r == 0)
+
+    def one(i, carry):
+        body(pl.multiple_of(i * step, 16), step)
+        return carry
+
+    lax.fori_loop(0, count // step, one, 0)
+
+
+def spot(base, i, step):
+    return pl.ds(pl.multiple_of(base + i, 16), step)
+
+
+HALF = INNER // 2
+LEVELS = 4
+EARLY_ROWS = HALF * (KERNEL + D // INNER)
+ROWS = 768
+SMALL_ROWS = 256
+
+
+def stream_scratch():
+    dma = pltpu.SemaphoreType.DMA
+    out = [pltpu.VMEM((2, 4 * ROWS, INNER), F32)]
+    moved = ROWS - (ROWS >> LEVELS)
+    out += [pltpu.VMEM((2, ROWS // 2, INNER), BF16)] * 4
+    out += [pltpu.VMEM((2, moved, INNER), BF16)] * 4
+    out += [pltpu.VMEM((2, ROWS >> LEVELS, INNER), BF16)] * 4
+    out += [pltpu.VMEM((4 * ROWS, INNER), BF16)]
+    out += [
+        pltpu.VMEM((2, SMALL_ROWS, LANES), F32),
+        pltpu.VMEM((2, SMALL_ROWS // 2, LANES), BF16),
+        pltpu.VMEM((2, SMALL_ROWS - (SMALL_ROWS >> LEVELS), LANES), BF16),
+        pltpu.VMEM((2, SMALL_ROWS >> LEVELS, LANES), BF16),
+        pltpu.VMEM((SMALL_ROWS, LANES), BF16),
+    ]
+    out += [dma((2 * (KERNEL + D // INNER),)), dma((5, 2 * LEVELS + 1)), dma((5, 2 * LEVELS + 1))]
+    return out
+
+
+def streams_of(refs):
+    acc, send, recv, swap, res = refs[0], refs[1:5], refs[5:9], refs[9:13], refs[13]
+    sems = refs[20:22]
+    out = []
+    for q, order in enumerate(ORDERS[:4]):
+        out.append(Stream(order, q * ROWS, ROWS, (acc, send[q], recv[q], swap[q], res, sems), q))
+    out.append(Stream(ORDERS[4], 0, SMALL_ROWS, (*refs[14:19], sems), 4))
+    return out
+
+
+def taps_kernel(group, pre, dconv_ref, before_ref, after_ref, mid_ref, gcw_ref, pad_ref, cat_ref):
+    length = mid_ref.shape[2]
+
+    @pl.when(pl.program_id(0) == 0)
+    def _():
+        gcw_ref[...] = jnp.zeros_like(gcw_ref)
+
+    cats = [cat_ref.at[:, j * length : (j + 1) * length] for j in range(TWO)]
+    gather_windows(group, dconv_ref, before_ref, after_ref, pad_ref, cats, -1)
+    mid = jnp.concatenate([mid_ref[j] for j in range(TWO)], axis=1)
+    gcw_ref[...] += lax.dot_general(cat_ref[...], mid, (((1,), (1,)), ((), ())), preferred_element_type=F32)
+
+
+def taps_call(pre, dconv, before, after, mid, group):
+    count, _, length = dconv.shape
+    edge = pl.BlockSpec((1, INNER, group * REACH), lambda i, pre: (i // (group // TWO), 0, 0))
+    own = pl.BlockSpec((TWO, INNER, length), lambda i, pre: (i, 0, 0))
+    return call(
+        functools.partial(taps_kernel, group),
+        (count // TWO,),
+        [own, edge, edge, own],
+        const((KERNEL * INNER, INNER)),
+        sds((KERNEL * INNER, INNER), F32),
+        scratch=[
+            pltpu.VMEM((TWO, INNER, length + 2 * LANES), BF16),
+            pltpu.VMEM((KERNEL * INNER, TWO * length), BF16),
+        ],
+        cost=cost_of(count * KERNEL * INNER * INNER * length, KERNEL * INNER * INNER * 4),
+    )(pre, dconv, before, after, mid)
+
+
+def tail_kernel(group, *refs):
+    dconv_ref, before_ref, after_ref, hat_ref, gp_ref, scale_ref, keep_ref, x_ref, stat_ref = refs[:9]
+    mid_ref, before_oth, after_oth, wct_ref, wc_ref, wi_ref, p1_ref, p2_ref, rows_ref = refs[9:18]
+    gcw_ref, gwo_ref = refs[18:20]
+    mine_ref, last_ref, total_ref, small_ref, got_ref = refs[20:25]
+    stream_refs = refs[25:47]
+    pad_ref, cat_ref, d_ref, dn_ref, df_ref = refs[47:52]
+    gg2_ref, gb2_ref, gbi_ref, gg1_ref, gb1_ref, give_send, give_recv = refs[52:]
+    give_ref = dn_ref
+    acc, small_acc, res, small_res, load_sem = (stream_refs[k] for k in (0, 14, 13, 18, 19))
+    base = 3 * ROWS
+    share, length = give_ref.shape[1], give_ref.shape[2]
     seq, ch = lax.axis_index("seq"), lax.axis_index("ch")
-    streams, levels = len(stages), len(stages[0])
-    rows = acc.shape[1] // streams
-    size = [rows >> (t + 1) for t in range(levels)]
-    at = [rows - (rows >> t) for t in range(levels)]
-
-    def bit(b):
-        return (seq // (1 << b)) % 2
-
-    def partner(b):
-        return {"seq": seq + (1 - 2 * bit(b)) * (1 << b)}
-
-    low = []
-    for q in range(streams):
-        place = [q * rows]
-        for t in range(levels):
-            place.append(place[-1] + bit(stages[q][t]) * size[t])
-        low.append(place)
+    step, steps = pl.program_id(0), pl.num_programs(0)
+    count = give_ref.shape[0]
+    streams = streams_of(stream_refs)
 
     def loads():
         out = []
         for h in range(2):
-            mine = pl.ds(h * half_rows, half_rows)
+            mine = pl.ds(h * HALF, HALF)
             pieces = [gcw_ref.at[k, mine, :] for k in range(KERNEL)]
-            for ref in (gwi_ref, gwo_ref):
-                pieces += [ref.at[mine, pl.ds(j * INNER, INNER)] for j in range(D // INNER)]
+            pieces += [gwo_ref.at[mine, pl.ds(j * INNER, INNER)] for j in range(D // INNER)]
             for j, piece in enumerate(pieces):
-                out.append((piece, acc.at[h, pl.ds(j * half_rows, half_rows), :]))
-            used = len(pieces) * half_rows
-            out.append((small_ref.at[h], acc.at[h, pl.ds(used, small_ref.shape[1]), :]))
+                out.append((piece, acc.at[h, pl.ds(j * HALF, HALF), :]))
         return [pltpu.make_async_copy(a, b, load_sem.at[j]) for j, (a, b) in enumerate(out)]
 
-    def begin():
-        used = half_rows * (KERNEL + 2 * D // INNER) + small_ref.shape[1]
+    def give(i):
+        return pltpu.make_async_remote_copy(
+            src_ref=give_ref.at[i],
+            dst_ref=got_ref.at[i],
+            send_sem=give_send.at[i],
+            recv_sem=give_recv.at[i],
+            device_id={"ch": 1 - ch},
+            device_id_type=pl.DeviceIdType.MESH,
+        )
+
+    def fill_inner():
+        inner = [row_sums(ref)[0:1] for ref in (gbi_ref, gg2_ref, gb2_ref)]
+        inner += [rows_ref[0:1, k * INNER : (k + 1) * INNER] for k in range(3)]
+        at = base + HALF * D // INNER
         for h in range(2):
-            acc[h, used:, :] = jnp.zeros((acc.shape[1] - used, INNER), F32)
+            for k, v in enumerate(inner):
+                acc[h, at + k : at + k + 1, :HALF] = v[:, h * HALF : (h + 1) * HALF]
+
+    def fill_outer():
+        small_acc[...] = jnp.zeros_like(small_acc)
+        outer = [row_sums(ref)[0:1] for ref in (gg1_ref, gb1_ref)] + [rows_ref[0:1, 3 * INNER :]]
+        for h in range(2):
+            for k, v in enumerate(outer):
+                for j in range(INNER // LANES):
+                    lanes = slice(h * INNER + j * LANES, h * INNER + (j + 1) * LANES)
+                    row = k * (INNER // LANES) + j
+                    small_acc[h, row : row + 1, :] = v[:, lanes]
+
+    def act(actions):
+        for q, k in actions:
+            if q == GIVE:
+                if k > 0:
+                    give(k - 1).wait()
+                if k < count:
+                    give(k).start()
+                continue
+            if k > 0:
+                streams[q].finish(k - 1)
+            elif q == 3:
+                fill_inner()
+            elif q == 4:
+                fill_outer()
+            if k <= 2 * LEVELS:
+                streams[q].start(k)
+
+    @pl.when(step == 0)
+    def _():
+        for h in range(2):
+            acc[h, EARLY_ROWS:, :] = jnp.zeros((4 * ROWS - EARLY_ROWS, INNER), F32)
         for copy in loads():
             copy.start()
         barrier = pltpu.get_barrier_semaphore()
-        for device in [partner(b) for b in sorted(stages[0])] + [{"ch": 1 - ch}]:
+        for device in [streams[0].partner(b) for b in range(LEVELS)] + [{"ch": 1 - ch}]:
             pl.semaphore_signal(barrier, inc=1, device_id=device, device_id_type=pl.DeviceIdType.MESH)
-        pl.semaphore_wait(barrier, levels + 1)
-
-    def remote(src, dst, q, k, device):
-        slot = q * (2 * levels + 1) + k
-        return pltpu.make_async_remote_copy(
-            src_ref=src,
-            dst_ref=dst,
-            send_sem=send_sem.at[slot],
-            recv_sem=recv_sem.at[slot],
-            device_id=device,
-            device_id_type=pl.DeviceIdType.MESH,
-        )
-
-    def sliced(count, body):
-        step = next(r for r in (96, 48, 32, 16) if count % r == 0)
-
-        def one(i, carry):
-            body(pl.multiple_of(i * step, 16), step)
+        pl.semaphore_wait(barrier, LEVELS + 1)
+        for ref in (gg2_ref, gb2_ref, gbi_ref, gg1_ref, gb1_ref):
+            ref[...] = jnp.zeros_like(ref)
+
+    @pl.when(step == min(SCHEDULE))
+    def _():
+        for copy in loads():
+            copy.wait()
+
+    for at, actions in SCHEDULE.items():
+        if at < 3 * count:
+
+            @pl.when(step == at)
+            def _():
+                act(actions)
+
+    @pl.when(step < count)
+    def _():
+        gather_windows(group, dconv_ref, before_ref, after_ref, pad_ref, [cat_ref], -1, step)
+        d_ref[...] = jnp.dot(wct_ref[...], cat_ref[...], preferred_element_type=F32)
+
+        def put(sl, v):
+            dn_ref[step, sl, :] = v
+
+        norm_back(d_ref, gp_ref, hat_ref, scale_ref[0], p2_ref.at[1:2], gg2_ref, gb2_ref, gbi_ref, put)
+        for h in range(2):
+            for j in range(D // INNER):
+                part = lax.dot_general(
+                    dn_ref[step, h * HALF : (h + 1) * HALF, :],
+                    keep_ref[0, j * INNER : (j + 1) * INNER, :],
+                    (((1,), (1,)), ((), ())),
+                    preferred_element_type=F32,
+                )
+                acc[h, base + j * HALF : base + (j + 1) * HALF, :] += part
+
+    @pl.when(jnp.logical_and(step >= count, step < 2 * count))
+    def _():
+        now = step - count
+        df_ref[...] = jnp.dot(wi_ref[...], dn_ref[now], preferred_element_type=F32)
+        mean_in, scale_in = stat_ref[0, 0:1, :], stat_ref[0, 1:2, :]
+        zero = jnp.zeros((8, length), F32)
+
+        def inner(sl, carry):
+            hat = (x_ref[0, sl, :].astype(F32) - mean_in) * scale_in
+            gain = spread(p1_ref[0, sl, :], length)
+            point = hat * gain + spread(p1_ref[1, sl, :], length)
+            d_pre = df_ref[sl, :] * slope(point, cdf(point))
+            gg1_ref[sl, :] += fold_lanes(d_pre * hat)
+            gb1_ref[sl, :] += fold_lanes(d_pre)
+            e = d_pre * gain
+            df_ref[sl, :] = e
+            return carry[0] + fold_rows(e), carry[1] + fold_rows(e * hat)
+
+        total, dot = straight(D, length, inner, (zero, zero))
+        total = total.sum(0, keepdims=True) * (scale_in / D)
+        dot = dot.sum(0, keepdims=True) * (scale_in / D)
+        for r in range(2):
+            start = ((ch + r) % 2) * share
+
+            def out(to, carry):
+                rows = pl.ds(pl.multiple_of(start + to.start, 16), to.size)
+                hat = (x_ref[0, rows, :].astype(F32) - mean_in) * scale_in
+                v = (df_ref[rows, :] * scale_in - total - hat * dot).astype(BF16)
+                if r == 0:
+                    mine_ref[0, to, :] = v
+                else:
+                    give_ref[now, to, :] = v
+                return carry
+
+            straight(share, length, out, 0)
+
+    @pl.when(step >= 2 * count)
+    def _():
+        gather_windows(group, mid_ref, before_oth, after_oth, pad_ref, [cat_ref], 1, step)
+        conv = jnp.dot(wc_ref[...], cat_ref[...], preferred_element_type=F32)
+        d_ref[...] = conv + spread(p2_ref[3], length)
+        mean, scale = norm_stats(lambda sl: d_ref[sl, :], INNER, length)
+
+        def body(sl, carry):
+            hat = (d_ref[sl, :] - mean) * scale
+            point = hat * spread(p2_ref[4, sl, :], length) + spread(p2_ref[5, sl, :], length)
+            last_ref[0, sl, :] = (point * cdf(point)).astype(BF16)
             return carry
 
-        lax.fori_loop(0, count // step, one, 0)
-
-    def spot(base, i, step):
-        return pl.ds(pl.multiple_of(base + i, 16), step)
-
-    def copy_of(q, k):
-        if k < levels:
-            window = pl.ds(at[k], size[k])
-            return remote(send.at[q, :, window, :], recv.at[q, :, window, :], q, k, partner(stages[q][k]))
-        if k == levels:
-            return remote(swap.at[0, q], swap.at[1, q], q, k, {"ch": 1 - ch})
-        t = 2 * levels - k
-        place = pl.ds(pl.multiple_of(low[q][t + 1], 16), size[t])
-        return remote(res.at[place, :], res.at[place, :], q, k, partner(stages[q][t]))
-
-    def start(q, k):
-        if k < levels:
-            away = low[q][k] + (1 - bit(stages[q][k])) * size[k]
-            for h in range(2):
-
-                def pack(i, step, h=h):
-                    send[q, h, spot(at[k], i, step), :] = acc[h, spot(away, i, step), :].astype(BF16)
-
-                sliced(size[k], pack)
-        elif k == levels:
-            place = spot(low[q][levels], 0, size[-1])
-            swap[0, q] = acc[1 - ch, place, :].astype(BF16)
-        copy_of(q, k).start()
-
-    def finish(q, k):
-        copy_of(q, k).wait()
-        if k < levels:
-            for h in range(2):
-
-                def add(i, step, h=h):
-                    place = spot(low[q][k + 1], i, step)
-                    acc[h, place, :] += recv[q, h, spot(at[k], i, step), :].astype(F32)
-
-                sliced(size[k], add)
-        elif k == levels:
-            place = spot(low[q][levels], 0, size[-1])
-            res[place, :] = (acc[ch, place, :] + swap[1, q].astype(F32)).astype(BF16)
-
-    def tick(now):
-        if now == 0:
-            for copy in loads():
-                copy.wait()
-        for q in range(streams):
-            k = now - starts[q]
-            if 1 <= k <= 2 * levels + 1:
-                finish(q, k - 1)
-            if 0 <= k <= 2 * levels:
-                start(q, k)
-
-    def end():
-        done = pltpu.make_async_copy(res, out_ref, load_sem.at[0])
-        done.start()
-        done.wait()
-
-    return (
-        [begin]
-        + [functools.partial(tick, now) for now in range(max(starts) + 2 * levels + 2)]
-        + [end]
-    )
-
-
-def reduce_plan(small, seq_count):
-    half_rows = INNER // 2
-    levels = seq_count.bit_length() - 1
-    order = list(range(levels))
-    one, two = tuple(order), tuple(order[:1] + order[2:] + order[1:2])
-    stages, starts = streams_of(one, two)
-    streams = len(stages)
-    used = half_rows * (KERNEL + 2 * D // INNER) + small.shape[1]
-    unit = streams * seq_count * 16
-    rows = -(-used // unit) * unit
-    each = rows // streams
-    slots = streams * (2 * levels + 1)
-    dma = pltpu.SemaphoreType.DMA
-    scratch = [
-        pltpu.VMEM((2, rows, INNER), F32),
-        pltpu.VMEM((streams, 2, each - each // seq_count, INNER), BF16),
-        pltpu.VMEM((streams, 2, each - each // seq_count, INNER), BF16),
-        pltpu.VMEM((2, streams, each // seq_count, INNER), BF16),
-        pltpu.VMEM((rows, INNER), BF16),
-        dma((2 * (KERNEL + 2 * D // INNER + 1),)),
-        dma((slots,)),
-        dma((slots,)),
-    ]
-    return stages, starts, half_rows, rows, scratch
-
-
-def streams_of(one, two):
-    return (one, one, two, one), (0, 1, 0, 2)
-
-
-def tail_kernel(plan, group, mid_ref, before_ref, after_ref, x_ref, wc_ref, wo_ref, p_ref, b_ref, *rest):
-    mixed_in, sums, mixed_ref, total_ref = rest[0], rest[1:5], rest[5], rest[6]
-    ticks = reduce_ticks(*plan, (*sums, total_ref, *rest[7:15]))
-    step = pl.program_id(0)
-    last = 3
-    for i in range(last + 1):
-
-        @pl.when(step == i)
-        def _():
-            ticks[i]()
-
-    last_kernel(
-        group, False, None, mid_ref, before_ref, after_ref, x_ref, wc_ref, wo_ref, p_ref, b_ref,
-        mixed_in, mixed_ref, *rest[15:],
-    )
-
-    @pl.when(step == last)
+        straight(INNER, length, body, 0)
+
+    @pl.when(step == steps - 1)
     def _():
-        for tick in ticks[last + 1 :]:
-            tick()
-
-
-def tail_call(mid, before, after, tokens, wc, wo_t, p2, b_out, mixed, sums, group):
-    count, _, length = mid.shape
-    seqs, share = tokens.shape[0], wo_t.shape[0]
-    stages, starts, half_rows, rows, scratch = reduce_plan(sums[3], lax.axis_size("seq"))
+        act(SCHEDULE[max(SCHEDULE)])
+        done = [
+            pltpu.make_async_copy(res, total_ref, load_sem.at[0]),
+            pltpu.make_async_copy(small_res, small_ref, load_sem.at[1]),
+        ]
+        for copy in done:
+            copy.start()
+        for copy in done:
+            copy.wait()
+
+
+def tail_call(dconv, rims_own, hat, gp, scale, first, tokens, stat, mid, rims_oth, wc_t, wc, wi_t, p1, p2, rows, gcw, gwo, group):
+    count, _, length = dconv.shape
+    share = D // 2
     any_spec = pl.BlockSpec(memory_space=pl.ANY)
-
-    def pair_at(i):
-        return ((lax.axis_index("ch") + 1) * (seqs // 2 // TWO) + i) % (seqs // TWO)
 
     def fixed(shape):
         return pl.BlockSpec(shape, lambda i: (0,) * len(shape), pipeline_mode=pl.Buffered(1))
 
-    edge = pl.BlockSpec((1, INNER, group * REACH), lambda i: (i // (group // TWO), 0, 0))
+    def phase(k):
+        return lambda i: jnp.clip(i - k * count, 0, count - 1)
+
+    def block(k, width):
+        return pl.BlockSpec((1, width, length), lambda i: (phase(k)(i), 0, 0))
+
+    def edge(k):
+        return pl.BlockSpec((1, INNER, group * REACH), lambda i: (phase(k)(i) // group, 0, 0))
+
+    dma = pltpu.SemaphoreType.DMA
     return pl.pallas_call(
-        functools.partial(tail_kernel, (stages, starts, half_rows), group),
-        grid=(count // TWO,),
+        functools.partial(tail_kernel, group),
+        grid=(3 * count,),
         in_specs=[
-            pl.BlockSpec((TWO, INNER, length), lambda i: (i, 0, 0)),
-            edge,
-            edge,
-            pl.BlockSpec((TWO, share, length), lambda i: (pair_at(i), lax.axis_index("ch"), 0)),
-            fixed((INNER, KERNEL * INNER)),
-            fixed((share, INNER)),
-            fixed((3, INNER, LANES)),
-            fixed((share, LANES)),
-        ]
-        + [any_spec] * 5,
-        out_specs=(pl.BlockSpec((TWO, share, length), lambda i: (pair_at(i), 0, 0)), any_spec),
-        out_shape=(sds((seqs, share, length), BF16), sds((rows, INNER), BF16)),
-        scratch_shapes=scratch
-        + [pltpu.VMEM((TWO, INNER, length + 2 * LANES), BF16)]
-        + [pltpu.VMEM((KERNEL * INNER, length), BF16)] * TWO
-        + [pltpu.VMEM((INNER, length), F32)] * TWO
-        + [pltpu.VMEM((INNER, length), BF16)] * TWO,
-        input_output_aliases={8: 0},
-        cost_estimate=cost_of(count * INNER * (KERNEL * INNER + share) * length * 4, rows * INNER * 12),
-        compiler_params=pltpu.CompilerParams(vmem_limit_bytes=VMEM_BYTES, collective_id=2, has_side_effects=True),
-    )(mid, before, after, tokens, wc, wo_t, p2, b_out, mixed, *sums)
-
-
-def reduce_kernel(plan, *refs):
-    for tick in reduce_ticks(*plan, refs):
-        tick()
-
-
-def reduce_call(sums, seq_count):
-    stages, starts, half_rows, rows, scratch = reduce_plan(sums[3], seq_count)
-    any_spec = pl.BlockSpec(memory_space=pl.ANY)
-    return pl.pallas_call(
-        functools.partial(reduce_kernel, (stages, starts, half_rows)),
-        in_specs=[any_spec] * 4,
-        out_specs=any_spec,
-        out_shape=sds((rows, INNER), BF16),
-        scratch_shapes=scratch,
-        compiler_params=pltpu.CompilerParams(vmem_limit_bytes=VMEM_BYTES, collective_id=2, has_side_effects=True),
-    )(*sums)
+            block(0, INNER),
+            edge(0),
+            edge(0),
+            block(0, INNER),
+            block(0, INNER),
+            block(0, 1),
+            block(0, D),
+            pl.BlockSpec((1, D, length), lambda i: (lax.axis_index("ch") * count + phase(1)(i), 0, 0)),
+            block(1, 2),
+            block(2, INNER),
+            edge(2),
+            edge(2),
+            fixed(wc_t.shape),
+            fixed(wc.shape),
+            fixed(wi_t.shape),
+            fixed(p1.shape),
+            fixed(p2.shape),
+            fixed(rows.shape),
+            any_spec,
+            any_spec,
+        ],
+        out_specs=(block(1, share), block(2, INNER), any_spec, any_spec, any_spec),
+        out_shape=(
+            sds((count, share, length), BF16),
+            sds((count, INNER, length), BF16),
+            sds((4 * ROWS, INNER), BF16),
+            sds((SMALL_ROWS, LANES), BF16),
+            sds((count, share, length), BF16),
+        ),
+        scratch_shapes=stream_scratch()
+        + [
+            pltpu.VMEM((1, INNER, length + 2 * LANES), BF16),
+            pltpu.VMEM((KERNEL * INNER, length), BF16),
+            pltpu.VMEM((INNER, length), F32),
+            pltpu.VMEM((count, INNER, length), BF16),
+            pltpu.VMEM((D, length), F32),
+            pltpu.VMEM((INNER, LANES), F32),
+            pltpu.VMEM((INNER, LANES), F32),
+            pltpu.VMEM((INNER, LANES), F32),
+            pltpu.VMEM((D, LANES), F32),
+            pltpu.VMEM((D, LANES), F32),
+            dma((count,)),
+            dma((count,)),
+        ],
+        cost_estimate=cost_of(count * INNER * (KERNEL * INNER + D) * length * 4, 4 * ROWS * INNER * 12),
+        compiler_params=pltpu.CompilerParams(
+            vmem_limit_bytes=TAIL_BYTES, collective_id=2, has_side_effects=True
+        ),
+    )(dconv, *rims_own, hat, gp, scale, first, tokens, stat, mid, *rims_oth, wc_t, wc, wi_t, p1, p2, rows, gcw, gwo)
+
+
+TAIL_BYTES = 63 * 1024 * 1024
+
+
+def finish_kernel(pre, mine_ref, got_ref, dy_ref, last_ref, x_ref, wo_ref, b_ref, total_ref, small_ref, _, *outs):
+    gt_ref, mixed_ref, gcw_ref, gwi_ref, gwo_ref, inner_ref, outer_ref = outs
+    length = dy_ref.shape[2]
+    step, count = pl.program_id(0), pl.num_programs(0) // 2
+    part = gcw_ref.shape[1]
+
+    @pl.when(step < count)
+    def _():
+        gt_ref[...] = mine_ref[...].astype(F32) + dy_ref[...].astype(F32)
+
+    @pl.when(step >= count)
+    def _():
+        gt_ref[...] = got_ref[...].astype(F32) + dy_ref[...].astype(F32)
+        for j in range(TWO):
+            branch = jnp.dot(wo_ref[...], last_ref[j], preferred_element_type=F32)
+            mixed_ref[j] = (x_ref[j].astype(F32) + branch + spread(b_ref[...], length)).astype(BF16)
+
+    for k in range(KERNEL):
+
+        @pl.when(step == k // TWO)
+        def _():
+            gcw_ref[k] = total_ref[k * part : (k + 1) * part, :].astype(F32)
+
+    for k, (ref, start) in enumerate(((gwo_ref, KERNEL * part), (gwi_ref, 3 * ROWS))):
+
+        @pl.when(step == KERNEL // TWO + 1 + k)
+        def _():
+            for j in range(D // INNER):
+                ref[:, j * INNER : (j + 1) * INNER] = total_ref[start + j * part : start + (j + 1) * part, :].astype(F32)
+
+    @pl.when(step == 0)
+    def _():
+        at = 3 * ROWS + part * D // INNER
+        inner_ref[...] = total_ref[at : at + 16, :].astype(F32)
+        outer_ref[...] = small_ref[:16, :].astype(F32)
+
+
+def finish_call(pre, mine, got, cot, last, tokens, wo_t, b_out, total, small, mixed, part):
+    seqs, share, length = cot.shape
+    count = got.shape[0] // TWO
+    early = lambda i: jnp.minimum(i, count - 1)
+    late = lambda i: jnp.maximum(i - count, 0)
+    return call(
+        finish_kernel,
+        (2 * count,),
+        [
+            pl.BlockSpec((TWO, share, length), lambda i, pre: (early(i), 0, 0)),
+            pl.BlockSpec((TWO, share, length), lambda i, pre: (late(i), 0, 0)),
+            pl.BlockSpec((TWO, share, length), lambda i, pre: ((pre[0] // TWO + i) % (seqs // TWO), 0, 0)),
+            pl.BlockSpec((TWO, INNER, length), lambda i, pre: (late(i), 0, 0)),
+            pl.BlockSpec((TWO, share, length), lambda i, pre: (pre[2] // TWO + late(i), pre[1], 0)),
+            whole(wo_t.shape),
+            whole(b_out.shape),
+            whole(total.shape),
+            whole(small.shape),
+            pl.BlockSpec(memory_space=pl.ANY),
+        ],
+        (
+            pl.BlockSpec((TWO, share, length), lambda i, pre: ((pre[0] // TWO + i) % (seqs // TWO), 0, 0)),
+            pl.BlockSpec((TWO, share, length), lambda i, pre: (pre[2] // TWO + late(i), 0, 0)),
+            const((KERNEL, part, INNER)),
+            const((part, D)),
+            const((part, D)),
+            const((16, INNER)),
+            const((16, LANES)),
+        ),
+        (
+            sds((seqs, share, length), F32),
+            sds(mixed.shape, BF16),
+            sds((KERNEL, part, INNER), F32),
+            sds((part, D), F32),
+            sds((part, D), F32),
+            sds((16, INNER), F32),
+            sds((16, LANES), F32),
+        ),
+        aliases={10: 1},
+    )(pre, mine, got, cot, last, tokens, wo_t, b_out, total, small, mixed)
 
 
 def rotate(value, axis, count, by):
@@ -1009,15 +1305,16 @@
     group = min(4, n)
     starts = [((ch + chs - r) % chs) * n for r in range(1, chs)]
     pre = jnp.stack([ch * n, ch] + starts).astype(jnp.int32)
-    pair = chs == 2
+    pair = chs == 2 and lax.axis_size("seq") == 1 << LEVELS
 
     p1 = lane_copies(jnp.stack([ln1_gain, first_norm_bias]))
     bo = lane_copies(b_out)
     vec = jnp.stack([b_in, ln2_gain, ln2_bias, conv_b, ln3_gain, ln3_bias, b_in, b_in])
     if pair:
-        first, stat, w_in_full, conv_full, w_out_full, vec_full = first_call(
-            pre, tokens, p1, (w_in, conv_w, w_out), vec
+        first, stat, w_in_full, conv_full, w_out_full, vec_full, away = first_call(
+            pre, tokens, p1, (w_in, conv_w, w_out), vec, cotangent
         )
+        others = [rotate(away, "ch", chs, 1)]
         inner = vec_full.transpose(1, 0, 2).reshape(8, INNER)[:6]
     else:
         first, stat = first_call(pre, tokens, p1, None, None)
@@ -1025,65 +1322,51 @@
         conv_full = lax.all_gather(conv_w, "ch", axis=1, tiled=True)
         w_out_full = lax.all_gather(w_out, "ch", axis=0, tiled=True)
         inner = lax.all_gather(vec, "ch", axis=1, tiled=True)[:6]
-
-    others = []
-    for r in range(1, chs):
-        block = lax.dynamic_slice_in_dim(cotangent, ((ch + r) % chs) * n, n, 0)
-        block, _ = lax.optimization_barrier((block, stat))
-        others.append(rotate(block, "ch", chs, r))
+        others = []
+        for r in range(1, chs):
+            block = lax.dynamic_slice_in_dim(cotangent, ((ch + r) % chs) * n, n, 0)
+            others.append(rotate(block, "ch", chs, r))
+
     p2 = lane_copies(inner)
     wc, wc_t = turn_call(pre, conv_full)
     wi_t = w_in_full.T
     wo_t = lax.dynamic_slice_in_dim(w_out_full, ch * share, share, 1).T
 
     mid_own, lead, trail, hat_mid, gp_mid, scale_mid = middle_call(
-        pre, first, pad_mask, w_in_full, p2[0:3], n, 0, group, True
+        pre, first, pad_mask, w_in_full, p2, n, 0, group, True
     )
     before, after = rims(lead, trail)
-    mid_oth, lead, trail = middle_call(pre, first, pad_mask, w_in_full, p2[0:3], seqs - n, n, group, False)
+    mid_oth, lead, trail = middle_call(pre, first, pad_mask, w_in_full, p2, seqs - n, n, group, False)
     before_oth, after_oth = rims(lead, trail)
     mixed, hat_out, gp_out, scale_out, last_own = last_call(
-        pre, mid_own, before, after, tokens, wc, wo_t, p2[3:6], bo, n, 0, group, True, None
+        pre, mid_own, before, after, tokens, wc, wo_t, p2, bo, n, 0, group, True, None
     )
-    dconv, lead, trail, gg3, gb3, gcb, gwo, gbo = rear_call(
-        pre, cotangent, others, w_out_full, hat_out, gp_out, last_own, scale_out, p2[4:5], group
+    dconv, lead, trail, gg3, gb3, gcb, gwo, gbo, rows = rear_call(
+        pre, cotangent, others, w_out_full, hat_out, gp_out, last_own, scale_out, p2, group
     )
     lead, trail = rims(lead, trail)
-    gt, *rest = front_call(
-        pre, dconv, lead, trail, mid_own, hat_mid, gp_mid, scale_mid, tokens, stat, cotangent,
-        wc_t, wi_t, p2[1:2], p1, chs, group,
-    )
-    sends = [rotate(v, "ch", chs, r + 1) for r, v in enumerate(rest[: chs - 1])]
-    gcw, gwi, gg2, gb2, gbi, gg1, gb1 = rest[chs - 1 :]
-    gcw = gcw.reshape(KERNEL, INNER, INNER)
-    inner_sums = jnp.stack([v.sum(1) for v in (gbi, gg2, gb2, gcb, gg3, gb3)])
-    outer_sums = jnp.stack([v.sum(1) for v in (gg1, gb1, gbo)])
-
     if pair:
-        small = jnp.concatenate(
-            [
-                inner_sums.reshape(6, 2, part).transpose(1, 0, 2).reshape(2, 3, INNER),
-                outer_sums.reshape(3, 2, share).transpose(1, 0, 2),
-                jnp.zeros((2, 10, INNER), F32),
-            ],
-            axis=1,
+        gcw = taps_call(pre, dconv, lead, trail, mid_own, group)
+        mine, last_oth, total, small, got = tail_call(
+            dconv, (lead, trail), hat_mid, gp_mid, scale_mid, first, tokens, stat, mid_oth, (before_oth, after_oth),
+            wc_t, wc, wi_t, p1, p2, rows, gcw.reshape(KERNEL, INNER, INNER), gwo, group,
         )
-        mixed, total = tail_call(
-            mid_oth, before_oth, after_oth, tokens, wc, wo_t, p2[3:6], bo, mixed, (gcw, gwi, gwo, small), group
+        gt, mixed, gcw, gwi, gwo, inner_sums, outer_sums = finish_call(
+            pre, mine, got, cotangent, last_oth, tokens, wo_t, bo, total, small, mixed, part
         )
-        gcw = total[: KERNEL * part].reshape(KERNEL, part, INNER).astype(F32)
-        base = KERNEL * part
-        wide = []
-        for k in range(2):
-            blocks = [total[base + (2 * k + j) * part : base + (2 * k + j + 1) * part] for j in range(2)]
-            wide.append(jnp.concatenate(blocks, axis=1).astype(F32))
-        gwi, gwo = wide
-        base += 4 * part
-        inner_sums = total[base : base + 3].reshape(6, part).astype(F32)
-        outer_sums = total[base + 3 : base + 6].astype(F32)
+        inner_sums, outer_sums = inner_sums[:6, :part], outer_sums[:15].reshape(3, share)
     else:
+        gt, *rest = front_call(
+            pre, dconv, lead, trail, mid_own, hat_mid, gp_mid, scale_mid, tokens, stat, cotangent,
+            wc_t, wi_t, p2, p1, chs, group,
+        )
+        sends = [rotate(v, "ch", chs, r + 1) for r, v in enumerate(rest[: chs - 1])]
+        gcw, gwi, gg2, gb2, gbi, gg1, gb1 = rest[chs - 1 :]
+        gcw = gcw.reshape(KERNEL, INNER, INNER)
+        inner_sums = jnp.stack([v.sum(1) for v in (gbi, gg2, gb2, gcb, gg3, gb3)])
+        outer_sums = jnp.stack([v.sum(1) for v in (gg1, gb1, gbo)])
         mixed, = last_call(
-            pre, mid_oth, before_oth, after_oth, tokens, wc, wo_t, p2[3:6], bo, seqs - n, n, group, False, mixed
+            pre, mid_oth, before_oth, after_oth, tokens, wc, wo_t, p2, bo, seqs - n, n, group, False, mixed
         )
         gcw, gwi, gwo, inner_sums, outer_sums = lax.psum((gcw, gwi, gwo, inner_sums, outer_sums), ("seq", "ch"))
         gcw = own_slice(gcw, part, 1)
@@ -1091,8 +1374,8 @@
         gwo = own_slice(gwo, part, 0)
         inner_sums = own_slice(inner_sums, part, 1)
         outer_sums = own_slice(outer_sums, share, 1)
-    for r in range(chs - 1):
-        gt = add_call(pre, sends[r], cotangent, gt, 2 + r)
+        for r in range(chs - 1):
+            gt = add_call(pre, sends[r], cotangent, gt, 2 + r)
     return (
         mixed,
         gt,

time: 350 us -> 325 us (0.929)
  local copies, waits for them, and re-layouts: 34 us -> 20.7 us
  other arithmetic: 13.2 us -> 0.61 us
    reduce_sum x9 -> x0, other arithmetic: 6.87 us -> none  [the longest x6 3.97 us: body(): inner_sums = jnp.stack([v.sum(1) for v in (gbi, gg2, gb2, gcb, gg3, gb3)])]
    slice x11 -> x1, local copies, waits for them, and re-layouts: 5.89 us -> 0.75 us  [body(): inner = vec_full.transpose(1, 0, 2).reshape(8, INNER)[:6]]
    convert_element_type x3 -> x0, other arithmetic: 4.98 us -> none  [the longest x1 2.25 us: body(): gcw = total[:KERNEL * part].reshape(KERNEL, part, INNER).astype(F32)]
    unnamed x17 -> x14, local copies, waits for them, and re-layouts: 5.34 us -> 1.54 us
  transfers between devices with their start and end apart: 8 -> 7, of which waited for: 0 -> 0; matrix products, arithmetic and copies ran while one was open for 9% -> 3% of each run, Pallas kernels for 63% -> 24%
where the time goes in v4:
time: 325 us; the launch traced here: 324 us
  Pallas kernels  287 us (88%)
  local copies, waits for them, and re-layouts  20.7 us (6%)
  starting transfers between devices  14.5 us (4%)
    pallas_call x1, Pallas kernels, tail_call(): pl.pallas_call(functools.partial(tail_kernel, group), grid=(3 * count,),...  131 us
    pallas_call x1, Pallas kernels, first_call(): pl.pallas_call(lambda *refs: first_kernel(True, None, *refs), grid=(seqs,...  39 us
    pallas_call x2, Pallas kernels, middle_call(): call(functools.partial(middle_kernel, group, keep), (count // TWO,), [pl....  26.1 us
    pallas_call x1, Pallas kernels, last_call(): call(functools.partial(last_kernel, group, keep), (count // TWO,), in_spe...  24.4 us
    pallas_call x1, Pallas kernels, rear_call(): call(functools.partial(rear_kernel, group, chs), (count // TWO,), [pl.Blo...  19.9 us
    pallas_call x1, Pallas kernels, taps_call(): call(functools.partial(taps_kernel, group), (count // TWO,), [own, edge,...  18.5 us
    pallas_call x1, Pallas kernels, finish_call(): call(finish_kernel, (2 * count,), [pl.BlockSpec((TWO, share, length), lam...  18.2 us
    ppermute x6, starting transfers between devices, shift(): return lax.ppermute(value, 'seq', pairs)  13.8 us
  transfers between devices with their start and end apart: 7, of which 0 were waited for; matrix products, arithmetic and copies ran while one was open for 3% of the time, Pallas kernels for 24%

profile of v4, /device:TPU:0, one launch (start us, length us, event | category | flops | bytes accessed | tf_op | source)
XLA Modules:
  0.0 323.7 jit_solution(4966400459312525325)
XLA Ops:
  0.6 0.7 stack.51
  1.3 0.7 stack.52
  2.0 0.7 stack.53
  2.7 0.7 stack.54
  4.7 0.7 stack.48
  5.4 0.7 stack.49
  6.8 1.5 broadcast_in_dim.8.refs_1_.refs_15_
  8.3 39.0 %shard_map.254 = (bf16[16,1280,256]{2,1,0:T(8,128)(2,1)}, f32[16,2,256]{2,1,0:T(2,128)}, bf16[640,1280]{1,0:T(8,128)(2,1)}, bf16[5,640,640]{2,1,0:T(8,128)(2,1)}...) custom-call(bf16[16,1280,256]{2,1,0:T(8,128)(2,1)} %x_ref.3, ...), custom_call_target="tpu_custom_call" | custom-call | flops 419430400 | bytes 20971520 | tf_op jit(solution)/shard_map/pallas_call | solution.py:280
  48.6 0.7 copy.32
  50.0 1.9 broadcast_in_dim.10.p_ref.refs_7_.refs_16_
  51.9 14.3 %shard_map.255 = (bf16[8,640,256]{2,1,0:T(8,128)(2,1)}, bf16[2,640,128]{2,1,0:T(8,128)(2,1)}, bf16[2,640,128]{2,1,0:T(8,128)(2,1)}, bf16[8,640,256]{2,1,0:T(8,12...) custom-call(s32[3]{0:T(128)} %pad_add_fusion.pre, bf16[16,1280,256]{2,1,0:T(8,128)(2,1)} %get-tuple-element.56.first_ref.refs_6_, ...), custom_call_target="tpu_custom_call" | custom-call | flops 5033164800 | bytes 13107200 | tf_op jit(solution)/shard_map/pallas_call | solution.py:359
  66.2 2.7 collective-permute-start.1
  68.9 1.5 collective-permute-start.2
  70.4 1.3 copy.33
  71.7 1.0 dynamic-slice_bitcast_fusion.wo_ref
  72.7 9.4 %shard_map.256 = (bf16[640,3200]{1,0:T(8,128)(2,1)}, bf16[640,3200]{1,0:T(8,128)(2,1)}) custom-call(s32[3]{0:T(128)} %pad_add_fusion.pre, bf16[5,640,640]{2,1,0:T(8,128)(2,1)} %get-tuple-element.62.w_ref), custom_call_target="tpu_custom_call" | custom-call | flops 2621440000 | bytes 12288000 | tf_op jit(solution)/shard_map/pallas_call | solution.py:742
  82.1 0.9 broadcast_in_dim.11.b_ref
  83.0 24.4 %shard_map.257 = (bf16[16,640,256]{2,1,0:T(8,128)(2,1)}, bf16[8,640,256]{2,1,0:T(8,128)(2,1)}, f32[8,640,256]{2,1,0:T(8,128)}, f32[8,1,256]{2,1,0:T(1,128)}, bf16[8,640,256]{2,1,0:T(8,128)(2,1)}) custom-call(s32[3]{0:T(128)} %pad_add_fusion.pre, bf16[8,640,256]{2,1,0:T(8,128)(2,1)} %get-tuple-element.59.mid_ref, ...), custom_call_target="tpu_custom_call" | custom-call | flops 13086228480 | bytes 15728640 | tf_op jit(solution)/shard_map/pallas_call | solution.py:466
  107.4 19.9 %shard_map.258 = (bf16[8,640,256]{2,1,0:T(8,128)(2,1)}, bf16[2,640,128]{2,1,0:T(8,128)(2,1)}, bf16[2,640,128]{2,1,0:T(8,128)(2,1)}, f32[640,128]{1,0:T(8,128)}, ...) custom-call(s32[3]{0:T(128)} %pad_add_fusion.pre, ...), custom_call_target="tpu_custom_call" | custom-call | flops 8388608000 | bytes 13107200 | tf_op jit(solution)/shard_map/pallas_call | solution.py:566
  127.3 3.1 collective-permute-start.3
  130.4 1.6 collective-permute-start.4
  132.1 11.8 %shard_map.259 = (bf16[8,640,256]{2,1,0:T(8,128)(2,1)}, bf16[2,640,128]{2,1,0:T(8,128)(2,1)}, bf16[2,640,128]{2,1,0:T(8,128)(2,1)}) custom-call(s32[3]{0:T(128)} %pad_add_fusion.pre, bf16[16,1280,256]{2,1,0:T(8,128)(2,1)} %get-tuple-element.56.first_ref.refs_6_, s32[16,1,256]{2,1,0:T(1,128)} %reshape.48.mask_ref, bf16[640,1280]{1,0:T(8,128)(2,1)} %get-tuple-element.57.w_ref, ...), custom_call_target="tpu_custom_call" | custom-call | flops 5033164800 | bytes 13107200 | tf_op jit(solution)/shard_map/pallas_call | solution.py:359
  143.9 3.7 %collective-permute-start.5 = (bf16[2,640,128]{2,1,0:T(8,128)(2,1)}, bf16[2,640,128]{2,1,0:T(8,128)(2,1)S(1)}, u32[]{:S(2)}, u32[]{:S(2)}) collective-permute-start(bf16[2,640,128]{2,1,0:T(8,128)(2,1)} %get-tuple-element.76), channel_id=1, source_target_pairs={{0,2},{2,4},{4,6},{6,8},{8,10},{10,12},{12,14},{14,16},{16,18},{18... | collective-permute-start | bytes 983048 | tf_op jit(solution)/shard_map/ppermute | solution.py:1267
  147.6 1.3 collective-permute-start.6
  148.9 2.2 copy.34
  151.1 0.7 copy-done.4
  151.9 18.5 %shard_map.260 = f32[3200,640]{1,0:T(8,128)} custom-call(s32[3]{0:T(128)} %pad_add_fusion.pre, bf16[8,640,256]{2,1,0:T(8,128)(2,1)} %get-tuple-element.68.dconv_ref.refs_0_, bf16[2,640,128]{2,1,0:T(8,128)(2,1)} %copy-done.4, bf16[2,640,128]{2,1,0:T(8,128)(2,1)} %copy-done.5, bf16[8,640,256]{2,1,0:T(8,128)(2,1)} %get-tuple-element.59.mid_ref), custom_call_target="tpu_custom_call" | custom-call | flops 8388608000 | bytes 8192000 | tf_op jit(solution)/shard_map/pallas_call | solution.py:911
  170.5 0.7 copy-done.6
  171.2 131.3 %shard_map.261 = (bf16[8,640,256]{2,1,0:T(8,128)(2,1)}, bf16[8,640,256]{2,1,0:T(8,128)(2,1)}, bf16[3072,640]{1,0:T(8,128)(2,1)}, bf16[256,128]{1,0:T(8,128)(2,1)}, bf16[8,640,256]{2,1,0:T(8,128)(2,1)}) custom-call(bf16[8,640,256]{2,1,0:T(8,128)(2,1)} %get-tuple-element.68.dconv_ref.refs_0_, bf16[2,640,128]{2,1,0:T(8,128)(2,1)} %copy-done.4, ...), custom_call_target="tpu_custom_call" | custom-call | flops 46976204800 | bytes 23592960 | tf_op jit(solution)/shard_map/pallas_call | solution.py:1123
  302.5 18.2 %shard_map.262 = (f32[16,640,256]{2,1,0:T(8,128)}, bf16[16,640,256]{2,1,0:T(8,128)(2,1)}, f32[5,320,640]{2,1,0:T(8,128)}, f32[320,1280]{1,0:T(8,128)}, f32[320,1...) custom-call(s32[3]{0:T(128)} %pad_add_fusion.pre, ...), custom_call_target="tpu_custom_call", output_to_operand_aliasing={{1}: (10, {})} | custom-call | tf_op jit(solution)/shard_map/pallas_call | solution.py:1223
  320.8 1.6 slice_reduce_fusion
  322.3 1.4 slice_bitcast_fusion
  (27 shorter events, 4.1 us)
Async XLA Ops:
  8.2 39.7 %copy-start.2 = (s32[16,256]{1,0:T(8,128)S(1)}, s32[16,256]{1,0:T(8,128)}, u32[]{:S(2)}) copy-start(s32[16,256]{1,0:T(8,128)} %param.16) | copy-start | bytes 49156
  47.3 60.1 %collective-permute-start = (bf16[8,640,256]{2,1,0:T(8,128)(2,1)}, bf16[8,640,256]{2,1,0:T(8,128)(2,1)}, u32[]{:S(2)}, u32[]{:S(2)}) collective-permute-start(bf16[8,640,256]{2,1,0:T(8,128)(2,1)} %get-tuple-element.54), channel_id=1, source_target_pairs={{0,1},{1,0},{2,3},{3,2},{4,5},{5,4},{6,7},{7,6},{8,9},{9,8},{10,11... | collective-permute-start | bytes 7864328 | tf_op jit(solution)/shard_map/ppermute | solution.py:1261
  51.9 18.5 %copy-start.1 = (bf16[640,1280]{1,0:T(8,128)(2,1)S(1)}, bf16[640,1280]{1,0:T(8,128)(2,1)}, u32[]{:S(2)}) copy-start(bf16[640,1280]{1,0:T(8,128)(2,1)} %get-tuple-element.55.refs_2_) | copy-start | bytes 4915204
  66.2 15.9 %collective-permute-start.1 = (bf16[2,640,128]{2,1,0:T(8,128)(2,1)}, bf16[2,640,128]{2,1,0:T(8,128)(2,1)}, u32[]{:S(2)}, u32[]{:S(2)}) collective-permute-start(bf16[2,640,128]{2,1,0:T(8,128)(2,1)} %get-tuple-element.60), channel_id=1, source_target_pairs={{0,2},{2,4},{4,6},{6,8},{8,10},{10,12},{12,14},{14,16},{16,18},{18... | collective-permute-start | bytes 983048 | tf_op jit(solution)/shard_map/ppermute | solution.py:1267
  68.9 13.2 %collective-permute-start.2 = (bf16[2,640,128]{2,1,0:T(8,128)(2,1)}, bf16[2,640,128]{2,1,0:T(8,128)(2,1)}, u32[]{:S(2)}, u32[]{:S(2)}) collective-permute-start(bf16[2,640,128]{2,1,0:T(8,128)(2,1)} %get-tuple-element.61), channel_id=1, source_target_pairs={{2,0},{4,2},{6,4},{8,6},{10,8},{12,10},{14,12},{16,14},{18,16},{20... | collective-permute-start | bytes 983048 | tf_op jit(solution)/shard_map/ppermute | solution.py:1267
  72.7 9.4 %copy-start.3 = (f32[640]{0:T(1024)S(1)}, f32[640]{0:T(1024)}, u32[]{:S(2)}) copy-start(f32[640]{0:T(1024)} %param.29) | copy-start | bytes 7684
  127.3 23.8 %collective-permute-start.3 = (bf16[2,640,128]{2,1,0:T(8,128)(2,1)}, bf16[2,640,128]{2,1,0:T(8,128)(2,1)S(1)}, u32[]{:S(2)}, u32[]{:S(2)}) collective-permute-start(bf16[2,640,128]{2,1,0:T(8,128)(2,1)} %get-tuple-element.69), channel_id=1, source_target_pairs={{0,2},{2,4},{4,6},{6,8},{8,10},{10,12},{12,14},{14,16},{16,18},{18... | collective-permute-start | bytes 983048 | tf_op jit(solution)/shard_map/ppermute | solution.py:1267
  130.4 18.5 %copy-start = (bf16[640,1280]{1,0:T(8,128)(2,1)S(1)}, bf16[640,1280]{1,0:T(8,128)(2,1)}, u32[]{:S(2)}) copy-start(bf16[640,1280]{1,0:T(8,128)(2,1)} %get-tuple-element.57.w_ref) | copy-start | bytes 4915204
  130.4 20.7 %collective-permute-start.4 = (bf16[2,640,128]{2,1,0:T(8,128)(2,1)}, bf16[2,640,128]{2,1,0:T(8,128)(2,1)S(1)}, u32[]{:S(2)}, u32[]{:S(2)}) collective-permute-start(bf16[2,640,128]{2,1,0:T(8,128)(2,1)} %get-tuple-element.70), channel_id=1, source_target_pairs={{2,0},{4,2},{6,4},{8,6},{10,8},{12,10},{14,12},{16,14},{18,16},{20... | collective-permute-start | bytes 983048 | tf_op jit(solution)/shard_map/ppermute | solution.py:1267
  143.9 26.6 %collective-permute-start.5 = (bf16[2,640,128]{2,1,0:T(8,128)(2,1)}, bf16[2,640,128]{2,1,0:T(8,128)(2,1)S(1)}, u32[]{:S(2)}, u32[]{:S(2)}) collective-permute-start(bf16[2,640,128]{2,1,0:T(8,128)(2,1)} %get-tuple-element.76), channel_id=1, source_target_pairs={{0,2},{2,4},{4,6},{6,8},{8,10},{10,12},{12,14},{14,16},{16,18},{18... | collective-permute-start | bytes 983048 | tf_op jit(solution)/shard_map/ppermute | solution.py:1267
  147.6 22.9 %collective-permute-start.6 = (bf16[2,640,128]{2,1,0:T(8,128)(2,1)}, bf16[2,640,128]{2,1,0:T(8,128)(2,1)}, u32[]{:S(2)}, u32[]{:S(2)}) collective-permute-start(bf16[2,640,128]{2,1,0:T(8,128)(2,1)} %get-tuple-element.77), channel_id=1, source_target_pairs={{2,0},{4,2},{6,4},{8,6},{10,8},{12,10},{14,12},{16,14},{18,16},{20... | collective-permute-start | bytes 983048 | tf_op jit(solution)/shard_map/ppermute | solution.py:1267
  151.1 0.7 copy-start.4
  151.1 0.8 copy-start.5
  170.5 0.7 copy-start.6

commit v5 on v4

--- a/solution.py
+++ b/solution.py
@@ -301,6 +301,81 @@
     return call(kernel, (seqs,), in_specs, tuple(out_specs), tuple(shapes))(*args)
 
 
+class Rims:
+    def __init__(self, lead, trail, before, after, send_sem, recv_sem):
+        self.seq, self.count = lax.axis_index("seq"), lax.axis_size("seq")
+        self.before, self.after = before, after
+
+        def remote(src, dst, k, by):
+            return pltpu.make_async_remote_copy(
+                src_ref=src,
+                dst_ref=dst,
+                send_sem=send_sem.at[k],
+                recv_sem=recv_sem.at[k],
+                device_id={"seq": self.seq + by},
+                device_id_type=pl.DeviceIdType.MESH,
+            )
+
+        self.up = lambda: remote(trail, before, 0, 1)
+        self.down = lambda: remote(lead, after, 1, -1)
+        self.has_up, self.has_down = self.seq < self.count - 1, self.seq > 0
+
+    def greet(self):
+        barrier = pltpu.get_barrier_semaphore()
+        for there, by in ((self.has_up, 1), (self.has_down, -1)):
+
+            @pl.when(there)
+            def _():
+                pl.semaphore_signal(
+                    barrier, inc=1, device_id={"seq": self.seq + by}, device_id_type=pl.DeviceIdType.MESH
+                )
+        return self.has_up.astype(jnp.int32) + self.has_down.astype(jnp.int32)
+
+    def start(self):
+        pl.when(self.has_up)(lambda: self.up().start())
+        pl.when(self.has_down)(lambda: self.down().start())
+
+    def wait(self):
+        @pl.when(self.has_up)
+        def _():
+            self.up().wait_send()
+            self.down().wait_recv()
+
+        @pl.when(self.has_down)
+        def _():
+            self.down().wait_send()
+            self.up().wait_recv()
+
+
+def rim_steps(lead, trail, before, after, zeros, send_sem, recv_sem, local_sem):
+    rims = Rims(lead, trail, before, after, send_sem, recv_sem)
+    step, steps = pl.program_id(0), pl.num_programs(0)
+    ends = (
+        (jnp.logical_not(rims.has_down), lambda: pltpu.make_async_copy(zeros, before, local_sem.at[0])),
+        (jnp.logical_not(rims.has_up), lambda: pltpu.make_async_copy(zeros, after, local_sem.at[1])),
+    )
+
+    @pl.when(step == 0)
+    def _():
+        zeros[...] = jnp.zeros_like(zeros)
+        pl.semaphore_wait(pltpu.get_barrier_semaphore(), rims.greet())
+        rims.start()
+        for there, copy in ends:
+            pl.when(there)(lambda: copy().start())
+
+    def last():
+        rims.wait()
+        for there, copy in ends:
+            pl.when(there)(lambda: copy().wait())
+
+    pl.when(step == steps - 1)(last)
+
+
+def rim_scratch(shape):
+    dma = pltpu.SemaphoreType.DMA
+    return [pltpu.VMEM(shape, BF16), dma((2,)), dma((2,)), dma((2,))]
+
+
 def put_edges(group, ref, lead_ref, trail_ref):
     length = ref.shape[2]
     place = pl.program_id(0) % (group // TWO)
@@ -312,6 +387,43 @@
                 lanes = slice((k * TWO + j) * REACH, (k * TWO + j + 1) * REACH)
                 lead_ref[0, :, lanes] = ref[j, :, :REACH]
                 trail_ref[0, :, lanes] = ref[j, :, length - REACH :]
+
+
+def middle_rims_kernel(group, lead_in, trail_in, first_ref, mask_ref, w_ref, p_ref, *rest):
+    rim_steps(lead_in, trail_in, *rest[3:5], *rest[5:9])
+    middle_kernel(group, False, None, first_ref, mask_ref, w_ref, p_ref, *rest[:3], *rest[9:])
+
+
+def middle_rims_call(edges, first, mask, w_in, p2, count, group):
+    _, _, length = first.shape
+    seqs = mask.shape[0]
+    edge = pl.BlockSpec((1, INNER, group * REACH), lambda i: (i // (group // TWO), 0, 0))
+    edge_shape = sds((count // group, INNER, group * REACH), BF16)
+    any_spec = pl.BlockSpec(memory_space=pl.ANY)
+
+    def fixed(shape):
+        return pl.BlockSpec(shape, lambda i: (0,) * len(shape), pipeline_mode=pl.Buffered(1))
+
+    def mask_at(i):
+        return (((lax.axis_index("ch") + 1) * (count // TWO) + i) % (seqs // TWO), 0, 0)
+
+    return pl.pallas_call(
+        functools.partial(middle_rims_kernel, group),
+        grid=(count // TWO,),
+        in_specs=[
+            any_spec,
+            any_spec,
+            pl.BlockSpec((TWO, D, length), lambda i: (count // TWO + i, 0, 0)),
+            pl.BlockSpec((TWO, 1, length), mask_at),
+            fixed((INNER, D)),
+            fixed((3, INNER, LANES)),
+        ],
+        out_specs=(pl.BlockSpec((TWO, INNER, length), lambda i: (i, 0, 0)), edge, edge, any_spec, any_spec),
+        out_shape=(sds((count, INNER, length), BF16), *[edge_shape] * 4),
+        scratch_shapes=rim_scratch(edge_shape.shape) + [pltpu.VMEM((INNER, length), F32)] * TWO,
+        cost_estimate=cost_of(count * INNER * D * length * 1.5, count * (D + INNER * 3) * length * 2),
+        compiler_params=pltpu.CompilerParams(vmem_limit_bytes=VMEM_BYTES, collective_id=4, has_side_effects=True),
+    )(*edges, first, mask.reshape(seqs, 1, length), w_in, p2)
 
 
 def middle_kernel(group, keep, pre, first_ref, mask_ref, w_ref, p_ref, mid_ref, lead_ref, trail_ref, *rest):
@@ -726,19 +838,41 @@
     )(pre, part, cot, gt)
 
 
-def turn_kernel(pre, w_ref, flat_ref, turned_ref):
+def turned(square):
     unit = (
         lax.broadcasted_iota(jnp.int32, (INNER, INNER), 0) == lax.broadcasted_iota(jnp.int32, (INNER, INNER), 1)
     ).astype(F32).astype(BF16)
+    return lax.dot_general(unit, square, (((1,), (1,)), ((), ())), preferred_element_type=F32).astype(BF16)
+
+
+def turn_kernel(pre, w_ref, flat_ref, turned_ref):
     flat_ref[...] = w_ref[0]
-    turned_ref[...] = lax.dot_general(
-        unit, w_ref[0], (((1,), (1,)), ((), ())), preferred_element_type=F32
-    ).astype(BF16)
-
-
-def turn_call(pre, conv):
+    turned_ref[...] = turned(w_ref[0])
+
+
+def turn_rims_kernel(lead, trail, w_ref, flat_ref, turned_ref, *rest):
+    rim_steps(lead, trail, *rest)
+    turn_kernel(None, w_ref, flat_ref, turned_ref)
+
+
+def turn_call(pre, conv, edges=None):
+    shape = sds((INNER, KERNEL * INNER), BF16)
+    if edges is not None:
+        any_spec = pl.BlockSpec(memory_space=pl.ANY)
+        column = pl.BlockSpec((INNER, INNER), lambda k: (0, k))
+        return pl.pallas_call(
+            turn_rims_kernel,
+            grid=(KERNEL,),
+            in_specs=[any_spec, any_spec, pl.BlockSpec((1, INNER, INNER), lambda k: (k, 0, 0))],
+            out_specs=(column, column, any_spec, any_spec),
+            out_shape=(shape, shape, *[sds(e.shape, BF16) for e in edges]),
+            scratch_shapes=rim_scratch(edges[0].shape),
+            cost_estimate=cost_of(KERNEL * INNER**3, KERNEL * INNER * INNER * 6),
+            compiler_params=pltpu.CompilerParams(
+                vmem_limit_bytes=VMEM_BYTES, collective_id=3, has_side_effects=True
+            ),
+        )(*edges, conv)
     block = pl.BlockSpec((INNER, INNER), lambda k, pre: (0, k))
-    shape = sds((INNER, KERNEL * INNER), BF16)
     return call(
         turn_kernel,
         (KERNEL,),
@@ -749,26 +883,22 @@
     )(pre, conv)
 
 
-ORDERS = ((0, 1, 2, 3), (0, 1, 2, 3), (0, 2, 3, 1), (0, 2, 3, 1), (0, 1, 2, 3))
+ORDERS = ((0, 1, 2, 3), (0, 1, 2, 3), (0, 2, 3, 1), (0, 1, 2, 3), (0, 1, 2, 3))
 GIVE = 5
 SCHEDULE = {
-    1: [(2, 0)],
-    2: [(0, 0), (2, 1)],
-    3: [(0, 1)],
-    6: [(2, 2)],
-    9: [(5, 0), (3, 0), (0, 2), (1, 0)],
-    10: [(3, 1), (1, 1), (2, 3), (5, 1)],
-    13: [(0, 3), (2, 4)],
-    14: [(5, 2)],
-    15: [(3, 2), (1, 2)],
-    16: [(5, 3), (4, 0), (2, 5)],
-    17: [(4, 1), (2, 6), (3, 3), (4, 2), (0, 4), (5, 4), (1, 3), (2, 7)],
-    19: [(4, 3), (3, 4), (0, 5), (1, 4), (5, 5), (3, 5), (1, 5)],
-    20: [(0, 6)],
-    21: [(1, 6), (4, 4), (3, 6), (5, 6), (2, 8), (4, 5), (0, 7)],
-    22: [(4, 6), (1, 7), (4, 7), (3, 7), (0, 8), (5, 7)],
-    23: [(4, 8), (1, 8), (3, 8), (2, 9)],
-    24: [(3, 9), (4, 9), (1, 9), (5, 8), (0, 9)],
+    1: [(5, 0), (0, 0)],
+    2: [(2, 0), (0, 1), (1, 0)],
+    3: [(5, 1), (2, 1)],
+    5: [(1, 1), (3, 0)],
+    7: [(0, 2), (2, 2), (5, 2)],
+    8: [(3, 1)],
+    9: [(1, 2), (5, 3)],
+    10: [(0, 3)],
+    12: [(5, 4), (2, 3), (3, 2), (1, 3), (0, 4), (4, 0), (0, 5), (4, 1), (2, 4), (5, 5), (3, 3), (1, 4)],
+    13: [(4, 2)],
+    14: [(1, 5), (0, 6), (3, 4), (2, 5), (4, 3), (1, 6), (0, 7), (3, 5), (5, 6)],
+    15: [(2, 6), (1, 7), (3, 6)],
+    16: [(4, 4), (4, 5), (2, 7), (0, 8), (3, 7), (5, 7), (1, 8), (0, 9), (4, 6), (5, 8), (4, 7), (2, 8), (3, 8), (4, 8), (5, 9), (1, 9), (4, 9), (2, 9), (3, 9)],
 }
 
 
@@ -877,7 +1007,7 @@
         pltpu.VMEM((2, SMALL_ROWS >> LEVELS, LANES), BF16),
         pltpu.VMEM((SMALL_ROWS, LANES), BF16),
     ]
-    out += [dma((2 * (KERNEL + D // INNER),)), dma((5, 2 * LEVELS + 1)), dma((5, 2 * LEVELS + 1))]
+    out += [dma((2 * (KERNEL + 2 * D // INNER),)), dma((5, 2 * LEVELS + 1)), dma((5, 2 * LEVELS + 1))]
     return out
 
 
@@ -891,46 +1021,93 @@
     return out
 
 
-def taps_kernel(group, pre, dconv_ref, before_ref, after_ref, mid_ref, gcw_ref, pad_ref, cat_ref):
+def inner_kernel(group, pre, *refs):
+    dconv_ref, before_ref, after_ref, mid_ref, hat_ref, gp_ref, scale_ref, first_ref, wc_ref, p2_ref = refs[:10]
+    dn_ref, gcw_ref, gwi_ref, rows_ref = refs[10:14]
+    pad_ref, cat_ref, d_ref, gg_ref, gb_ref, gbi_ref = refs[14:]
     length = mid_ref.shape[2]
 
     @pl.when(pl.program_id(0) == 0)
     def _():
-        gcw_ref[...] = jnp.zeros_like(gcw_ref)
+        for ref in (gcw_ref, gwi_ref, gg_ref, gb_ref, gbi_ref):
+            ref[...] = jnp.zeros_like(ref)
 
     cats = [cat_ref.at[:, j * length : (j + 1) * length] for j in range(TWO)]
     gather_windows(group, dconv_ref, before_ref, after_ref, pad_ref, cats, -1)
+    d_ref[...] = jnp.dot(wc_ref[...], cat_ref[...], preferred_element_type=F32)
     mid = jnp.concatenate([mid_ref[j] for j in range(TWO)], axis=1)
     gcw_ref[...] += lax.dot_general(cat_ref[...], mid, (((1,), (1,)), ((), ())), preferred_element_type=F32)
 
-
-def taps_call(pre, dconv, before, after, mid, group):
+    def put(sl, v):
+        for j in range(TWO):
+            dn_ref[j, sl, :] = v[:, j * length : (j + 1) * length]
+
+    norm_back(d_ref, gp_ref, hat_ref, across(scale_ref, 0), p2_ref, gg_ref, gb_ref, gbi_ref, put)
+    dn = jnp.concatenate([dn_ref[j] for j in range(TWO)], axis=1)
+    first = jnp.concatenate([first_ref[j] for j in range(TWO)], axis=1)
+    gwi_ref[...] += lax.dot_general(dn, first, (((1,), (1,)), ((), ())), preferred_element_type=F32)
+
+    @pl.when(pl.program_id(0) == pl.num_programs(0) - 1)
+    def _():
+        for k, ref in enumerate((gbi_ref, gg_ref, gb_ref)):
+            rows_ref[:, k * INNER : (k + 1) * INNER] = row_sums(ref)
+
+
+def inner_call(pre, dconv, before, after, mid, hat, gp, scale, first, wc_t, p2, group):
     count, _, length = dconv.shape
     edge = pl.BlockSpec((1, INNER, group * REACH), lambda i, pre: (i // (group // TWO), 0, 0))
     own = pl.BlockSpec((TWO, INNER, length), lambda i, pre: (i, 0, 0))
+    sums = [(KERNEL * INNER, INNER), (INNER, D), (8, 3 * INNER)]
     return call(
-        functools.partial(taps_kernel, group),
+        functools.partial(inner_kernel, group),
         (count // TWO,),
-        [own, edge, edge, own],
-        const((KERNEL * INNER, INNER)),
-        sds((KERNEL * INNER, INNER), F32),
+        [
+            own,
+            edge,
+            edge,
+            own,
+            own,
+            own,
+            pl.BlockSpec((TWO, 1, length), lambda i, pre: (i, 0, 0)),
+            pl.BlockSpec((TWO, D, length), lambda i, pre: (i, 0, 0)),
+            whole(wc_t.shape),
+            whole((1, INNER, LANES), 1),
+        ],
+        tuple([own] + [const(v) for v in sums]),
+        tuple([sds(dconv.shape, BF16)] + [sds(v, F32) for v in sums]),
         scratch=[
             pltpu.VMEM((TWO, INNER, length + 2 * LANES), BF16),
             pltpu.VMEM((KERNEL * INNER, TWO * length), BF16),
-        ],
-        cost=cost_of(count * KERNEL * INNER * INNER * length, KERNEL * INNER * INNER * 4),
-    )(pre, dconv, before, after, mid)
+            pltpu.VMEM((INNER, TWO * length), F32),
+        ]
+        + [pltpu.VMEM((INNER, LANES), F32)] * 3,
+        cost=cost_of(count * (2 * KERNEL * INNER + D) * INNER * length, KERNEL * INNER * INNER * 4),
+    )(pre, dconv, before, after, mid, hat, gp, scale, first, wc_t, p2)
+
+
+KINDS = [0, 0, 0, 0, 0, 0, 1, 0, 0, 1, 1, 1, 1, 1, 1, 1]
+
+
+def turn_of(kind, step):
+    steps = [k for k, v in enumerate(KINDS) if v == kind]
+    return sum((jnp.asarray(step >= k).astype(jnp.int32) for k in steps[1:]), jnp.int32(0))
+
+
+def is_turn(kind, step):
+    return functools.reduce(jnp.logical_or, (step == k for k, v in enumerate(KINDS) if v == kind))
 
 
 def tail_kernel(group, *refs):
-    dconv_ref, before_ref, after_ref, hat_ref, gp_ref, scale_ref, keep_ref, x_ref, stat_ref = refs[:9]
-    mid_ref, before_oth, after_oth, wct_ref, wc_ref, wi_ref, p1_ref, p2_ref, rows_ref = refs[9:18]
-    gcw_ref, gwo_ref = refs[18:20]
-    mine_ref, last_ref, total_ref, small_ref, got_ref = refs[20:25]
-    stream_refs = refs[25:47]
-    pad_ref, cat_ref, d_ref, dn_ref, df_ref = refs[47:52]
-    gg2_ref, gb2_ref, gbi_ref, gg1_ref, gb1_ref, give_send, give_recv = refs[52:]
-    give_ref = dn_ref
+    dn_ref, x_ref, stat_ref, mid_ref, lead_oth, trail_oth, wc_ref, wi_ref, p1_ref, p2_ref = refs[:10]
+    rows_ref, rows_in_ref, gcw_ref, gwo_ref, gwi_ref = refs[10:15]
+    w_in_ref, wi_ref = wi_ref, refs[-1]
+    refs = refs[:-1]
+    mine_ref, last_ref, total_ref, small_ref, got_ref = refs[15:20]
+    stream_refs = refs[20:42]
+    pad_ref, cat_ref, d_ref, give_ref, df_ref = refs[42:47]
+    gg1_ref, gb1_ref, give_send, give_recv = refs[47:51]
+    before_oth, after_oth, rim_send, rim_recv = refs[51:]
+    rims = Rims(lead_oth, trail_oth, before_oth, after_oth, rim_send, rim_recv)
     acc, small_acc, res, small_res, load_sem = (stream_refs[k] for k in (0, 14, 13, 18, 19))
     base = 3 * ROWS
     share, length = give_ref.shape[1], give_ref.shape[2]
@@ -938,6 +1115,7 @@
     step, steps = pl.program_id(0), pl.num_programs(0)
     count = give_ref.shape[0]
     streams = streams_of(stream_refs)
+    outer_now, conv_now = turn_of(0, step), turn_of(1, step)
 
     def loads():
         out = []
@@ -947,6 +1125,9 @@
             pieces += [gwo_ref.at[mine, pl.ds(j * INNER, INNER)] for j in range(D // INNER)]
             for j, piece in enumerate(pieces):
                 out.append((piece, acc.at[h, pl.ds(j * HALF, HALF), :]))
+            for j in range(D // INNER):
+                piece = gwi_ref.at[mine, pl.ds(j * INNER, INNER)]
+                out.append((piece, acc.at[h, pl.ds(base + j * HALF, HALF), :]))
         return [pltpu.make_async_copy(a, b, load_sem.at[j]) for j, (a, b) in enumerate(out)]
 
     def give(i):
@@ -960,8 +1141,7 @@
         )
 
     def fill_inner():
-        inner = [row_sums(ref)[0:1] for ref in (gbi_ref, gg2_ref, gb2_ref)]
-        inner += [rows_ref[0:1, k * INNER : (k + 1) * INNER] for k in range(3)]
+        inner = [ref[0:1, k * INNER : (k + 1) * INNER] for ref in (rows_in_ref, rows_ref) for k in range(3)]
         at = base + HALF * D // INNER
         for h in range(2):
             for k, v in enumerate(inner):
@@ -980,8 +1160,8 @@
     def act(actions):
         for q, k in actions:
             if q == GIVE:
-                if k > 0:
-                    give(k - 1).wait()
+                if k > 1:
+                    give(k - 2).wait()
                 if k < count:
                     give(k).start()
                 continue
@@ -997,15 +1177,23 @@
     @pl.when(step == 0)
     def _():
         for h in range(2):
-            acc[h, EARLY_ROWS:, :] = jnp.zeros((4 * ROWS - EARLY_ROWS, INNER), F32)
+            acc[h, EARLY_ROWS:base, :] = jnp.zeros((base - EARLY_ROWS, INNER), F32)
+            used = base + HALF * D // INNER
+            acc[h, used:, :] = jnp.zeros((4 * ROWS - used, INNER), F32)
         for copy in loads():
             copy.start()
+        before_oth[...] = jnp.zeros_like(before_oth)
+        after_oth[...] = jnp.zeros_like(after_oth)
         barrier = pltpu.get_barrier_semaphore()
         for device in [streams[0].partner(b) for b in range(LEVELS)] + [{"ch": 1 - ch}]:
             pl.semaphore_signal(barrier, inc=1, device_id=device, device_id_type=pl.DeviceIdType.MESH)
-        pl.semaphore_wait(barrier, LEVELS + 1)
-        for ref in (gg2_ref, gb2_ref, gbi_ref, gg1_ref, gb1_ref):
+        pl.semaphore_wait(barrier, LEVELS + 1 + rims.greet())
+        rims.start()
+        for ref in (gg1_ref, gb1_ref):
             ref[...] = jnp.zeros_like(ref)
+        for j in range(D // INNER):
+            block = slice(j * INNER, (j + 1) * INNER)
+            wi_ref[block, :] = turned(w_in_ref[:, block])
 
     @pl.when(step == min(SCHEDULE))
     def _():
@@ -1013,35 +1201,16 @@
             copy.wait()
 
     for at, actions in SCHEDULE.items():
-        if at < 3 * count:
+        if at < len(KINDS):
 
             @pl.when(step == at)
             def _():
                 act(actions)
 
-    @pl.when(step < count)
+    @pl.when(is_turn(0, step))
     def _():
-        gather_windows(group, dconv_ref, before_ref, after_ref, pad_ref, [cat_ref], -1, step)
-        d_ref[...] = jnp.dot(wct_ref[...], cat_ref[...], preferred_element_type=F32)
-
-        def put(sl, v):
-            dn_ref[step, sl, :] = v
-
-        norm_back(d_ref, gp_ref, hat_ref, scale_ref[0], p2_ref.at[1:2], gg2_ref, gb2_ref, gbi_ref, put)
-        for h in range(2):
-            for j in range(D // INNER):
-                part = lax.dot_general(
-                    dn_ref[step, h * HALF : (h + 1) * HALF, :],
-                    keep_ref[0, j * INNER : (j + 1) * INNER, :],
-                    (((1,), (1,)), ((), ())),
-                    preferred_element_type=F32,
-                )
-                acc[h, base + j * HALF : base + (j + 1) * HALF, :] += part
-
-    @pl.when(jnp.logical_and(step >= count, step < 2 * count))
-    def _():
-        now = step - count
-        df_ref[...] = jnp.dot(wi_ref[...], dn_ref[now], preferred_element_type=F32)
+        now = outer_now
+        df_ref[...] = jnp.dot(wi_ref[...], dn_ref[0], preferred_element_type=F32)
         mean_in, scale_in = stat_ref[0, 0:1, :], stat_ref[0, 1:2, :]
         zero = jnp.zeros((8, length), F32)
 
@@ -1074,9 +1243,12 @@
 
             straight(share, length, out, 0)
 
-    @pl.when(step >= 2 * count)
+    pl.when(step == KINDS.index(1))(rims.wait)
+
+    @pl.when(is_turn(1, step))
     def _():
-        gather_windows(group, mid_ref, before_oth, after_oth, pad_ref, [cat_ref], 1, step)
+        held = pl.ds(conv_now // group, 1)
+        gather_windows(group, mid_ref, before_oth.at[held], after_oth.at[held], pad_ref, [cat_ref], 1, conv_now)
         conv = jnp.dot(wc_ref[...], cat_ref[...], preferred_element_type=F32)
         d_ref[...] = conv + spread(p2_ref[3], length)
         mean, scale = norm_stats(lambda sl: d_ref[sl, :], INNER, length)
@@ -1102,50 +1274,39 @@
             copy.wait()
 
 
-def tail_call(dconv, rims_own, hat, gp, scale, first, tokens, stat, mid, rims_oth, wc_t, wc, wi_t, p1, p2, rows, gcw, gwo, group):
-    count, _, length = dconv.shape
+def tail_call(dn, tokens, stat, mid, rims_oth, wc, w_in, p1, p2, rows, rows_in, gcw, gwo, gwi, group):
+    count, _, length = dn.shape
     share = D // 2
     any_spec = pl.BlockSpec(memory_space=pl.ANY)
 
     def fixed(shape):
         return pl.BlockSpec(shape, lambda i: (0,) * len(shape), pipeline_mode=pl.Buffered(1))
 
-    def phase(k):
-        return lambda i: jnp.clip(i - k * count, 0, count - 1)
-
     def block(k, width):
-        return pl.BlockSpec((1, width, length), lambda i: (phase(k)(i), 0, 0))
-
-    def edge(k):
-        return pl.BlockSpec((1, INNER, group * REACH), lambda i: (phase(k)(i) // group, 0, 0))
+        return pl.BlockSpec((1, width, length), lambda i: (turn_of(k, i), 0, 0))
 
     dma = pltpu.SemaphoreType.DMA
     return pl.pallas_call(
         functools.partial(tail_kernel, group),
-        grid=(3 * count,),
+        grid=(len(KINDS),),
         in_specs=[
             block(0, INNER),
-            edge(0),
-            edge(0),
-            block(0, INNER),
-            block(0, INNER),
-            block(0, 1),
-            block(0, D),
-            pl.BlockSpec((1, D, length), lambda i: (lax.axis_index("ch") * count + phase(1)(i), 0, 0)),
-            block(1, 2),
-            block(2, INNER),
-            edge(2),
-            edge(2),
-            fixed(wc_t.shape),
+            pl.BlockSpec((1, D, length), lambda i: (lax.axis_index("ch") * count + turn_of(0, i), 0, 0)),
+            block(0, 2),
+            block(1, INNER),
+            any_spec,
+            any_spec,
             fixed(wc.shape),
-            fixed(wi_t.shape),
+            fixed(w_in.shape),
             fixed(p1.shape),
             fixed(p2.shape),
             fixed(rows.shape),
+            fixed(rows_in.shape),
+            any_spec,
             any_spec,
             any_spec,
         ],
-        out_specs=(block(1, share), block(2, INNER), any_spec, any_spec, any_spec),
+        out_specs=(block(0, share), block(1, INNER), any_spec, any_spec, any_spec),
         out_shape=(
             sds((count, share, length), BF16),
             sds((count, INNER, length), BF16),
@@ -1158,21 +1319,23 @@
             pltpu.VMEM((1, INNER, length + 2 * LANES), BF16),
             pltpu.VMEM((KERNEL * INNER, length), BF16),
             pltpu.VMEM((INNER, length), F32),
-            pltpu.VMEM((count, INNER, length), BF16),
+            pltpu.VMEM((count, share, length), BF16),
             pltpu.VMEM((D, length), F32),
-            pltpu.VMEM((INNER, LANES), F32),
-            pltpu.VMEM((INNER, LANES), F32),
-            pltpu.VMEM((INNER, LANES), F32),
             pltpu.VMEM((D, LANES), F32),
             pltpu.VMEM((D, LANES), F32),
             dma((count,)),
             dma((count,)),
+            pltpu.VMEM(rims_oth[0].shape, BF16),
+            pltpu.VMEM(rims_oth[0].shape, BF16),
+            dma((2,)),
+            dma((2,)),
+            pltpu.VMEM((D, INNER), BF16),
         ],
         cost_estimate=cost_of(count * INNER * (KERNEL * INNER + D) * length * 4, 4 * ROWS * INNER * 12),
         compiler_params=pltpu.CompilerParams(
             vmem_limit_bytes=TAIL_BYTES, collective_id=2, has_side_effects=True
         ),
-    )(dconv, *rims_own, hat, gp, scale, first, tokens, stat, mid, *rims_oth, wc_t, wc, wi_t, p1, p2, rows, gcw, gwo)
+    )(dn, tokens, stat, mid, *rims_oth, wc, w_in, p1, p2, rows, rows_in, gcw, gwo, gwi)
 
 
 TAIL_BYTES = 63 * 1024 * 1024
@@ -1309,47 +1472,59 @@
 
     p1 = lane_copies(jnp.stack([ln1_gain, first_norm_bias]))
     bo = lane_copies(b_out)
-    vec = jnp.stack([b_in, ln2_gain, ln2_bias, conv_b, ln3_gain, ln3_bias, b_in, b_in])
+    vectors = [b_in, ln2_gain, ln2_bias, conv_b, ln3_gain, ln3_bias]
     if pair:
+        vec = jnp.pad(jnp.concatenate(vectors), (0, 2048 - 6 * part)).reshape(16, LANES)
         first, stat, w_in_full, conv_full, w_out_full, vec_full, away = first_call(
             pre, tokens, p1, (w_in, conv_w, w_out), vec, cotangent
         )
         others = [rotate(away, "ch", chs, 1)]
-        inner = vec_full.transpose(1, 0, 2).reshape(8, INNER)[:6]
+        vec_full = vec_full.reshape(2, 2048)[:, : 6 * part].reshape(2, 6, part)
+        inner = vec_full.transpose(1, 0, 2).reshape(6, INNER)
     else:
         first, stat = first_call(pre, tokens, p1, None, None)
         w_in_full = lax.all_gather(w_in, "ch", axis=0, tiled=True)
         conv_full = lax.all_gather(conv_w, "ch", axis=1, tiled=True)
         w_out_full = lax.all_gather(w_out, "ch", axis=0, tiled=True)
-        inner = lax.all_gather(vec, "ch", axis=1, tiled=True)[:6]
+        inner = lax.all_gather(jnp.stack(vectors), "ch", axis=1, tiled=True)
         others = []
         for r in range(1, chs):
             block = lax.dynamic_slice_in_dim(cotangent, ((ch + r) % chs) * n, n, 0)
             others.append(rotate(block, "ch", chs, r))
 
     p2 = lane_copies(inner)
-    wc, wc_t = turn_call(pre, conv_full)
-    wi_t = w_in_full.T
     wo_t = lax.dynamic_slice_in_dim(w_out_full, ch * share, share, 1).T
 
     mid_own, lead, trail, hat_mid, gp_mid, scale_mid = middle_call(
         pre, first, pad_mask, w_in_full, p2, n, 0, group, True
     )
-    before, after = rims(lead, trail)
-    mid_oth, lead, trail = middle_call(pre, first, pad_mask, w_in_full, p2, seqs - n, n, group, False)
-    before_oth, after_oth = rims(lead, trail)
+    if pair:
+        wc, wc_t, before, after = turn_call(pre, conv_full, (lead, trail))
+    else:
+        wc, wc_t = turn_call(pre, conv_full)
+        before, after = rims(lead, trail)
+        mid_oth, lead, trail = middle_call(pre, first, pad_mask, w_in_full, p2, seqs - n, n, group, False)
+        rims_oth = rims(lead, trail)
     mixed, hat_out, gp_out, scale_out, last_own = last_call(
         pre, mid_own, before, after, tokens, wc, wo_t, p2, bo, n, 0, group, True, None
     )
     dconv, lead, trail, gg3, gb3, gcb, gwo, gbo, rows = rear_call(
         pre, cotangent, others, w_out_full, hat_out, gp_out, last_own, scale_out, p2, group
     )
-    lead, trail = rims(lead, trail)
     if pair:
-        gcw = taps_call(pre, dconv, lead, trail, mid_own, group)
+        mid_oth, lead_oth, trail_oth, lead, trail = middle_rims_call(
+            (lead, trail), first, pad_mask, w_in_full, p2, n, group
+        )
+        rims_oth = (lead_oth, trail_oth)
+    else:
+        lead, trail = rims(lead, trail)
+    if pair:
+        dn, gcw, gwi, rows_in = inner_call(
+            pre, dconv, lead, trail, mid_own, hat_mid, gp_mid, scale_mid, first, wc_t, p2, group
+        )
         mine, last_oth, total, small, got = tail_call(
-            dconv, (lead, trail), hat_mid, gp_mid, scale_mid, first, tokens, stat, mid_oth, (before_oth, after_oth),
-            wc_t, wc, wi_t, p1, p2, rows, gcw.reshape(KERNEL, INNER, INNER), gwo, group,
+            dn, tokens, stat, mid_oth, rims_oth, wc, w_in_full, p1, p2, rows, rows_in,
+            gcw.reshape(KERNEL, INNER, INNER), gwo, gwi, group,
         )
         gt, mixed, gcw, gwi, gwo, inner_sums, outer_sums = finish_call(
             pre, mine, got, cotangent, last_oth, tokens, wo_t, bo, total, small, mixed, part
@@ -1358,7 +1533,7 @@
     else:
         gt, *rest = front_call(
             pre, dconv, lead, trail, mid_own, hat_mid, gp_mid, scale_mid, tokens, stat, cotangent,
-            wc_t, wi_t, p2, p1, chs, group,
+            wc_t, w_in_full.T, p2, p1, chs, group,
         )
         sends = [rotate(v, "ch", chs, r + 1) for r, v in enumerate(rest[: chs - 1])]
         gcw, gwi, gg2, gb2, gbi, gg1, gb1 = rest[chs - 1 :]
@@ -1366,7 +1541,7 @@
         inner_sums = jnp.stack([v.sum(1) for v in (gbi, gg2, gb2, gcb, gg3, gb3)])
         outer_sums = jnp.stack([v.sum(1) for v in (gg1, gb1, gbo)])
         mixed, = last_call(
-            pre, mid_oth, before_oth, after_oth, tokens, wc, wo_t, p2, bo, seqs - n, n, group, False, mixed
+            pre, mid_oth, *rims_oth, tokens, wc, wo_t, p2, bo, seqs - n, n, group, False, mixed
         )
         gcw, gwi, gwo, inner_sums, outer_sums = lax.psum((gcw, gwi, gwo, inner_sums, outer_sums), ("seq", "ch"))
         gcw = own_slice(gcw, part, 1)

time: 325 us -> 299 us (0.920)
  starting transfers between devices: 14.5 us -> 0.67 us
  Pallas kernels: 287 us -> 278 us
  local copies, waits for them, and re-layouts: 20.7 us -> 15.3 us
    ppermute x6 -> x0, starting transfers between devices: 13.8 us -> none  [shift(): return lax.ppermute(value, 'seq', pairs)]
    pallas_call x2 -> x1, Pallas kernels: 26.1 us -> 14.2 us  [middle_call(): call(functools.partial(middle_kernel, group, keep), (count // TWO,), [pl....]
    another operation x7 -> x0, local copies, waits for them, and re-layouts: 4.72 us -> none  [body(): jnp.stack([b_in, ln2_gain, ln2_bias, conv_b, ln3_gain, ln3_bias, b_in, b_...]
    pallas_call x3 -> x4, Pallas kernels: 159 us -> 162 us  [the longest x1 102 us: tail_call(): pl.pallas_call(functools.partial(tail_kernel, group), grid=(len(KINDS),),...]
  transfers between devices with their start and end apart: 7 -> 1, of which waited for: 0 -> 1; matrix products, arithmetic and copies ran while one was open for 3% -> 3% of each run, Pallas kernels for 24% -> 16%
where the time goes in v5:
time: 299 us; the launch traced here: 298 us
  Pallas kernels  278 us (93%)
  local copies, waits for them, and re-layouts  15.3 us (5%)
    pallas_call x1, Pallas kernels, tail_call(): pl.pallas_call(functools.partial(tail_kernel, group), grid=(len(KINDS),),...  102 us
    pallas_call x1, Pallas kernels, inner_call(): call(functools.partial(inner_kernel, group), (count // TWO,), [own, edge,...  39.4 us
    pallas_call x1, Pallas kernels, first_call(): pl.pallas_call(lambda *refs: first_kernel(True, None, *refs), grid=(seqs,...  38.9 us
    pallas_call x1, Pallas kernels, last_call(): call(functools.partial(last_kernel, group, keep), (count // TWO,), in_spe...  24.4 us
    pallas_call x1, Pallas kernels, rear_call(): call(functools.partial(rear_kernel, group, chs), (count // TWO,), [pl.Blo...  20.1 us
    pallas_call x1, Pallas kernels, finish_call(): call(finish_kernel, (2 * count,), [pl.BlockSpec((TWO, share, length), lam...  18.2 us
    pallas_call x1, Pallas kernels, middle_call(): call(functools.partial(middle_kernel, group, keep), (count // TWO,), [pl....  14.2 us
    pallas_call x1, Pallas kernels, middle_rims_call(): pl.pallas_call(functools.partial(middle_rims_kernel, group), grid=(count...  11.9 us
  transfers between devices with their start and end apart: 1, of which 1 were waited for; matrix products, arithmetic and copies ran while one was open for 3% of the time, Pallas kernels for 16%

profile of v5, /device:TPU:0, one launch (start us, length us, event | category | flops | bytes accessed | tf_op | source)
XLA Modules:
  0.0 298.0 jit_solution(9202774588574842298)
XLA Ops:
  0.6 0.7 stack.25
  1.3 0.7 stack.26
  2.0 0.8 concatenate.3
  2.9 0.6 pad_bitcast_fusion.refs_5_
  3.5 1.5 broadcast_in_dim.8.refs_1_.refs_8_
  5.0 0.0 copy-start
  5.0 38.9 %shard_map.254 = (bf16[16,1280,256]{2,1,0:T(8,128)(2,1)}, f32[16,2,256]{2,1,0:T(2,128)}, bf16[640,1280]{1,0:T(8,128)(2,1)}, bf16[5,640,640]{2,1,0:T(8,128)(2,1)}...) custom-call(bf16[16,1280,256]{2,1,0:T(8,128)(2,1)} %x_ref.3, ...), custom_call_target="tpu_custom_call" | custom-call | flops 419430400 | bytes 20971520 | tf_op jit(solution)/shard_map/pallas_call | solution.py:280
  43.9 0.7 collective-permute-start
  44.6 0.0 copy-done
  44.6 0.6 reshape.55.mask_ref
  45.2 0.7 copy.37
  45.9 0.1 reshape.57
  46.0 0.1 broadcast_in_dim.9
  46.1 2.9 copy.34
  49.0 0.6 pad_add_fusion.pre
  49.6 1.0 dynamic-slice_bitcast_fusion.wo_ref
  50.5 1.9 broadcast_in_dim.10.p_ref.refs_7_.refs_9_
  52.4 14.2 %shard_map.255 = (bf16[8,640,256]{2,1,0:T(8,128)(2,1)}, bf16[2,640,128]{2,1,0:T(8,128)(2,1)}, bf16[2,640,128]{2,1,0:T(8,128)(2,1)}, bf16[8,640,256]{2,1,0:T(8,12...) custom-call(s32[3]{0:T(128)} %pad_add_fusion.pre, bf16[16,1280,256]{2,1,0:T(8,128)(2,1)} %get-tuple-element.64.first_ref.refs_7_, ...), custom_call_target="tpu_custom_call" | custom-call | flops 5033164800 | bytes 13107200 | tf_op jit(solution)/shard_map/pallas_call | solution.py:471
  66.6 0.0 copy-start.1
  66.6 8.9 %shard_map.256 = (bf16[640,3200]{1,0:T(8,128)(2,1)}, bf16[640,3200]{1,0:T(8,128)(2,1)}, bf16[2,640,128]{2,1,0:T(8,128)(2,1)}, bf16[2,640,128]{2,1,0:T(8,128)(2,1)}) custom-call(bf16[2,640,128]{2,1,0:T(8,128)(2,1)} %get-tuple-element.68.lead, bf16[2,640,128]{2,1,0:T(8,128)(2,1)} %get-tuple-element.69.trail, bf16[5,640,640]{2,1,0:T(8,128)(2,1)} %get-tuple-element.70.w_ref), custom_call_target="tpu_custom_call" | custom-call | flops 2621440000 | bytes 12288000 | tf_op jit(solution)/shard_map/pallas_call | solution.py:863
  75.5 0.0 copy-done.1
  75.5 0.9 broadcast_in_dim.22.b_ref
  76.3 24.4 %shard_map.257 = (bf16[16,640,256]{2,1,0:T(8,128)(2,1)}, bf16[8,640,256]{2,1,0:T(8,128)(2,1)}, f32[8,640,256]{2,1,0:T(8,128)}, f32[8,1,256]{2,1,0:T(1,128)}, bf16[8,640,256]{2,1,0:T(8,128)(2,1)}) custom-call(s32[3]{0:T(128)} %pad_add_fusion.pre, bf16[8,640,256]{2,1,0:T(8,128)(2,1)} %get-tuple-element.67.mid_ref.refs_3_, ...), custom_call_target="tpu_custom_call" | custom-call | flops 13086228480 | bytes 15728640 | tf_op jit(solution)/shard_map/pallas_call | solution.py:578
  100.8 2.7 collective-permute-done.refs_1_
  103.4 20.1 %shard_map.258 = (bf16[8,640,256]{2,1,0:T(8,128)(2,1)}, bf16[2,640,128]{2,1,0:T(8,128)(2,1)}, bf16[2,640,128]{2,1,0:T(8,128)(2,1)}, f32[640,128]{1,0:T(8,128)}, ...) custom-call(s32[3]{0:T(128)} %pad_add_fusion.pre, ...), custom_call_target="tpu_custom_call" | custom-call | flops 8388608000 | bytes 13107200 | tf_op jit(solution)/shard_map/pallas_call | solution.py:678
  123.5 11.9 %shard_map.259 = (bf16[8,640,256]{2,1,0:T(8,128)(2,1)}, bf16[2,640,128]{2,1,0:T(8,128)(2,1)}, bf16[2,640,128]{2,1,0:T(8,128)(2,1)}, bf16[2,640,128]{2,1,0:T(8,128)(2,1)}, bf16[2,640,128]{2,1,0:T(8,128)(2,1)}) custom-call(bf16[2,640,128]{2,1,0:T(8,128)(2,1)} %get-tuple-element.79.lead_in, bf16[2,640,128]{2,1,0:T(8,128)(2,1)} %get-tuple-element.80.trail_in, ...), custom_call_target="tpu_custom_call" | custom-call | flops 5033164800 | bytes 13107200 | tf_op jit(solution)/shard_map/pallas_call | solution.py:410
  135.5 39.4 %shard_map.260 = (bf16[8,640,256]{2,1,0:T(8,128)(2,1)}, f32[3200,640]{1,0:T(8,128)}, f32[640,1280]{1,0:T(8,128)}, f32[8,1920]{1,0:T(8,128)}) custom-call(s32[3]{0:T(128)} %pad_add_fusion.pre, bf16[8,640,256]{2,1,0:T(8,128)(2,1)} %get-tuple-element.78.refs_0_, bf16[2,640,128]{2,1,0:T(8,128)(2,1)} %get-tuple-element.81.refs_1_, ...), custom_call_target="tpu_custom_call" | custom-call | flops 20132659200 | bytes 8192000 | tf_op jit(solution)/shard_map/pallas_call | solution.py:1061
  174.9 102.0 %shard_map.261 = (bf16[8,640,256]{2,1,0:T(8,128)(2,1)}, bf16[8,640,256]{2,1,0:T(8,128)(2,1)}, bf16[3072,640]{1,0:T(8,128)(2,1)}, bf16[256,128]{1,0:T(8,128)(2,1)}, bf16[8,640,256]{2,1,0:T(8,128)(2,1)}) custom-call(bf16[8,640,256]{2,1,0:T(8,128)(2,1)} %get-tuple-element.87.refs_0_, bf16[16,1280,256]{2,1,0:T(8,128)(2,1)} %x_ref.3, ...), custom_call_target="tpu_custom_call" | custom-call | flops 46976204800 | bytes 23592960 | tf_op jit(solution)/shard_map/pallas_call | solution.py:1289
  276.9 18.2 %shard_map.262 = (f32[16,640,256]{2,1,0:T(8,128)}, bf16[16,640,256]{2,1,0:T(8,128)(2,1)}, f32[5,320,640]{2,1,0:T(8,128)}, f32[320,1280]{1,0:T(8,128)}, f32[320,1...) custom-call(s32[3]{0:T(128)} %pad_add_fusion.pre, ...), custom_call_target="tpu_custom_call", output_to_operand_aliasing={{1}: (10, {})} | custom-call | tf_op jit(solution)/shard_map/pallas_call | solution.py:1386
  295.1 1.6 slice_reduce_fusion
  296.7 1.4 slice_bitcast_fusion
  (3 shorter events, 0.0 us)
Async XLA Ops:
  5.0 39.6 %copy-start = (s32[16,256]{1,0:T(8,128)S(1)}, s32[16,256]{1,0:T(8,128)}, u32[]{:S(2)}) copy-start(s32[16,256]{1,0:T(8,128)} %param.16) | copy-start | bytes 49156
  43.9 59.5 %collective-permute-start = (bf16[8,640,256]{2,1,0:T(8,128)(2,1)}, bf16[8,640,256]{2,1,0:T(8,128)(2,1)}, u32[]{:S(2)}, u32[]{:S(2)}) collective-permute-start(bf16[8,640,256]{2,1,0:T(8,128)(2,1)} %get-tuple-element.62), channel_id=1, source_target_pairs={{0,1},{1,0},{2,3},{3,2},{4,5},{5,4},{6,7},{7,6},{8,9},{9,8},{10,11... | collective-permute-start | bytes 7864328 | tf_op jit(solution)/shard_map/ppermute | solution.py:1424
  66.6 8.9 %copy-start.1 = (f32[640]{0:T(1024)S(1)}, f32[640]{0:T(1024)}, u32[]{:S(2)}) copy-start(f32[640]{0:T(1024)} %param.29) | copy-start | bytes 7684

commit v6 on v5

--- a/solution.py
+++ b/solution.py
@@ -850,12 +850,16 @@
     turned_ref[...] = turned(w_ref[0])
 
 
-def turn_rims_kernel(lead, trail, w_ref, flat_ref, turned_ref, *rest):
-    rim_steps(lead, trail, *rest)
+def turn_rims_kernel(lead, trail, w_ref, wo_ref, flat_ref, turned_ref, before, after, wo_t_ref, *rest):
+    rim_steps(lead, trail, before, after, *rest)
     turn_kernel(None, w_ref, flat_ref, turned_ref)
 
-
-def turn_call(pre, conv, edges=None):
+    @pl.when(pl.program_id(0) == 0)
+    def _():
+        wo_t_ref[...] = turned(wo_ref[...])
+
+
+def turn_call(pre, conv, edges=None, w_out=None):
     shape = sds((INNER, KERNEL * INNER), BF16)
     if edges is not None:
         any_spec = pl.BlockSpec(memory_space=pl.ANY)
@@ -863,15 +867,20 @@
         return pl.pallas_call(
             turn_rims_kernel,
             grid=(KERNEL,),
-            in_specs=[any_spec, any_spec, pl.BlockSpec((1, INNER, INNER), lambda k: (k, 0, 0))],
-            out_specs=(column, column, any_spec, any_spec),
-            out_shape=(shape, shape, *[sds(e.shape, BF16) for e in edges]),
+            in_specs=[
+                any_spec,
+                any_spec,
+                pl.BlockSpec((1, INNER, INNER), lambda k: (k, 0, 0)),
+                pl.BlockSpec((INNER, INNER), lambda k: (0, lax.axis_index("ch"))),
+            ],
+            out_specs=(column, column, any_spec, any_spec, pl.BlockSpec((INNER, INNER), lambda k: (0, 0))),
+            out_shape=(shape, shape, *[sds(e.shape, BF16) for e in edges], sds((INNER, INNER), BF16)),
             scratch_shapes=rim_scratch(edges[0].shape),
             cost_estimate=cost_of(KERNEL * INNER**3, KERNEL * INNER * INNER * 6),
             compiler_params=pltpu.CompilerParams(
                 vmem_limit_bytes=VMEM_BYTES, collective_id=3, has_side_effects=True
             ),
-        )(*edges, conv)
+        )(*edges, conv, w_out)
     block = pl.BlockSpec((INNER, INNER), lambda k, pre: (0, k))
     return call(
         turn_kernel,
@@ -1029,14 +1038,16 @@
 
     @pl.when(pl.program_id(0) == 0)
     def _():
-        for ref in (gcw_ref, gwi_ref, gg_ref, gb_ref, gbi_ref):
+        for ref in (gg_ref, gb_ref, gbi_ref):
             ref[...] = jnp.zeros_like(ref)
 
     cats = [cat_ref.at[:, j * length : (j + 1) * length] for j in range(TWO)]
     gather_windows(group, dconv_ref, before_ref, after_ref, pad_ref, cats, -1)
     d_ref[...] = jnp.dot(wc_ref[...], cat_ref[...], preferred_element_type=F32)
     mid = jnp.concatenate([mid_ref[j] for j in range(TWO)], axis=1)
-    gcw_ref[...] += lax.dot_general(cat_ref[...], mid, (((1,), (1,)), ((), ())), preferred_element_type=F32)
+    fresh = pl.program_id(0) == 0
+    gcw = lax.dot_general(cat_ref[...], mid, (((1,), (1,)), ((), ())), preferred_element_type=F32)
+    gcw_ref[...] = jnp.where(fresh, 0.0, gcw_ref[...]) + gcw
 
     def put(sl, v):
         for j in range(TWO):
@@ -1045,7 +1056,8 @@
     norm_back(d_ref, gp_ref, hat_ref, across(scale_ref, 0), p2_ref, gg_ref, gb_ref, gbi_ref, put)
     dn = jnp.concatenate([dn_ref[j] for j in range(TWO)], axis=1)
     first = jnp.concatenate([first_ref[j] for j in range(TWO)], axis=1)
-    gwi_ref[...] += lax.dot_general(dn, first, (((1,), (1,)), ((), ())), preferred_element_type=F32)
+    gwi = lax.dot_general(dn, first, (((1,), (1,)), ((), ())), preferred_element_type=F32)
+    gwi_ref[...] = jnp.where(fresh, 0.0, gwi_ref[...]) + gwi
 
     @pl.when(pl.program_id(0) == pl.num_programs(0) - 1)
     def _():
@@ -1342,7 +1354,8 @@
 
 
 def finish_kernel(pre, mine_ref, got_ref, dy_ref, last_ref, x_ref, wo_ref, b_ref, total_ref, small_ref, _, *outs):
-    gt_ref, mixed_ref, gcw_ref, gwi_ref, gwo_ref, inner_ref, outer_ref = outs
+    gt_ref, mixed_ref, gcw_ref, gwi_ref, gwo_ref = outs[:5]
+    inner_refs, outer_refs = outs[5:11], outs[11:]
     length = dy_ref.shape[2]
     step, count = pl.program_id(0), pl.num_programs(0) // 2
     part = gcw_ref.shape[1]
@@ -1354,19 +1367,18 @@
     @pl.when(step >= count)
     def _():
         gt_ref[...] = got_ref[...].astype(F32) + dy_ref[...].astype(F32)
-        for j in range(TWO):
-            branch = jnp.dot(wo_ref[...], last_ref[j], preferred_element_type=F32)
-            mixed_ref[j] = (x_ref[j].astype(F32) + branch + spread(b_ref[...], length)).astype(BF16)
-
+
+    branch = jnp.dot(wo_ref[...], last_ref[0], preferred_element_type=F32)
+    mixed_ref[0] = (x_ref[0].astype(F32) + branch + spread(b_ref[...], length)).astype(BF16)
     for k in range(KERNEL):
 
-        @pl.when(step == k // TWO)
+        @pl.when(step == k)
         def _():
-            gcw_ref[k] = total_ref[k * part : (k + 1) * part, :].astype(F32)
+            gcw_ref[0] = total_ref[k * part : (k + 1) * part, :].astype(F32)
 
     for k, (ref, start) in enumerate(((gwo_ref, KERNEL * part), (gwi_ref, 3 * ROWS))):
 
-        @pl.when(step == KERNEL // TWO + 1 + k)
+        @pl.when(step == KERNEL + k)
         def _():
             for j in range(D // INNER):
                 ref[:, j * INNER : (j + 1) * INNER] = total_ref[start + j * part : start + (j + 1) * part, :].astype(F32)
@@ -1374,8 +1386,14 @@
     @pl.when(step == 0)
     def _():
         at = 3 * ROWS + part * D // INNER
-        inner_ref[...] = total_ref[at : at + 16, :].astype(F32)
-        outer_ref[...] = small_ref[:16, :].astype(F32)
+        rows = total_ref[at : at + 16, :].astype(F32)
+        for k, ref in enumerate(inner_refs):
+            ref[...] = rows[k, :part]
+        rows = small_ref[:16, :].astype(F32)
+        each = outer_refs[0].shape[0] // LANES
+        for k, ref in enumerate(outer_refs):
+            for j in range(each):
+                ref[j * LANES : (j + 1) * LANES] = rows[k * each + j]
 
 
 def finish_call(pre, mine, got, cot, last, tokens, wo_t, b_out, total, small, mixed, part):
@@ -1390,8 +1408,8 @@
             pl.BlockSpec((TWO, share, length), lambda i, pre: (early(i), 0, 0)),
             pl.BlockSpec((TWO, share, length), lambda i, pre: (late(i), 0, 0)),
             pl.BlockSpec((TWO, share, length), lambda i, pre: ((pre[0] // TWO + i) % (seqs // TWO), 0, 0)),
-            pl.BlockSpec((TWO, INNER, length), lambda i, pre: (late(i), 0, 0)),
-            pl.BlockSpec((TWO, share, length), lambda i, pre: (pre[2] // TWO + late(i), pre[1], 0)),
+            pl.BlockSpec((1, INNER, length), lambda i, pre: (i, 0, 0)),
+            pl.BlockSpec((1, share, length), lambda i, pre: (pre[2] + i, pre[1], 0)),
             whole(wo_t.shape),
             whole(b_out.shape),
             whole(total.shape),
@@ -1400,12 +1418,12 @@
         ],
         (
             pl.BlockSpec((TWO, share, length), lambda i, pre: ((pre[0] // TWO + i) % (seqs // TWO), 0, 0)),
-            pl.BlockSpec((TWO, share, length), lambda i, pre: (pre[2] // TWO + late(i), 0, 0)),
-            const((KERNEL, part, INNER)),
+            pl.BlockSpec((1, share, length), lambda i, pre: (pre[2] + i, 0, 0)),
+            pl.BlockSpec((1, part, INNER), lambda i, pre: (jnp.minimum(i, KERNEL - 1), 0, 0)),
             const((part, D)),
             const((part, D)),
-            const((16, INNER)),
-            const((16, LANES)),
+            *[const((part,))] * 6,
+            *[const((share,))] * 3,
         ),
         (
             sds((seqs, share, length), F32),
@@ -1413,8 +1431,8 @@
             sds((KERNEL, part, INNER), F32),
             sds((part, D), F32),
             sds((part, D), F32),
-            sds((16, INNER), F32),
-            sds((16, LANES), F32),
+            *[sds((part,), F32)] * 6,
+            *[sds((share,), F32)] * 3,
         ),
         aliases={10: 1},
     )(pre, mine, got, cot, last, tokens, wo_t, b_out, total, small, mixed)
@@ -1493,14 +1511,13 @@
             others.append(rotate(block, "ch", chs, r))
 
     p2 = lane_copies(inner)
-    wo_t = lax.dynamic_slice_in_dim(w_out_full, ch * share, share, 1).T
-
     mid_own, lead, trail, hat_mid, gp_mid, scale_mid = middle_call(
         pre, first, pad_mask, w_in_full, p2, n, 0, group, True
     )
     if pair:
-        wc, wc_t, before, after = turn_call(pre, conv_full, (lead, trail))
+        wc, wc_t, before, after, wo_t = turn_call(pre, conv_full, (lead, trail), w_out_full)
     else:
+        wo_t = lax.dynamic_slice_in_dim(w_out_full, ch * share, share, 1).T
         wc, wc_t = turn_call(pre, conv_full)
         before, after = rims(lead, trail)
         mid_oth, lead, trail = middle_call(pre, first, pad_mask, w_in_full, p2, seqs - n, n, group, False)
@@ -1526,10 +1543,10 @@
             dn, tokens, stat, mid_oth, rims_oth, wc, w_in_full, p1, p2, rows, rows_in,
             gcw.reshape(KERNEL, INNER, INNER), gwo, gwi, group,
         )
-        gt, mixed, gcw, gwi, gwo, inner_sums, outer_sums = finish_call(
+        gt, mixed, gcw, gwi, gwo, *sums = finish_call(
             pre, mine, got, cotangent, last_oth, tokens, wo_t, bo, total, small, mixed, part
         )
-        inner_sums, outer_sums = inner_sums[:6, :part], outer_sums[:15].reshape(3, share)
+        inner_sums, outer_sums = sums[:6], sums[6:]
     else:
         gt, *rest = front_call(
             pre, dconv, lead, trail, mid_own, hat_mid, gp_mid, scale_mid, tokens, stat, cotangent,

time: 299 us -> 294 us (0.983)
  local copies, waits for them, and re-layouts: 15.3 us -> 10 us
  transfers between devices with their start and end apart: 1 -> 1, of which waited for: 1 -> 1; matrix products, arithmetic and copies ran while one was open for 3% -> 2% of each run, Pallas kernels for 16% -> 17%
where the time goes in v6:
time: 294 us
  Pallas kernels  277 us (94%)
  local copies, waits for them, and re-layouts  10 us (3%)
  waiting for transfers between devices  4.71 us (2%)
    pallas_call x1, Pallas kernels, tail_call(): pl.pallas_call(functools.partial(tail_kernel, group), grid=(len(KINDS),),...  99.9 us
    pallas_call x1, Pallas kernels, inner_call(): call(functools.partial(inner_kernel, group), (count // TWO,), [own, edge,...  39 us
    pallas_call x1, Pallas kernels, first_call(): pl.pallas_call(lambda *refs: first_kernel(True, None, *refs), grid=(seqs,...  38.9 us
    pallas_call x1, Pallas kernels, last_call(): call(functools.partial(last_kernel, group, keep), (count // TWO,), in_spe...  24.4 us
    pallas_call x1, Pallas kernels, rear_call(): call(functools.partial(rear_kernel, group, chs), (count // TWO,), [pl.Blo...  20.1 us
    pallas_call x1, Pallas kernels, finish_call(): call(finish_kernel, (2 * count,), [pl.BlockSpec((TWO, share, length), lam...  18.2 us
    pallas_call x1, Pallas kernels, middle_call(): call(functools.partial(middle_kernel, group, keep), (count // TWO,), [pl....  14.2 us
    pallas_call x1, Pallas kernels, middle_rims_call(): pl.pallas_call(functools.partial(middle_rims_kernel, group), grid=(count...  11.4 us
  transfers between devices with their start and end apart: 1, of which 1 were waited for; matrix products, arithmetic and copies ran while one was open for 2% of the time, Pallas kernels for 17%

profile of v6, /device:TPU:0, one launch (start us, length us, event | category | flops | bytes accessed | tf_op | source)
XLA Modules:
  0.0 293.6 jit_solution(11783193376119046591)
XLA Ops:
  0.6 0.7 stack.25
  1.3 0.7 stack.26
  2.0 0.8 concatenate.3
  2.9 0.6 pad_bitcast_fusion.refs_5_
  3.5 1.5 broadcast_in_dim.8.refs_1_.refs_8_
  5.0 0.0 copy-start
  5.0 38.9 %shard_map.254 = (bf16[16,1280,256]{2,1,0:T(8,128)(2,1)}, f32[16,2,256]{2,1,0:T(2,128)}, bf16[640,1280]{1,0:T(8,128)(2,1)}, bf16[5,640,640]{2,1,0:T(8,128)(2,1)}...) custom-call(bf16[16,1280,256]{2,1,0:T(8,128)(2,1)} %x_ref.3, ...), custom_call_target="tpu_custom_call" | custom-call | flops 419430400 | bytes 20971520 | tf_op jit(solution)/shard_map/pallas_call | solution.py:280
  43.9 0.7 collective-permute-start
  44.6 0.0 copy-done
  44.6 0.6 reshape.48.mask_ref
  45.2 0.7 copy.34
  45.9 0.1 reshape.50
  46.1 0.1 broadcast_in_dim.9
  46.1 0.7 pad_add_fusion.pre
  46.8 1.9 broadcast_in_dim.10.p_ref.refs_7_.refs_9_
  48.7 14.2 %shard_map.255 = (bf16[8,640,256]{2,1,0:T(8,128)(2,1)}, bf16[2,640,128]{2,1,0:T(8,128)(2,1)}, bf16[2,640,128]{2,1,0:T(8,128)(2,1)}, bf16[8,640,256]{2,1,0:T(8,12...) custom-call(s32[3]{0:T(128)} %pad_add_fusion.pre, bf16[16,1280,256]{2,1,0:T(8,128)(2,1)} %get-tuple-element.72.first_ref.refs_7_, ...), custom_call_target="tpu_custom_call" | custom-call | flops 5033164800 | bytes 13107200 | tf_op jit(solution)/shard_map/pallas_call | solution.py:471
  62.8 0.0 copy-start.1
  62.8 10.5 %shard_map.256 = (bf16[640,3200]{1,0:T(8,128)(2,1)}, bf16[640,3200]{1,0:T(8,128)(2,1)}, bf16[2,640,128]{2,1,0:T(8,128)(2,1)}, bf16[2,640,128]{2,1,0:T(8,128)(2,1)}, bf16[640,640]{1,0:T(8,128)(2,1)}) custom-call(bf16[2,640,128]{2,1,0:T(8,128)(2,1)} %get-tuple-element.76.lead, bf16[2,640,128]{2,1,0:T(8,128)(2,1)} %get-tuple-element.77.trail, ...), custom_call_target="tpu_custom_call" | custom-call | flops 2621440000 | bytes 12288000 | tf_op jit(solution)/shard_map/pallas_call | solution.py:867
  73.3 0.0 copy-done.1
  73.3 0.9 broadcast_in_dim.22.b_ref
  74.2 24.4 %shard_map.257 = (bf16[16,640,256]{2,1,0:T(8,128)(2,1)}, bf16[8,640,256]{2,1,0:T(8,128)(2,1)}, f32[8,640,256]{2,1,0:T(8,128)}, f32[8,1,256]{2,1,0:T(1,128)}, bf16[8,640,256]{2,1,0:T(8,128)(2,1)}) custom-call(s32[3]{0:T(128)} %pad_add_fusion.pre, bf16[8,640,256]{2,1,0:T(8,128)(2,1)} %get-tuple-element.75.mid_ref.refs_3_, ...), custom_call_target="tpu_custom_call" | custom-call | flops 13086228480 | bytes 15728640 | tf_op jit(solution)/shard_map/pallas_call | solution.py:578
  98.6 4.7 %collective-permute-done.refs_1_ = bf16[8,640,256]{2,1,0:T(8,128)(2,1)S(1)} collective-permute-done((bf16[8,640,256]{2,1,0:T(8,128)(2,1)}, bf16[8,640,256]{2,1,0:T(8,128)(2,1)S(1)}, u32[]{:S(2)}, u32[]{:S(2)}) %collective-permute-start) | collective-permute-done | bytes 2621472 | tf_op jit(solution)/shard_map/ppermute | solution.py:1442
  103.3 0.0 copy-start.2
  103.3 1.5 copy-done.2
  104.8 20.1 %shard_map.258 = (bf16[8,640,256]{2,1,0:T(8,128)(2,1)}, bf16[2,640,128]{2,1,0:T(8,128)(2,1)}, bf16[2,640,128]{2,1,0:T(8,128)(2,1)}, f32[640,128]{1,0:T(8,128)}, ...) custom-call(s32[3]{0:T(128)} %pad_add_fusion.pre, ...), custom_call_target="tpu_custom_call" | custom-call | flops 8388608000 | bytes 13107200 | tf_op jit(solution)/shard_map/pallas_call | solution.py:678
  124.9 11.4 %shard_map.259 = (bf16[8,640,256]{2,1,0:T(8,128)(2,1)}, bf16[2,640,128]{2,1,0:T(8,128)(2,1)}, bf16[2,640,128]{2,1,0:T(8,128)(2,1)}, bf16[2,640,128]{2,1,0:T(8,128)(2,1)}, bf16[2,640,128]{2,1,0:T(8,128)(2,1)}) custom-call(bf16[2,640,128]{2,1,0:T(8,128)(2,1)} %get-tuple-element.88.lead_in, bf16[2,640,128]{2,1,0:T(8,128)(2,1)} %get-tuple-element.89.trail_in, ...), custom_call_target="tpu_custom_call" | custom-call | flops 5033164800 | bytes 13107200 | tf_op jit(solution)/shard_map/pallas_call | solution.py:410
  136.3 39.0 %shard_map.260 = (bf16[8,640,256]{2,1,0:T(8,128)(2,1)}, f32[3200,640]{1,0:T(8,128)}, f32[640,1280]{1,0:T(8,128)}, f32[8,1920]{1,0:T(8,128)}) custom-call(s32[3]{0:T(128)} %pad_add_fusion.pre, bf16[8,640,256]{2,1,0:T(8,128)(2,1)} %get-tuple-element.87.refs_0_, bf16[2,640,128]{2,1,0:T(8,128)(2,1)} %get-tuple-element.90.refs_1_, ...), custom_call_target="tpu_custom_call" | custom-call | flops 20132659200 | bytes 8192000 | tf_op jit(solution)/shard_map/pallas_call | solution.py:1073
  175.3 99.9 %shard_map.261 = (bf16[8,640,256]{2,1,0:T(8,128)(2,1)}, bf16[8,640,256]{2,1,0:T(8,128)(2,1)}, bf16[3072,640]{1,0:T(8,128)(2,1)}, bf16[256,128]{1,0:T(8,128)(2,1)}, bf16[8,640,256]{2,1,0:T(8,128)(2,1)}) custom-call(bf16[8,640,256]{2,1,0:T(8,128)(2,1)} %get-tuple-element.96.refs_0_, bf16[16,1280,256]{2,1,0:T(8,128)(2,1)} %x_ref.3, ...), custom_call_target="tpu_custom_call" | custom-call | flops 46976204800 | bytes 23592960 | tf_op jit(solution)/shard_map/pallas_call | solution.py:1301
  275.2 18.2 %shard_map.262 = (f32[16,640,256]{2,1,0:T(8,128)}, bf16[16,640,256]{2,1,0:T(8,128)(2,1)}, f32[5,320,640]{2,1,0:T(8,128)}, f32[320,1280]{1,0:T(8,128)}, f32[320,1...) custom-call(s32[3]{0:T(128)} %pad_add_fusion.pre, ...), custom_call_target="tpu_custom_call", output_to_operand_aliasing={{1}: (10, {})} | custom-call | tf_op jit(solution)/shard_map/pallas_call | solution.py:1404
  (3 shorter events, 0.0 us)
Async XLA Ops:
  5.0 39.6 %copy-start = (s32[16,256]{1,0:T(8,128)S(1)}, s32[16,256]{1,0:T(8,128)}, u32[]{:S(2)}) copy-start(s32[16,256]{1,0:T(8,128)} %param.16) | copy-start | bytes 49156
  43.9 59.4 %collective-permute-start = (bf16[8,640,256]{2,1,0:T(8,128)(2,1)}, bf16[8,640,256]{2,1,0:T(8,128)(2,1)S(1)}, u32[]{:S(2)}, u32[]{:S(2)}) collective-permute-start(bf16[8,640,256]{2,1,0:T(8,128)(2,1)} %get-tuple-element.70), channel_id=1, source_target_pairs={{0,1},{1,0},{2,3},{3,2},{4,5},{5,4},{6,7},{7,6},{8,9},{9,8},{10,11... | collective-permute-start | bytes 7864328 | tf_op jit(solution)/shard_map/ppermute | solution.py:1442
  62.8 10.5 %copy-start.1 = (f32[640]{0:T(1024)S(1)}, f32[640]{0:T(1024)}, u32[]{:S(2)}) copy-start(f32[640]{0:T(1024)} %param.29) | copy-start | bytes 7684
  103.3 1.5 copy-start.2

commit v7 on v6

--- a/solution.py
+++ b/solution.py
@@ -216,7 +216,7 @@
 
         if k > 0:
 
-            @pl.when(step == (0, 1, 4, 7)[k])
+            @pl.when(step == (0, 1, 3, 5)[k])
             def _():
                 first_hop[k].start()
 

time: 294 us -> 294 us (level)
  no operation moved by 1% of the time
where the time goes in v7:
time: 294 us
  Pallas kernels  277 us (94%)
  local copies, waits for them, and re-layouts  10 us (3%)
  waiting for transfers between devices  4.71 us (2%)
    pallas_call x1, Pallas kernels, tail_call(): pl.pallas_call(functools.partial(tail_kernel, group), grid=(len(KINDS),),...  99.9 us
    pallas_call x1, Pallas kernels, inner_call(): call(functools.partial(inner_kernel, group), (count // TWO,), [own, edge,...  39 us
    pallas_call x1, Pallas kernels, first_call(): pl.pallas_call(lambda *refs: first_kernel(True, None, *refs), grid=(seqs,...  38.9 us
    pallas_call x1, Pallas kernels, last_call(): call(functools.partial(last_kernel, group, keep), (count // TWO,), in_spe...  24.4 us
    pallas_call x1, Pallas kernels, rear_call(): call(functools.partial(rear_kernel, group, chs), (count // TWO,), [pl.Blo...  20.1 us
    pallas_call x1, Pallas kernels, finish_call(): call(finish_kernel, (2 * count,), [pl.BlockSpec((TWO, share, length), lam...  18.2 us
    pallas_call x1, Pallas kernels, middle_call(): call(functools.partial(middle_kernel, group, keep), (count // TWO,), [pl....  14.2 us
    pallas_call x1, Pallas kernels, middle_rims_call(): pl.pallas_call(functools.partial(middle_rims_kernel, group), grid=(count...  11.4 us
  transfers between devices with their start and end apart: 1, of which 1 were waited for; matrix products, arithmetic and copies ran while one was open for 2% of the time, Pallas kernels for 17%

profile of v7, /device:TPU:0, one launch (start us, length us, event | category | flops | bytes accessed | tf_op | source)
XLA Modules:
  0.0 293.6 jit_solution(1606887224364433655)
XLA Ops:
  0.6 0.7 stack.25
  1.3 0.7 stack.26
  2.0 0.8 concatenate.3
  2.9 0.6 pad_bitcast_fusion.refs_5_
  3.5 1.5 broadcast_in_dim.8.refs_1_.refs_8_
  5.0 0.0 copy-start
  5.0 38.9 %shard_map.254 = (bf16[16,1280,256]{2,1,0:T(8,128)(2,1)}, f32[16,2,256]{2,1,0:T(2,128)}, bf16[640,1280]{1,0:T(8,128)(2,1)}, bf16[5,640,640]{2,1,0:T(8,128)(2,1)}...) custom-call(bf16[16,1280,256]{2,1,0:T(8,128)(2,1)} %x_ref.3, ...), custom_call_target="tpu_custom_call" | custom-call | flops 419430400 | bytes 20971520 | tf_op jit(solution)/shard_map/pallas_call | solution.py:280
  43.9 0.7 collective-permute-start
  44.6 0.0 copy-done
  44.6 0.6 reshape.48.mask_ref
  45.2 0.7 copy.34
  45.9 0.1 reshape.50
  46.1 0.1 broadcast_in_dim.9
  46.1 0.7 pad_add_fusion.pre
  46.8 1.9 broadcast_in_dim.10.p_ref.refs_7_.refs_9_
  48.7 14.2 %shard_map.255 = (bf16[8,640,256]{2,1,0:T(8,128)(2,1)}, bf16[2,640,128]{2,1,0:T(8,128)(2,1)}, bf16[2,640,128]{2,1,0:T(8,128)(2,1)}, bf16[8,640,256]{2,1,0:T(8,12...) custom-call(s32[3]{0:T(128)} %pad_add_fusion.pre, bf16[16,1280,256]{2,1,0:T(8,128)(2,1)} %get-tuple-element.72.first_ref.refs_7_, ...), custom_call_target="tpu_custom_call" | custom-call | flops 5033164800 | bytes 13107200 | tf_op jit(solution)/shard_map/pallas_call | solution.py:471
  62.8 0.0 copy-start.1
  62.8 10.5 %shard_map.256 = (bf16[640,3200]{1,0:T(8,128)(2,1)}, bf16[640,3200]{1,0:T(8,128)(2,1)}, bf16[2,640,128]{2,1,0:T(8,128)(2,1)}, bf16[2,640,128]{2,1,0:T(8,128)(2,1)}, bf16[640,640]{1,0:T(8,128)(2,1)}) custom-call(bf16[2,640,128]{2,1,0:T(8,128)(2,1)} %get-tuple-element.76.lead, bf16[2,640,128]{2,1,0:T(8,128)(2,1)} %get-tuple-element.77.trail, ...), custom_call_target="tpu_custom_call" | custom-call | flops 2621440000 | bytes 12288000 | tf_op jit(solution)/shard_map/pallas_call | solution.py:867
  73.3 0.0 copy-done.1
  73.3 0.9 broadcast_in_dim.22.b_ref
  74.2 24.4 %shard_map.257 = (bf16[16,640,256]{2,1,0:T(8,128)(2,1)}, bf16[8,640,256]{2,1,0:T(8,128)(2,1)}, f32[8,640,256]{2,1,0:T(8,128)}, f32[8,1,256]{2,1,0:T(1,128)}, bf16[8,640,256]{2,1,0:T(8,128)(2,1)}) custom-call(s32[3]{0:T(128)} %pad_add_fusion.pre, bf16[8,640,256]{2,1,0:T(8,128)(2,1)} %get-tuple-element.75.mid_ref.refs_3_, ...), custom_call_target="tpu_custom_call" | custom-call | flops 13086228480 | bytes 15728640 | tf_op jit(solution)/shard_map/pallas_call | solution.py:578
  98.6 4.7 %collective-permute-done.refs_1_ = bf16[8,640,256]{2,1,0:T(8,128)(2,1)S(1)} collective-permute-done((bf16[8,640,256]{2,1,0:T(8,128)(2,1)}, bf16[8,640,256]{2,1,0:T(8,128)(2,1)S(1)}, u32[]{:S(2)}, u32[]{:S(2)}) %collective-permute-start) | collective-permute-done | bytes 2621472 | tf_op jit(solution)/shard_map/ppermute | solution.py:1442
  103.3 0.0 copy-start.2
  103.3 1.5 copy-done.2
  104.8 20.1 %shard_map.258 = (bf16[8,640,256]{2,1,0:T(8,128)(2,1)}, bf16[2,640,128]{2,1,0:T(8,128)(2,1)}, bf16[2,640,128]{2,1,0:T(8,128)(2,1)}, f32[640,128]{1,0:T(8,128)}, ...) custom-call(s32[3]{0:T(128)} %pad_add_fusion.pre, ...), custom_call_target="tpu_custom_call" | custom-call | flops 8388608000 | bytes 13107200 | tf_op jit(solution)/shard_map/pallas_call | solution.py:678
  124.9 11.4 %shard_map.259 = (bf16[8,640,256]{2,1,0:T(8,128)(2,1)}, bf16[2,640,128]{2,1,0:T(8,128)(2,1)}, bf16[2,640,128]{2,1,0:T(8,128)(2,1)}, bf16[2,640,128]{2,1,0:T(8,128)(2,1)}, bf16[2,640,128]{2,1,0:T(8,128)(2,1)}) custom-call(bf16[2,640,128]{2,1,0:T(8,128)(2,1)} %get-tuple-element.88.lead_in, bf16[2,640,128]{2,1,0:T(8,128)(2,1)} %get-tuple-element.89.trail_in, ...), custom_call_target="tpu_custom_call" | custom-call | flops 5033164800 | bytes 13107200 | tf_op jit(solution)/shard_map/pallas_call | solution.py:410
  136.3 39.0 %shard_map.260 = (bf16[8,640,256]{2,1,0:T(8,128)(2,1)}, f32[3200,640]{1,0:T(8,128)}, f32[640,1280]{1,0:T(8,128)}, f32[8,1920]{1,0:T(8,128)}) custom-call(s32[3]{0:T(128)} %pad_add_fusion.pre, bf16[8,640,256]{2,1,0:T(8,128)(2,1)} %get-tuple-element.87.refs_0_, bf16[2,640,128]{2,1,0:T(8,128)(2,1)} %get-tuple-element.90.refs_1_, ...), custom_call_target="tpu_custom_call" | custom-call | flops 20132659200 | bytes 8192000 | tf_op jit(solution)/shard_map/pallas_call | solution.py:1073
  175.3 99.9 %shard_map.261 = (bf16[8,640,256]{2,1,0:T(8,128)(2,1)}, bf16[8,640,256]{2,1,0:T(8,128)(2,1)}, bf16[3072,640]{1,0:T(8,128)(2,1)}, bf16[256,128]{1,0:T(8,128)(2,1)}, bf16[8,640,256]{2,1,0:T(8,128)(2,1)}) custom-call(bf16[8,640,256]{2,1,0:T(8,128)(2,1)} %get-tuple-element.96.refs_0_, bf16[16,1280,256]{2,1,0:T(8,128)(2,1)} %x_ref.3, ...), custom_call_target="tpu_custom_call" | custom-call | flops 46976204800 | bytes 23592960 | tf_op jit(solution)/shard_map/pallas_call | solution.py:1301
  275.1 18.2 %shard_map.262 = (f32[16,640,256]{2,1,0:T(8,128)}, bf16[16,640,256]{2,1,0:T(8,128)(2,1)}, f32[5,320,640]{2,1,0:T(8,128)}, f32[320,1280]{1,0:T(8,128)}, f32[320,1...) custom-call(s32[3]{0:T(128)} %pad_add_fusion.pre, ...), custom_call_target="tpu_custom_call", output_to_operand_aliasing={{1}: (10, {})} | custom-call | tf_op jit(solution)/shard_map/pallas_call | solution.py:1404
  (3 shorter events, 0.0 us)
Async XLA Ops:
  5.0 39.6 %copy-start = (s32[16,256]{1,0:T(8,128)S(1)}, s32[16,256]{1,0:T(8,128)}, u32[]{:S(2)}) copy-start(s32[16,256]{1,0:T(8,128)} %param.16) | copy-start | bytes 49156
  43.9 59.4 %collective-permute-start = (bf16[8,640,256]{2,1,0:T(8,128)(2,1)}, bf16[8,640,256]{2,1,0:T(8,128)(2,1)S(1)}, u32[]{:S(2)}, u32[]{:S(2)}) collective-permute-start(bf16[8,640,256]{2,1,0:T(8,128)(2,1)} %get-tuple-element.70), channel_id=1, source_target_pairs={{0,1},{1,0},{2,3},{3,2},{4,5},{5,4},{6,7},{7,6},{8,9},{9,8},{10,11... | collective-permute-start | bytes 7864328 | tf_op jit(solution)/shard_map/ppermute | solution.py:1442
  62.8 10.5 %copy-start.1 = (f32[640]{0:T(1024)S(1)}, f32[640]{0:T(1024)}, u32[]{:S(2)}) copy-start(f32[640]{0:T(1024)} %param.29) | copy-start | bytes 7684
  103.3 1.5 copy-start.2
